TPU v7x, 128 devices: a whole 4x4x4 slice. The times are simulated.
128 devices in a mesh: row: 8 (over z_hi, x), col: 8 (over y, core), rep: 2 (over z_lo).
Axes of the slice: x: 4, y: 4, z: 4 (z_hi: 2, z_lo: 2; z = z_hi * 2 + z_lo), core: 2. Of those that a mesh axis runs over, the one named last changes fastest.
Arguments:
- activations: bfloat16 [2048, 12288], P(('col', 'rep'), 'row'), may hold values from -6 to 6
- out_grad: bfloat16 [2048, 24576], P(('row', 'rep'), 'col'), may hold values from -0.1875 to 0.1875
Outputs:
- weight_grad: bfloat16 [12288, 24576], P('row', 'col')
All inputs are finite; a program needn't handle non-finite values.
Results may differ from a plain program's by a relative error of at most 0.0051.
Values may be sent and summed in bfloat16 or wider, within the bound.
No kernel may reach another device: no remote copies, remote signals or barrier semaphores. Data moves between devices by JAX's collectives and lax.ppermute only.
A program may use at most 128 MiB of HBM per device.

v0:
```python
import jax
import jax.numpy as jnp
from jax import lax
from jax.sharding import PartitionSpec as P


def from_root(array, axis, root):
    mine = lax.axis_index(axis) == root
    return lax.psum(jnp.where(mine, array, jnp.zeros_like(array)), axis)


def outer_add(total, left, right):
    return total + lax.dot_general(
        left, right, (((0,), (0,)), ((), ())), preferred_element_type=jnp.float32
    )


def shards(activations, out_grad):
    empty = jnp.zeros((activations.shape[1], out_grad.shape[1]), jnp.float32)

    def one_block(index, total):
        act_block = from_root(activations, "col", index)
        grad_block = from_root(out_grad, "row", index)
        return outer_add(total, act_block, grad_block)

    partial_grad = lax.fori_loop(0, lax.axis_size("col"), one_block, empty)
    rounded = partial_grad.astype(jnp.bfloat16).astype(jnp.float32)
    summed = lax.psum(rounded.astype(jnp.bfloat16), "rep")
    return summed


def solution(mesh):
    placed = (P(("col", "rep"), "row"), P(("row", "rep"), "col"))
    return jax.shard_map(
        shards, mesh=mesh, in_specs=placed, out_specs=P("row", "col"), check_vma=False
    )
```

profile of v0, /device:TPU:0, one launch (start us, length us, event | category | flops | bytes accessed | tf_op | source)
XLA Modules:
  0.0 1582.4 jit_solution(16076529391470042024)
XLA Ops:
  7.4 1323.1 %while.14 = (s32[]{:T(128)}, f32[1536,3072]{1,0:T(8,128)}, bf16[128,1536]{1,0:T(8,128)(2,1)}, bf16[128,3072]{1,0:T(8,128)(2,1)}, s32[]{:T(128)}, /*index=5*/u32[]{:T(128)}, u32[]{:T(128)}, u32[]{:T(128)}, s32[]{:T(128)}) while((s32[]{:T(128)}, f32[1536,3072]{1,0:T(8,128)}, bf16[128,1536]{1,0:T(8,128)(2,1)}, ...), condition=%wide.region_3.4_spmd.clone, body=%wide.region_0.3_spmd.clone.sunk | while | flops 1218576384 | bytes 48365840 | solution.py:26
  11.3 62.0 %all-reduce.6.cloned.1.call-done = bf16[128,1536]{1,0:T(8,128)(2,1)} async-done(((bf16[128,1536]{1,0:T(8,128)(2,1)}), bf16[128,1536]{1,0:T(8,128)(2,1)}) %all-reduce.6.cloned.1.call-update) | async-done | bytes 393232 | tf_op jit(solution)/shard_map/while/body/eval_jaxpr/psum | solution.py:9
  73.4 88.3 %all-reduce.8.cloned.1.call-done = bf16[128,3072]{1,0:T(8,128)(2,1)} async-done(((bf16[128,3072]{1,0:T(8,128)(2,1)}), bf16[128,3072]{1,0:T(8,128)(2,1)}) %all-reduce.8.cloned.1.call-update) | async-done | bytes 786448 | tf_op jit(solution)/shard_map/while/body/eval_jaxpr/psum | solution.py:9
  173.9 59.7 %all-reduce.6.cloned.1.call-done = bf16[128,1536]{1,0:T(8,128)(2,1)} async-done(((bf16[128,1536]{1,0:T(8,128)(2,1)}), bf16[128,1536]{1,0:T(8,128)(2,1)}) %all-reduce.6.cloned.1.call-update) | async-done | bytes 393232 | tf_op jit(solution)/shard_map/while/body/eval_jaxpr/psum | solution.py:9
  233.6 88.2 %all-reduce.8.cloned.1.call-done = bf16[128,3072]{1,0:T(8,128)(2,1)} async-done(((bf16[128,3072]{1,0:T(8,128)(2,1)}), bf16[128,3072]{1,0:T(8,128)(2,1)}) %all-reduce.8.cloned.1.call-update) | async-done | bytes 786448 | tf_op jit(solution)/shard_map/while/body/eval_jaxpr/psum | solution.py:9
  321.7 15.9 %select_add_fusion.2 = f32[1536,3072]{1,0:T(8,128)} fusion(f32[1536,3072]{1,0:T(8,128)} %get-tuple-element.143, bf16[128,1536]{1,0:T(8,128)(2,1)} %all-reduce.6.cloned.1.call-done, bf16[128,3072]{1,0:T(8,128)(2,1)} %all-reduce.8.cloned.1.call-done, pred[]{:T(512)S(6)} %compare.3), kind=kOutput, calls=%fused_computation.clone.1 | convolution fusion | flops 1217396736 | bytes 38928384 | tf_op jit(solution)/shard_map/while/body/eval_jaxpr/dot_general | solution.py:13
  339.4 59.4 %all-reduce.6.cloned.1.call-done = bf16[128,1536]{1,0:T(8,128)(2,1)} async-done(((bf16[128,1536]{1,0:T(8,128)(2,1)}), bf16[128,1536]{1,0:T(8,128)(2,1)}) %all-reduce.6.cloned.1.call-update) | async-done | bytes 393232 | tf_op jit(solution)/shard_map/while/body/eval_jaxpr/psum | solution.py:9
  398.8 88.2 %all-reduce.8.cloned.1.call-done = bf16[128,3072]{1,0:T(8,128)(2,1)} async-done(((bf16[128,3072]{1,0:T(8,128)(2,1)}), bf16[128,3072]{1,0:T(8,128)(2,1)}) %all-reduce.8.cloned.1.call-update) | async-done | bytes 786448 | tf_op jit(solution)/shard_map/while/body/eval_jaxpr/psum | solution.py:9
  487.0 15.9 %select_add_fusion.2 = f32[1536,3072]{1,0:T(8,128)} fusion(f32[1536,3072]{1,0:T(8,128)} %get-tuple-element.143, bf16[128,1536]{1,0:T(8,128)(2,1)} %all-reduce.6.cloned.1.call-done, bf16[128,3072]{1,0:T(8,128)(2,1)} %all-reduce.8.cloned.1.call-done, pred[]{:T(512)S(6)} %compare.3), kind=kOutput, calls=%fused_computation.clone.1 | convolution fusion | flops 1217396736 | bytes 38928384 | tf_op jit(solution)/shard_map/while/body/eval_jaxpr/dot_general | solution.py:13
  504.7 59.7 %all-reduce.6.cloned.1.call-done = bf16[128,1536]{1,0:T(8,128)(2,1)} async-done(((bf16[128,1536]{1,0:T(8,128)(2,1)}), bf16[128,1536]{1,0:T(8,128)(2,1)}) %all-reduce.6.cloned.1.call-update) | async-done | bytes 393232 | tf_op jit(solution)/shard_map/while/body/eval_jaxpr/psum | solution.py:9
  564.4 88.3 %all-reduce.8.cloned.1.call-done = bf16[128,3072]{1,0:T(8,128)(2,1)} async-done(((bf16[128,3072]{1,0:T(8,128)(2,1)}), bf16[128,3072]{1,0:T(8,128)(2,1)}) %all-reduce.8.cloned.1.call-update) | async-done | bytes 786448 | tf_op jit(solution)/shard_map/while/body/eval_jaxpr/psum | solution.py:9
  670.4 59.7 %all-reduce.6.cloned.1.call-done = bf16[128,1536]{1,0:T(8,128)(2,1)} async-done(((bf16[128,1536]{1,0:T(8,128)(2,1)}), bf16[128,1536]{1,0:T(8,128)(2,1)}) %all-reduce.6.cloned.1.call-update) | async-done | bytes 393232 | tf_op jit(solution)/shard_map/while/body/eval_jaxpr/psum | solution.py:9
  730.1 88.2 %all-reduce.8.cloned.1.call-done = bf16[128,3072]{1,0:T(8,128)(2,1)} async-done(((bf16[128,3072]{1,0:T(8,128)(2,1)}), bf16[128,3072]{1,0:T(8,128)(2,1)}) %all-reduce.8.cloned.1.call-update) | async-done | bytes 786448 | tf_op jit(solution)/shard_map/while/body/eval_jaxpr/psum | solution.py:9
  818.3 15.9 %select_add_fusion.2 = f32[1536,3072]{1,0:T(8,128)} fusion(f32[1536,3072]{1,0:T(8,128)} %get-tuple-element.143, bf16[128,1536]{1,0:T(8,128)(2,1)} %all-reduce.6.cloned.1.call-done, bf16[128,3072]{1,0:T(8,128)(2,1)} %all-reduce.8.cloned.1.call-done, pred[]{:T(512)S(6)} %compare.3), kind=kOutput, calls=%fused_computation.clone.1 | convolution fusion | flops 1217396736 | bytes 38928384 | tf_op jit(solution)/shard_map/while/body/eval_jaxpr/dot_general | solution.py:13
  835.9 59.7 %all-reduce.6.cloned.1.call-done = bf16[128,1536]{1,0:T(8,128)(2,1)} async-done(((bf16[128,1536]{1,0:T(8,128)(2,1)}), bf16[128,1536]{1,0:T(8,128)(2,1)}) %all-reduce.6.cloned.1.call-update) | async-done | bytes 393232 | tf_op jit(solution)/shard_map/while/body/eval_jaxpr/psum | solution.py:9
  895.7 88.2 %all-reduce.8.cloned.1.call-done = bf16[128,3072]{1,0:T(8,128)(2,1)} async-done(((bf16[128,3072]{1,0:T(8,128)(2,1)}), bf16[128,3072]{1,0:T(8,128)(2,1)}) %all-reduce.8.cloned.1.call-update) | async-done | bytes 786448 | tf_op jit(solution)/shard_map/while/body/eval_jaxpr/psum | solution.py:9
  983.8 15.9 %select_add_fusion.2 = f32[1536,3072]{1,0:T(8,128)} fusion(f32[1536,3072]{1,0:T(8,128)} %get-tuple-element.143, bf16[128,1536]{1,0:T(8,128)(2,1)} %all-reduce.6.cloned.1.call-done, bf16[128,3072]{1,0:T(8,128)(2,1)} %all-reduce.8.cloned.1.call-done, pred[]{:T(512)S(6)} %compare.3), kind=kOutput, calls=%fused_computation.clone.1 | convolution fusion | flops 1217396736 | bytes 38928384 | tf_op jit(solution)/shard_map/while/body/eval_jaxpr/dot_general | solution.py:13
  1001.5 59.7 %all-reduce.6.cloned.1.call-done = bf16[128,1536]{1,0:T(8,128)(2,1)} async-done(((bf16[128,1536]{1,0:T(8,128)(2,1)}), bf16[128,1536]{1,0:T(8,128)(2,1)}) %all-reduce.6.cloned.1.call-update) | async-done | bytes 393232 | tf_op jit(solution)/shard_map/while/body/eval_jaxpr/psum | solution.py:9
  1061.2 88.2 %all-reduce.8.cloned.1.call-done = bf16[128,3072]{1,0:T(8,128)(2,1)} async-done(((bf16[128,3072]{1,0:T(8,128)(2,1)}), bf16[128,3072]{1,0:T(8,128)(2,1)}) %all-reduce.8.cloned.1.call-update) | async-done | bytes 786448 | tf_op jit(solution)/shard_map/while/body/eval_jaxpr/psum | solution.py:9
  1149.4 15.9 %select_add_fusion.2 = f32[1536,3072]{1,0:T(8,128)} fusion(f32[1536,3072]{1,0:T(8,128)} %get-tuple-element.143, bf16[128,1536]{1,0:T(8,128)(2,1)} %all-reduce.6.cloned.1.call-done, bf16[128,3072]{1,0:T(8,128)(2,1)} %all-reduce.8.cloned.1.call-done, pred[]{:T(512)S(6)} %compare.3), kind=kOutput, calls=%fused_computation.clone.1 | convolution fusion | flops 1217396736 | bytes 38928384 | tf_op jit(solution)/shard_map/while/body/eval_jaxpr/dot_general | solution.py:13
  1167.1 59.4 %all-reduce.6.cloned.1.call-done = bf16[128,1536]{1,0:T(8,128)(2,1)} async-done(((bf16[128,1536]{1,0:T(8,128)(2,1)}), bf16[128,1536]{1,0:T(8,128)(2,1)}) %all-reduce.6.cloned.1.call-update) | async-done | bytes 393232 | tf_op jit(solution)/shard_map/while/body/eval_jaxpr/psum | solution.py:9
  1226.5 88.2 %all-reduce.8.cloned.1.call-done = bf16[128,3072]{1,0:T(8,128)(2,1)} async-done(((bf16[128,3072]{1,0:T(8,128)(2,1)}), bf16[128,3072]{1,0:T(8,128)(2,1)}) %all-reduce.8.cloned.1.call-update) | async-done | bytes 786448 | tf_op jit(solution)/shard_map/while/body/eval_jaxpr/psum | solution.py:9
  1314.6 15.9 %select_add_fusion.2 = f32[1536,3072]{1,0:T(8,128)} fusion(f32[1536,3072]{1,0:T(8,128)} %get-tuple-element.143, bf16[128,1536]{1,0:T(8,128)(2,1)} %all-reduce.6.cloned.1.call-done, bf16[128,3072]{1,0:T(8,128)(2,1)} %all-reduce.8.cloned.1.call-done, pred[]{:T(512)S(6)} %compare.3), kind=kOutput, calls=%fused_computation.clone.1 | convolution fusion | flops 1217396736 | bytes 38928384 | tf_op jit(solution)/shard_map/while/body/eval_jaxpr/dot_general | solution.py:13
  1341.8 225.2 %all-reduce.4.cloned.1.call-done = bf16[1536,3072]{1,0:T(8,128)(2,1)} async-done(((bf16[1536,3072]{1,0:T(8,128)(2,1)}), bf16[1536,3072]{1,0:T(8,128)(2,1)}) %all-reduce.4.cloned.1.call-update) | async-done | bytes 9437200 | tf_op jit(solution)/shard_map/psum | solution.py:28
  (55 shorter events, 62.3 us)
Async XLA Ops:
  7.4 66.0 %all-reduce.6.cloned.1.call-start = ((), (), s32[]{:S(2)}) async-start(), calls=%async_computation.1 | async-start | bytes 786432 | tf_op jit(solution)/shard_map/while/body/eval_jaxpr/psum | solution.py:9
  9.2 152.5 %all-reduce.8.cloned.1.call-start = ((), (), s32[]{:S(2)}) async-start(), calls=%async_computation.2 | async-start | bytes 1572864 | tf_op jit(solution)/shard_map/while/body/eval_jaxpr/psum | solution.py:9
  172.0 61.5 %all-reduce.6.cloned.1.call-start = ((), (), s32[]{:S(2)}) async-start(), calls=%async_computation.1 | async-start | bytes 786432 | tf_op jit(solution)/shard_map/while/body/eval_jaxpr/psum | solution.py:9
  172.8 148.9 %all-reduce.8.cloned.1.call-start = ((), (), s32[]{:S(2)}) async-start(), calls=%async_computation.2 | async-start | bytes 1572864 | tf_op jit(solution)/shard_map/while/body/eval_jaxpr/psum | solution.py:9
  337.6 61.2 %all-reduce.6.cloned.1.call-start = ((), (), s32[]{:S(2)}) async-start(), calls=%async_computation.1 | async-start | bytes 786432 | tf_op jit(solution)/shard_map/while/body/eval_jaxpr/psum | solution.py:9
  338.4 148.6 %all-reduce.8.cloned.1.call-start = ((), (), s32[]{:S(2)}) async-start(), calls=%async_computation.2 | async-start | bytes 1572864 | tf_op jit(solution)/shard_map/while/body/eval_jaxpr/psum | solution.py:9
  502.8 61.5 %all-reduce.6.cloned.1.call-start = ((), (), s32[]{:S(2)}) async-start(), calls=%async_computation.1 | async-start | bytes 786432 | tf_op jit(solution)/shard_map/while/body/eval_jaxpr/psum | solution.py:9
  503.6 149.1 %all-reduce.8.cloned.1.call-start = ((), (), s32[]{:S(2)}) async-start(), calls=%async_computation.2 | async-start | bytes 1572864 | tf_op jit(solution)/shard_map/while/body/eval_jaxpr/psum | solution.py:9
  668.6 61.5 %all-reduce.6.cloned.1.call-start = ((), (), s32[]{:S(2)}) async-start(), calls=%async_computation.1 | async-start | bytes 786432 | tf_op jit(solution)/shard_map/while/body/eval_jaxpr/psum | solution.py:9
  669.4 148.9 %all-reduce.8.cloned.1.call-start = ((), (), s32[]{:S(2)}) async-start(), calls=%async_computation.2 | async-start | bytes 1572864 | tf_op jit(solution)/shard_map/while/body/eval_jaxpr/psum | solution.py:9
  834.1 61.5 %all-reduce.6.cloned.1.call-start = ((), (), s32[]{:S(2)}) async-start(), calls=%async_computation.1 | async-start | bytes 786432 | tf_op jit(solution)/shard_map/while/body/eval_jaxpr/psum | solution.py:9
  834.9 148.9 %all-reduce.8.cloned.1.call-start = ((), (), s32[]{:S(2)}) async-start(), calls=%async_computation.2 | async-start | bytes 1572864 | tf_op jit(solution)/shard_map/while/body/eval_jaxpr/psum | solution.py:9
  999.7 61.5 %all-reduce.6.cloned.1.call-start = ((), (), s32[]{:S(2)}) async-start(), calls=%async_computation.1 | async-start | bytes 786432 | tf_op jit(solution)/shard_map/while/body/eval_jaxpr/psum | solution.py:9
  1000.5 148.9 %all-reduce.8.cloned.1.call-start = ((), (), s32[]{:S(2)}) async-start(), calls=%async_computation.2 | async-start | bytes 1572864 | tf_op jit(solution)/shard_map/while/body/eval_jaxpr/psum | solution.py:9
  1165.2 61.2 %all-reduce.6.cloned.1.call-start = ((), (), s32[]{:S(2)}) async-start(), calls=%async_computation.1 | async-start | bytes 786432 | tf_op jit(solution)/shard_map/while/body/eval_jaxpr/psum | solution.py:9
  1166.0 148.6 %all-reduce.8.cloned.1.call-start = ((), (), s32[]{:S(2)}) async-start(), calls=%async_computation.2 | async-start | bytes 1572864 | tf_op jit(solution)/shard_map/while/body/eval_jaxpr/psum | solution.py:9
  1330.5 236.5 %all-reduce.4.cloned.1.call-start = ((), (), s32[]{:S(2)}) async-start(), calls=%async_computation | async-start | bytes 18874368 | tf_op jit(solution)/shard_map/psum | solution.py:28
Sparse Core Ops, SparseCore 0:
  10.5 62.7 all-reduce.5
  76.0 85.6 all-reduce.7
  175.2 58.3 all-reduce.5
  236.1 85.6 all-reduce.7
  340.4 58.3 all-reduce.5
  401.3 85.6 all-reduce.7
  506.0 58.3 all-reduce.5
  567.0 85.6 all-reduce.7
  671.7 58.3 all-reduce.5
  732.6 85.6 all-reduce.7
  837.3 58.3 all-reduce.5
  898.2 85.6 all-reduce.7
  1002.8 58.3 all-reduce.5
  1063.7 85.6 all-reduce.7
  1168.1 58.3 all-reduce.5
  1229.0 85.6 all-reduce.7
Sparse Core Ops, SparseCore 1:
  1341.9 225.0 all-reduce.3
where the time goes:
time: 1580 us
  waiting for transfers between devices  1410 us (89%)
  matrix products  121 us (8%)
  other arithmetic  27.2 us (2%)
    psum x16, waiting for transfers between devices, from_root(): return lax.psum(jnp.where(mine, array, jnp.zeros_like(array)), axis)  1180 us
    psum x1, waiting for transfers between devices, shards(): summed = lax.psum(rounded.astype(jnp.bfloat16), 'rep')  225 us
    dot_general x8, matrix products, outer_add(): lax.dot_general(left, right, (((0,), (0,)), ((), ())), preferred_element_...  121 us
  transfers between devices with their start and end apart: 17, of which 17 were waited for; matrix products, arithmetic and copies ran while one was open for 1% of the time, Pallas kernels for 0%

commit v1 on v0

v1 whole, which is shorter than its diff:
```python
import functools

import jax
import jax.numpy as jnp
import numpy as np
from jax import lax
from jax.experimental import pallas as pl
from jax.experimental.pallas import tpu as pltpu
from jax.sharding import PartitionSpec as P

AXES = ("row", "col", "rep")
TOK = 128
PAIRS = ((768, 768), (768, 768))
GATHERED = 0


def device(x, y, z, core):
    return ((z // 2) * 4 + x) * 16 + (y * 2 + core) * 2 + z % 2


def every():
    return [(x, y, z, c) for x in range(4) for y in range(4) for z in range(4) for c in range(2)]


def ring(dx, dy, dz):
    pairs = []
    for x, y, z, c in every():
        s = 1 if c == 0 else -1
        to = ((x + s * dx) % 4, (y + s * dy) % 4, (z + s * dz) % 4, c)
        pairs.append((device(x, y, z, c), device(*to)))
    return pairs


X_RING, Y_RING, Z_RING = ring(1, 0, 0), ring(0, 1, 0), ring(0, 0, 1)
CORE_SWAP = [(device(x, y, z, c), device(x, y, z, 1 - c)) for x, y, z, c in every()]
REP_SWAP = [(device(x, y, z, c), device(x, y, z ^ 1, c)) for x, y, z, c in every()]


def tables():
    first = np.zeros((128, 16), np.int32)
    second = np.zeros((128, 16), np.int32)
    plain = np.zeros((128, 16), np.int32)
    for x0, y0, z0, c0 in every():
        me = device(x0, y0, z0, c0)
        s0 = 1 if c0 == 0 else -1

        def place(x, z):
            k = (z // 2) * 4 + x
            y, c = k // 2, k % 2
            s = 1 if c == 0 else -1
            return int(c != c0) * 8 + ((y0 - y) * s) % 4 * 2 + int(z % 2 != z0 % 2)

        for outer in range(4):
            for inner in range(4):
                at = outer * 4 + inner
                first[me, at] = place((x0 - s0 * inner) % 4, (z0 - s0 * outer) % 4)
                second[me, at] = place((x0 - s0 * outer) % 4, (z0 - s0 * inner) % 4)
                plain[me, at] = place(outer, inner)
    return np.stack([first, second, plain], axis=1)


def flip(pieces):
    rows, wide = pieces[0].shape

    def kernel(*refs):
        for n, ref in enumerate(refs[:-1]):
            refs[-1][:, n * rows : (n + 1) * rows] = ref[...].T

    total = rows * len(pieces)
    step = 512
    return pl.pallas_call(
        kernel,
        grid=(wide // step,),
        in_specs=[pl.BlockSpec((rows, step), lambda i: (0, i)) for _ in pieces],
        out_specs=pl.BlockSpec((step, total), lambda i: (i, 0)),
        out_shape=jax.ShapeDtypeStruct((wide, total), jnp.bfloat16),
        compiler_params=pltpu.CompilerParams(vmem_limit_bytes=32 << 20),
        cost_estimate=pl.CostEstimate(flops=0, bytes_accessed=4 * wide * total, transcendentals=0),
    )(*pieces)


def multiply(left, groups, places, before, start, full):
    widths = [g[0].shape[1] for g, _ in groups]
    width = sum(widths)
    rows = left[0].shape[0]
    step = 256
    counts = [len(g) for g, _ in groups]
    tokens = sum(a.shape[1] for a in left)

    def kernel(places_ref, *refs):
        left_refs = refs[: len(left)]
        refs = refs[len(left) :]
        grad_refs = refs[: sum(counts)]
        out_ref, held = refs[-2], refs[-1]

        @pl.when(pl.program_id(0) == 0)
        def _():
            n, column = 0, 0
            for (g, row), w in zip(groups, widths):
                at = 0
                for block in g:
                    for piece in range(block.shape[0] // TOK):
                        to = pl.multiple_of(places_ref[row, at] * TOK, TOK)
                        held[pl.ds(to, TOK), column : column + w] = grad_refs[n][
                            piece * TOK : (piece + 1) * TOK, :
                        ]
                        at += 1
                    n += 1
                column += w

        lhs = jnp.concatenate([r[...] for r in left_refs], axis=1) if len(left) > 1 else left_refs[0][...]
        out_ref[...] = jnp.dot(lhs, held[...], preferred_element_type=jnp.float32).astype(jnp.bfloat16)

    operands = list(left) + [b for g, _ in groups for b in g]
    in_specs = [pl.BlockSpec((step, a.shape[1]), lambda i, t: (i, 0)) for a in left]
    in_specs += [
        pl.BlockSpec(b.shape, lambda i, t: (0, 0), pipeline_mode=pl.Buffered(1)) for g, _ in groups for b in g
    ]
    aliases = {}
    if before is not None:
        operands.append(before)
        in_specs.append(pl.BlockSpec(memory_space=pl.ANY))
        aliases = {len(operands): 0}
    assert start % width == 0
    column_block = start // width
    return pl.pallas_call(
        kernel,
        grid_spec=pltpu.PrefetchScalarGridSpec(
            num_scalar_prefetch=1,
            grid=(rows // step,),
            in_specs=in_specs,
            out_specs=pl.BlockSpec((step, width), lambda i, t: (i, column_block)),
            scratch_shapes=[pltpu.VMEM((tokens, width), jnp.bfloat16)],
        ),
        out_shape=jax.ShapeDtypeStruct((rows, full), jnp.bfloat16),
        input_output_aliases=aliases,
        compiler_params=pltpu.CompilerParams(vmem_limit_bytes=32 << 20),
        cost_estimate=pl.CostEstimate(
            flops=2 * rows * width * tokens,
            bytes_accessed=2 * (rows * tokens + tokens * width + rows * width),
            transcendentals=0,
        ),
    )(places, *operands)


def around(block, pairs):
    blocks = [block]
    for _ in range(3):
        blocks.append(lax.ppermute(blocks[-1], AXES, pairs))
    return blocks


def shards(activations, out_grad):
    full = out_grad.shape[1]
    me = (lax.axis_index("row") * 8 + lax.axis_index("col")) * 2 + lax.axis_index("rep")
    places = lax.dynamic_index_in_dim(jnp.asarray(tables()), me, 0, keepdims=False)

    other = lax.ppermute(activations, AXES, REP_SWAP)
    mine = around(jnp.concatenate([activations, other], axis=0), Y_RING)
    sibling = [lax.ppermute(b, AXES, CORE_SWAP) for b in mine]
    left = [flip(mine), flip(sibling)]

    result = None
    start = 0
    jobs = []
    for w_a, w_b in PAIRS:
        a = out_grad[:, start : start + w_a]
        b = out_grad[:, start + w_a : start + w_a + w_b]
        a = around(jnp.concatenate(around(a, X_RING), axis=0), Z_RING)
        b = around(jnp.concatenate(around(b, Z_RING), axis=0), X_RING)
        jobs.append(([(a, 0), (b, 1)], start))
        start += w_a + w_b
    if GATHERED:
        order = [[((z // 2) * 4 + x) * 2 + z % 2 for x in range(4) for z in range(4)]]
        whole = lax.all_gather(
            out_grad[:, start:], ("row", "rep"), axis=0, tiled=True, axis_index_groups=order
        )
        jobs.append(([([whole], 2)], start))
    for groups, at in jobs:
        result = multiply(left, groups, places, result, at, full)
    return result


def solution(mesh):
    placed = (P(("col", "rep"), "row"), P(("row", "rep"), "col"))
    return jax.shard_map(
        shards, mesh=mesh, in_specs=placed, out_specs=P("row", "col"), check_vma=False
    )
```

time: 1580 us -> 119 us (0.08)
  waiting for transfers between devices: 1410 us -> 45 us
  matrix products: 121 us -> 0 us
  Pallas kernels: 0 us -> 34.7 us
  starting transfers between devices: 0.37 us -> 31.3 us
  other arithmetic: 27.2 us -> 0.21 us
    psum x17 -> x0, waiting for transfers between devices: 1410 us -> none  [the longest x16 1180 us: from_root(): return lax.psum(jnp.where(mine, array, jnp.zeros_like(array)), axis)]
    dot_general x8 -> x0, matrix products: 121 us -> none  [outer_add(): lax.dot_general(left, right, (((0,), (0,)), ((), ())), preferred_element_...]
    ppermute x0 -> x32, waiting for transfers between devices: none -> 45 us  [the longest x27 45 us: around(): blocks.append(lax.ppermute(blocks[-1], AXES, pairs))]
    pallas_call x0 -> x4, Pallas kernels: none -> 34.7 us  [the longest x2 29 us: multiply(): pl.pallas_call(kernel, grid_spec=pltpu.PrefetchScalarGridSpec(num_scalar_...]
    ppermute x0 -> x32, starting transfers between devices: none -> 31.3 us  [the longest x27 28.2 us: around(): blocks.append(lax.ppermute(blocks[-1], AXES, pairs))]
    select_n x16 -> x0, other arithmetic: 15.9 us -> none  [from_root(): return lax.psum(jnp.where(mine, array, jnp.zeros_like(array)), axis)]
  transfers between devices with their start and end apart: 17 -> 32, of which waited for: 17 -> 15; matrix products, arithmetic and copies ran while one was open for 1% -> 2% of each run, Pallas kernels for 0% -> 17%
where the time goes in v1:
time: 119 us
  waiting for transfers between devices  45 us (38%)
  Pallas kernels  34.7 us (29%)
  starting transfers between devices  31.3 us (26%)
  local copies, waits for them, and re-layouts  7.4 us (6%)
    ppermute x27, waiting for transfers between devices, around(): blocks.append(lax.ppermute(blocks[-1], AXES, pairs))  45 us
    pallas_call x2, Pallas kernels, multiply(): pl.pallas_call(kernel, grid_spec=pltpu.PrefetchScalarGridSpec(num_scalar_...  29 us
    ppermute x27, starting transfers between devices, around(): blocks.append(lax.ppermute(blocks[-1], AXES, pairs))  28.2 us
    pallas_call x2, Pallas kernels, flip(): pl.pallas_call(kernel, grid=(wide // step,), in_specs=[pl.BlockSpec((rows...  5.69 us
    unnamed x39, local copies, waits for them, and re-layouts  5.42 us
  transfers between devices with their start and end apart: 32, of which 15 were waited for; matrix products, arithmetic and copies ran while one was open for 2% of the time, Pallas kernels for 17%

profile of v1, /device:TPU:0, one launch (start us, length us, event | category | flops | bytes accessed | tf_op | source)
XLA Modules:
  0.0 118.8 jit_solution(5710922502271111233)
XLA Ops:
  0.0 2.0 %collective-permute-start = (bf16[128,1536]{1,0:T(8,128)(2,1)}, bf16[128,1536]{1,0:T(8,128)(2,1)S(1)}, u32[]{:S(2)}, u32[]{:S(2)}) collective-permute-start(bf16[128,1536]{1,0:T(8,128)(2,1)} %param.3), channel_id=1, source_target_pairs={{0,1},{2,3},{1,0},{3,2},{64,65},{66,67},{65,64},{67,66},{4,5},{6,7... | collective-permute-start | bytes 1179656 | tf_op jit(solution)/shard_map/ppermute | solution.py:158
  3.4 3.5 %collective-permute-start.14 = (bf16[128,768]{1,0:T(8,128)(2,1)S(1)}, bf16[128,768]{1,0:T(8,128)(2,1)S(1)}, u32[]{:S(2)}, u32[]{:S(2)}) collective-permute-start(bf16[128,768]{1,0:T(8,128)(2,1)S(1)} %get-tuple-element.6), channel_id=1, source_target_pairs={{0,1},{2,67},{1,64},{3,2},{64,65},{66,3},{65,0},{67,66},{4,5},{6,7... | collective-permute-start | bytes 589832 | tf_op jit(solution)/shard_map/ppermute | solution.py:149
  9.9 2.8 %collective-permute-done.26 = bf16[128,768]{1,0:T(8,128)(2,1)S(1)} collective-permute-done((bf16[128,768]{1,0:T(8,128)(2,1)S(1)}, bf16[128,768]{1,0:T(8,128)(2,1)S(1)}, u32[]{:S(2)}, u32[]{:S(2)}) %collective-permute-start.26) | collective-permute-done | bytes 196640 | tf_op jit(solution)/shard_map/ppermute | solution.py:149
  12.7 2.5 %collective-permute-start.27 = (bf16[128,768]{1,0:T(8,128)(2,1)S(1)}, bf16[128,768]{1,0:T(8,128)(2,1)S(1)}, u32[]{:S(2)}, u32[]{:S(2)}) collective-permute-start(bf16[128,768]{1,0:T(8,128)(2,1)S(1)} %collective-permute-done.26), channel_id=1, source_target_pairs={{0,1},{2,67},{1,64},{3,2},{64,65},{66,3},{65,0},{67,66},{4,5},{6,7... | collective-permute-start | bytes 589832 | tf_op jit(solution)/shard_map/ppermute | solution.py:149
  16.7 1.6 %collective-permute-start.1 = (bf16[256,1536]{1,0:T(8,128)(2,1)S(1)}, bf16[256,1536]{1,0:T(8,128)(2,1)S(1)}, u32[]{:S(2)}, u32[]{:S(2)}) collective-permute-start(bf16[256,1536]{1,0:T(8,128)(2,1)S(1)} %constant_dynamic-update-slice_fusion.refs_0_), channel_id=1, source_target_pairs={{0,4},{2,14},{1,5},{3,15},{64,68},{66,78},{65,69},{67,79},{4,8},{6... | collective-permute-start | bytes 2359304 | tf_op jit(solution)/shard_map/ppermute | solution.py:149
  22.8 2.5 %collective-permute-done.9 = bf16[128,768]{1,0:T(8,128)(2,1)S(1)} collective-permute-done((bf16[128,768]{1,0:T(8,128)(2,1)S(1)}, bf16[128,768]{1,0:T(8,128)(2,1)S(1)}, u32[]{:S(2)}, u32[]{:S(2)}) %collective-permute-start.9) | collective-permute-done | bytes 196640 | tf_op jit(solution)/shard_map/ppermute | solution.py:149
  25.5 2.3 %collective-permute-done.15 = bf16[128,768]{1,0:T(8,128)(2,1)S(1)} collective-permute-done((bf16[128,768]{1,0:T(8,128)(2,1)S(1)}, bf16[128,768]{1,0:T(8,128)(2,1)S(1)}, u32[]{:S(2)}, u32[]{:S(2)}) %collective-permute-start.15) | collective-permute-done | bytes 196640 | tf_op jit(solution)/shard_map/ppermute | solution.py:149
  27.8 1.8 %collective-permute-done.22 = bf16[128,768]{1,0:T(8,128)(2,1)S(1)} collective-permute-done((bf16[128,768]{1,0:T(8,128)(2,1)S(1)}, bf16[128,768]{1,0:T(8,128)(2,1)S(1)}, u32[]{:S(2)}, u32[]{:S(2)}) %collective-permute-start.22) | collective-permute-done | bytes 196640 | tf_op jit(solution)/shard_map/ppermute | solution.py:149
  30.4 1.7 %collective-permute-done.10 = bf16[128,768]{1,0:T(8,128)(2,1)S(1)} collective-permute-done((bf16[128,768]{1,0:T(8,128)(2,1)S(1)}, bf16[128,768]{1,0:T(8,128)(2,1)S(1)}, u32[]{:S(2)}, u32[]{:S(2)}) %collective-permute-start.10) | collective-permute-done | bytes 196640 | tf_op jit(solution)/shard_map/ppermute | solution.py:149
  33.2 3.6 %collective-permute-done.16 = bf16[128,768]{1,0:T(8,128)(2,1)S(1)} collective-permute-done((bf16[128,768]{1,0:T(8,128)(2,1)S(1)}, bf16[128,768]{1,0:T(8,128)(2,1)S(1)}, u32[]{:S(2)}, u32[]{:S(2)}) %collective-permute-start.16) | collective-permute-done | bytes 196640 | tf_op jit(solution)/shard_map/ppermute | solution.py:149
  36.9 1.6 %collective-permute-start.17 = (bf16[512,768]{1,0:T(8,128)(2,1)S(1)}, bf16[512,768]{1,0:T(8,128)(2,1)}, u32[]{:S(2)}, u32[]{:S(2)}) collective-permute-start(bf16[512,768]{1,0:T(8,128)(2,1)S(1)} %pad_maximum_fusion.1.refs_6_), channel_id=1, source_target_pairs={{0,16},{2,50},{1,17},{3,51},{64,80},{66,114},{65,81},{67,115},{4,2... | collective-permute-start | bytes 2359304 | tf_op jit(solution)/shard_map/ppermute | solution.py:149
  38.5 1.6 %collective-permute-start.2 = (bf16[256,1536]{1,0:T(8,128)(2,1)S(1)}, bf16[256,1536]{1,0:T(8,128)(2,1)S(1)}, u32[]{:S(2)}, u32[]{:S(2)}) collective-permute-start(bf16[256,1536]{1,0:T(8,128)(2,1)S(1)} %collective-permute-done.1.refs_1_), channel_id=1, source_target_pairs={{0,4},{2,14},{1,5},{3,15},{64,68},{66,78},{65,69},{67,79},{4,8},{6... | collective-permute-start | bytes 2359304 | tf_op jit(solution)/shard_map/ppermute | solution.py:149
  40.1 1.6 %collective-permute-start.29 = (bf16[512,768]{1,0:T(8,128)(2,1)S(1)}, bf16[512,768]{1,0:T(8,128)(2,1)S(1)}, u32[]{:S(2)}, u32[]{:S(2)}) collective-permute-start(bf16[512,768]{1,0:T(8,128)(2,1)S(1)} %pad_maximum_fusion.3.refs_6_), channel_id=1, source_target_pairs={{0,16},{2,50},{1,17},{3,51},{64,80},{66,114},{65,81},{67,115},{4,2... | collective-permute-start | bytes 2359304 | tf_op jit(solution)/shard_map/ppermute | solution.py:149
  42.5 2.8 %collective-permute-done.23.refs_3_ = bf16[512,768]{1,0:T(8,128)(2,1)S(1)} collective-permute-done((bf16[512,768]{1,0:T(8,128)(2,1)S(1)}, bf16[512,768]{1,0:T(8,128)(2,1)S(1)}, u32[]{:S(2)}, u32[]{:S(2)}) %collective-permute-start.23) | collective-permute-done | bytes 786464 | tf_op jit(solution)/shard_map/ppermute | solution.py:149
  45.3 8.4 %collective-permute-done.11.refs_3_ = bf16[512,768]{1,0:T(8,128)(2,1)S(1)} collective-permute-done((bf16[512,768]{1,0:T(8,128)(2,1)S(1)}, bf16[512,768]{1,0:T(8,128)(2,1)S(1)}, u32[]{:S(2)}, u32[]{:S(2)}) %collective-permute-start.11) | collective-permute-done | bytes 786464 | tf_op jit(solution)/shard_map/ppermute | solution.py:149
  54.6 1.6 %collective-permute-start.3 = (bf16[256,1536]{1,0:T(8,128)(2,1)S(1)}, bf16[256,1536]{1,0:T(8,128)(2,1)}, u32[]{:S(2)}, u32[]{:S(2)}) collective-permute-start(bf16[256,1536]{1,0:T(8,128)(2,1)S(1)} %collective-permute-done.2.refs_2_), channel_id=1, source_target_pairs={{0,4},{2,14},{1,5},{3,15},{64,68},{66,78},{65,69},{67,79},{4,8},{6... | collective-permute-start | bytes 2359304 | tf_op jit(solution)/shard_map/ppermute | solution.py:149
  56.2 2.3 %collective-permute-start.12 = (bf16[512,768]{1,0:T(8,128)(2,1)S(1)}, bf16[512,768]{1,0:T(8,128)(2,1)S(1)}, u32[]{:S(2)}, u32[]{:S(2)}) collective-permute-start(bf16[512,768]{1,0:T(8,128)(2,1)S(1)} %collective-permute-done.11.refs_3_), channel_id=1, source_target_pairs={{0,1},{2,67},{1,64},{3,2},{64,65},{66,3},{65,0},{67,66},{4,5},{6,7... | collective-permute-start | bytes 2359304 | tf_op jit(solution)/shard_map/ppermute | solution.py:149
  62.2 4.8 %collective-permute-done.24.refs_4_ = bf16[512,768]{1,0:T(8,128)(2,1)} collective-permute-done((bf16[512,768]{1,0:T(8,128)(2,1)S(1)}, bf16[512,768]{1,0:T(8,128)(2,1)}, u32[]{:S(2)}, u32[]{:S(2)}) %collective-permute-start.24) | collective-permute-done | bytes 786464 | tf_op jit(solution)/shard_map/ppermute | solution.py:149
  67.9 7.4 %collective-permute-done.12.refs_4_ = bf16[512,768]{1,0:T(8,128)(2,1)S(1)} collective-permute-done((bf16[512,768]{1,0:T(8,128)(2,1)S(1)}, bf16[512,768]{1,0:T(8,128)(2,1)S(1)}, u32[]{:S(2)}, u32[]{:S(2)}) %collective-permute-start.12) | collective-permute-done | bytes 786464 | tf_op jit(solution)/shard_map/ppermute | solution.py:149
  78.3 2.8 %shard_map.37.refs_0_ = bf16[1536,1024]{1,0:T(8,128)(2,1)S(1)} custom-call(bf16[256,1536]{1,0:T(8,128)(2,1)S(1)} %constant_dynamic-update-slice_fusion.refs_0_, bf16[256,1536]{1,0:T(8,128)(2,1)S(1)} %collective-permute-done.1.refs_1_, bf16[256,1536]{1,0:T(8,128)(2,1)S(1)} %collective-permute-done.2.refs_2_, bf16[256,1536]{1,0:T(8,128)(2,1)} %collective-permute-done.3.refs_3_), custom_call_target="tpu_custom_call" | custom-call | bytes 6291456 | tf_op jit(solution)/shard_map/pallas_call | solution.py:71
  83.1 2.9 %shard_map.38.refs_1_ = bf16[1536,1024]{1,0:T(8,128)(2,1)S(1)} custom-call(bf16[256,1536]{1,0:T(8,128)(2,1)S(1)} %collective-permute-done.4.refs_0_, bf16[256,1536]{1,0:T(8,128)(2,1)S(1)} %copy-done.1, bf16[256,1536]{1,0:T(8,128)(2,1)} %collective-permute-done.6.refs_2_, bf16[256,1536]{1,0:T(8,128)(2,1)} %collective-permute-done.7.refs_3_), custom_call_target="tpu_custom_call" | custom-call | bytes 6291456 | tf_op jit(solution)/shard_map/pallas_call | solution.py:71
  86.0 2.9 %collective-permute-done.25.refs_5_ = bf16[512,768]{1,0:T(8,128)(2,1)} collective-permute-done((bf16[512,768]{1,0:T(8,128)(2,1)}, bf16[512,768]{1,0:T(8,128)(2,1)}, u32[]{:S(2)}, u32[]{:S(2)}) %collective-permute-start.25) | collective-permute-done | bytes 786464 | tf_op jit(solution)/shard_map/ppermute | solution.py:149
  89.8 14.8 %shard_map.39.refs_10_ = bf16[1536,3072]{1,0:T(8,128)(2,1)} custom-call(s32[3,16]{1,0:T(4,128)S(1)} %dynamic-slice_bitcast_fusion.places_ref, bf16[1536,1024]{1,0:T(8,128)(2,1)S(1)} %shard_map.37.refs_0_, bf16[1536,1024]{1,0:T(8,128)(2,1)S(1)} %shard_map.38.refs_1_, bf16[512,768]{1,0:T(8,128)(2,1)S(1)} %copy-done.5, bf16[512,768]{1,0:T(8,128)(2,1)S(1)} %copy-done.13, ...), custom_call_target="tpu_custom_call" | custom-call | flops 9663676416 | bytes 17301504 | tf_op jit(solution)/shard_map/pallas_call | solution.py:126
  104.6 14.3 %shard_map.40 = bf16[1536,3072]{1,0:T(8,128)(2,1)} custom-call(s32[3,16]{1,0:T(4,128)S(1)} %dynamic-slice_bitcast_fusion.places_ref, bf16[1536,1024]{1,0:T(8,128)(2,1)S(1)} %shard_map.37.refs_0_, bf16[1536,1024]{1,0:T(8,128)(2,1)S(1)} %shard_map.38.refs_1_, bf16[512,768]{1,0:T(8,128)(2,1)S(1)} %copy-done.3, ...), custom_call_target="tpu_custom_call", output_to_operand_aliasing={{}: (11, {})} | custom-call | flops 9663676416 | bytes 17301504 | tf_op jit(solution)/shard_map/pallas_call | solution.py:126
  (90 shorter events, 24.7 us)
Async XLA Ops:
  0.0 16.7 %collective-permute-start = (bf16[128,1536]{1,0:T(8,128)(2,1)}, bf16[128,1536]{1,0:T(8,128)(2,1)S(1)}, u32[]{:S(2)}, u32[]{:S(2)}) collective-permute-start(bf16[128,1536]{1,0:T(8,128)(2,1)} %param.3), channel_id=1, source_target_pairs={{0,1},{2,3},{1,0},{3,2},{64,65},{66,67},{65,64},{67,66},{4,5},{6,7... | collective-permute-start | bytes 1179656 | tf_op jit(solution)/shard_map/ppermute | solution.py:158
  3.3 9.4 %collective-permute-start.26 = (bf16[128,768]{1,0:T(8,128)(2,1)S(1)}, bf16[128,768]{1,0:T(8,128)(2,1)S(1)}, u32[]{:S(2)}, u32[]{:S(2)}) collective-permute-start(bf16[128,768]{1,0:T(8,128)(2,1)S(1)} %get-tuple-element.5), channel_id=1, source_target_pairs={{0,1},{2,67},{1,64},{3,2},{64,65},{66,3},{65,0},{67,66},{4,5},{6,7... | collective-permute-start | bytes 589832 | tf_op jit(solution)/shard_map/ppermute | solution.py:149
  3.4 16.4 %collective-permute-start.14 = (bf16[128,768]{1,0:T(8,128)(2,1)S(1)}, bf16[128,768]{1,0:T(8,128)(2,1)S(1)}, u32[]{:S(2)}, u32[]{:S(2)}) collective-permute-start(bf16[128,768]{1,0:T(8,128)(2,1)S(1)} %get-tuple-element.6), channel_id=1, source_target_pairs={{0,1},{2,67},{1,64},{3,2},{64,65},{66,3},{65,0},{67,66},{4,5},{6,7... | collective-permute-start | bytes 589832 | tf_op jit(solution)/shard_map/ppermute | solution.py:149
  6.9 11.5 %collective-permute-start.8 = (bf16[128,768]{1,0:T(8,128)(2,1)S(1)}, bf16[128,768]{1,0:T(8,128)(2,1)S(1)}, u32[]{:S(2)}, u32[]{:S(2)}) collective-permute-start(bf16[128,768]{1,0:T(8,128)(2,1)S(1)} %get-tuple-element.7), channel_id=1, source_target_pairs={{0,16},{2,50},{1,17},{3,51},{64,80},{66,114},{65,81},{67,115},{4,2... | collective-permute-start | bytes 589832 | tf_op jit(solution)/shard_map/ppermute | solution.py:149
  16.7 21.8 %collective-permute-start.1 = (bf16[256,1536]{1,0:T(8,128)(2,1)S(1)}, bf16[256,1536]{1,0:T(8,128)(2,1)S(1)}, u32[]{:S(2)}, u32[]{:S(2)}) collective-permute-start(bf16[256,1536]{1,0:T(8,128)(2,1)S(1)} %constant_dynamic-update-slice_fusion.refs_0_), channel_id=1, source_target_pairs={{0,4},{2,14},{1,5},{3,15},{64,68},{66,78},{65,69},{67,79},{4,8},{6... | collective-permute-start | bytes 2359304 | tf_op jit(solution)/shard_map/ppermute | solution.py:149
  19.8 20.3 %collective-permute-start.4 = (bf16[256,1536]{1,0:T(8,128)(2,1)S(1)}, bf16[256,1536]{1,0:T(8,128)(2,1)S(1)}, u32[]{:S(2)}, u32[]{:S(2)}) collective-permute-start(bf16[256,1536]{1,0:T(8,128)(2,1)S(1)} %constant_dynamic-update-slice_fusion.refs_0_), channel_id=1, source_target_pairs={{0,2},{2,0},{1,3},{3,1},{64,66},{66,64},{65,67},{67,65},{4,6},{6,4... | collective-permute-start | bytes 2359304 | tf_op jit(solution)/shard_map/ppermute | solution.py:160
  27.8 9.1 %collective-permute-start.28 = (bf16[128,768]{1,0:T(8,128)(2,1)S(1)}, bf16[128,768]{1,0:T(8,128)(2,1)S(1)}, u32[]{:S(2)}, u32[]{:S(2)}) collective-permute-start(bf16[128,768]{1,0:T(8,128)(2,1)S(1)} %collective-permute-done.27), channel_id=1, source_target_pairs={{0,1},{2,67},{1,64},{3,2},{64,65},{66,3},{65,0},{67,66},{4,5},{6,7... | collective-permute-start | bytes 589832 | tf_op jit(solution)/shard_map/ppermute | solution.py:149
  32.1 13.2 %collective-permute-start.23 = (bf16[512,768]{1,0:T(8,128)(2,1)S(1)}, bf16[512,768]{1,0:T(8,128)(2,1)S(1)}, u32[]{:S(2)}, u32[]{:S(2)}) collective-permute-start(bf16[512,768]{1,0:T(8,128)(2,1)S(1)} %pad_maximum_fusion.2.refs_2_), channel_id=1, source_target_pairs={{0,1},{2,67},{1,64},{3,2},{64,65},{66,3},{65,0},{67,66},{4,5},{6,7... | collective-permute-start | bytes 2359304 | tf_op jit(solution)/shard_map/ppermute | solution.py:149
  36.8 16.9 %collective-permute-start.11 = (bf16[512,768]{1,0:T(8,128)(2,1)S(1)}, bf16[512,768]{1,0:T(8,128)(2,1)S(1)}, u32[]{:S(2)}, u32[]{:S(2)}) collective-permute-start(bf16[512,768]{1,0:T(8,128)(2,1)S(1)} %pad_maximum_fusion.refs_2_), channel_id=1, source_target_pairs={{0,1},{2,67},{1,64},{3,2},{64,65},{66,3},{65,0},{67,66},{4,5},{6,7... | collective-permute-start | bytes 2359304 | tf_op jit(solution)/shard_map/ppermute | solution.py:149
  36.9 19.3 %collective-permute-start.17 = (bf16[512,768]{1,0:T(8,128)(2,1)S(1)}, bf16[512,768]{1,0:T(8,128)(2,1)}, u32[]{:S(2)}, u32[]{:S(2)}) collective-permute-start(bf16[512,768]{1,0:T(8,128)(2,1)S(1)} %pad_maximum_fusion.1.refs_6_), channel_id=1, source_target_pairs={{0,16},{2,50},{1,17},{3,51},{64,80},{66,114},{65,81},{67,115},{4,2... | collective-permute-start | bytes 2359304 | tf_op jit(solution)/shard_map/ppermute | solution.py:149
  38.5 16.2 %collective-permute-start.2 = (bf16[256,1536]{1,0:T(8,128)(2,1)S(1)}, bf16[256,1536]{1,0:T(8,128)(2,1)S(1)}, u32[]{:S(2)}, u32[]{:S(2)}) collective-permute-start(bf16[256,1536]{1,0:T(8,128)(2,1)S(1)} %collective-permute-done.1.refs_1_), channel_id=1, source_target_pairs={{0,4},{2,14},{1,5},{3,15},{64,68},{66,78},{65,69},{67,79},{4,8},{6... | collective-permute-start | bytes 2359304 | tf_op jit(solution)/shard_map/ppermute | solution.py:149
  40.1 19.3 %collective-permute-start.29 = (bf16[512,768]{1,0:T(8,128)(2,1)S(1)}, bf16[512,768]{1,0:T(8,128)(2,1)S(1)}, u32[]{:S(2)}, u32[]{:S(2)}) collective-permute-start(bf16[512,768]{1,0:T(8,128)(2,1)S(1)} %pad_maximum_fusion.3.refs_6_), channel_id=1, source_target_pairs={{0,16},{2,50},{1,17},{3,51},{64,80},{66,114},{65,81},{67,115},{4,2... | collective-permute-start | bytes 2359304 | tf_op jit(solution)/shard_map/ppermute | solution.py:149
  45.3 15.1 %collective-permute-start.5 = (bf16[256,1536]{1,0:T(8,128)(2,1)S(1)}, bf16[256,1536]{1,0:T(8,128)(2,1)S(1)}, u32[]{:S(2)}, u32[]{:S(2)}) collective-permute-start(bf16[256,1536]{1,0:T(8,128)(2,1)S(1)} %collective-permute-done.1.refs_1_), channel_id=1, source_target_pairs={{0,2},{2,0},{1,3},{3,1},{64,66},{66,64},{65,67},{67,65},{4,6},{6,4... | collective-permute-start | bytes 2359304 | tf_op jit(solution)/shard_map/ppermute | solution.py:160
  53.7 13.3 %collective-permute-start.24 = (bf16[512,768]{1,0:T(8,128)(2,1)S(1)}, bf16[512,768]{1,0:T(8,128)(2,1)}, u32[]{:S(2)}, u32[]{:S(2)}) collective-permute-start(bf16[512,768]{1,0:T(8,128)(2,1)S(1)} %collective-permute-done.23.refs_3_), channel_id=1, source_target_pairs={{0,1},{2,67},{1,64},{3,2},{64,65},{66,3},{65,0},{67,66},{4,5},{6,7... | collective-permute-start | bytes 2359304 | tf_op jit(solution)/shard_map/ppermute | solution.py:149
  54.6 13.3 %collective-permute-start.3 = (bf16[256,1536]{1,0:T(8,128)(2,1)S(1)}, bf16[256,1536]{1,0:T(8,128)(2,1)}, u32[]{:S(2)}, u32[]{:S(2)}) collective-permute-start(bf16[256,1536]{1,0:T(8,128)(2,1)S(1)} %collective-permute-done.2.refs_2_), channel_id=1, source_target_pairs={{0,4},{2,14},{1,5},{3,15},{64,68},{66,78},{65,69},{67,79},{4,8},{6... | collective-permute-start | bytes 2359304 | tf_op jit(solution)/shard_map/ppermute | solution.py:149
  56.2 19.2 %collective-permute-start.12 = (bf16[512,768]{1,0:T(8,128)(2,1)S(1)}, bf16[512,768]{1,0:T(8,128)(2,1)S(1)}, u32[]{:S(2)}, u32[]{:S(2)}) collective-permute-start(bf16[512,768]{1,0:T(8,128)(2,1)S(1)} %collective-permute-done.11.refs_3_), channel_id=1, source_target_pairs={{0,1},{2,67},{1,64},{3,2},{64,65},{66,3},{65,0},{67,66},{4,5},{6,7... | collective-permute-start | bytes 2359304 | tf_op jit(solution)/shard_map/ppermute | solution.py:149
  59.4 16.0 %collective-permute-start.30 = (bf16[512,768]{1,0:T(8,128)(2,1)S(1)}, bf16[512,768]{1,0:T(8,128)(2,1)}, u32[]{:S(2)}, u32[]{:S(2)}) collective-permute-start(bf16[512,768]{1,0:T(8,128)(2,1)S(1)} %collective-permute-done.29.refs_7_), channel_id=1, source_target_pairs={{0,16},{2,50},{1,17},{3,51},{64,80},{66,114},{65,81},{67,115},{4,2... | collective-permute-start | bytes 2359304 | tf_op jit(solution)/shard_map/ppermute | solution.py:149
  61.3 20.0 %collective-permute-start.18 = (bf16[512,768]{1,0:T(8,128)(2,1)}, bf16[512,768]{1,0:T(8,128)(2,1)}, u32[]{:S(2)}, u32[]{:S(2)}) collective-permute-start(bf16[512,768]{1,0:T(8,128)(2,1)} %collective-permute-done.17.refs_7_), channel_id=1, source_target_pairs={{0,16},{2,50},{1,17},{3,51},{64,80},{66,114},{65,81},{67,115},{4,2... | collective-permute-start | bytes 2359304 | tf_op jit(solution)/shard_map/ppermute | solution.py:149
  67.1 14.6 %collective-permute-start.6 = (bf16[256,1536]{1,0:T(8,128)(2,1)S(1)}, bf16[256,1536]{1,0:T(8,128)(2,1)}, u32[]{:S(2)}, u32[]{:S(2)}) collective-permute-start(bf16[256,1536]{1,0:T(8,128)(2,1)S(1)} %collective-permute-done.2.refs_2_), channel_id=1, source_target_pairs={{0,2},{2,0},{1,3},{3,1},{64,66},{66,64},{65,67},{67,65},{4,6},{6,4... | collective-permute-start | bytes 2359304 | tf_op jit(solution)/shard_map/ppermute | solution.py:160
  67.9 15.1 %collective-permute-start.7 = (bf16[256,1536]{1,0:T(8,128)(2,1)}, bf16[256,1536]{1,0:T(8,128)(2,1)}, u32[]{:S(2)}, u32[]{:S(2)}) collective-permute-start(bf16[256,1536]{1,0:T(8,128)(2,1)} %collective-permute-done.3.refs_3_), channel_id=1, source_target_pairs={{0,2},{2,0},{1,3},{3,1},{64,66},{66,64},{65,67},{67,65},{4,6},{6,4... | collective-permute-start | bytes 2359304 | tf_op jit(solution)/shard_map/ppermute | solution.py:160
  75.4 13.5 %collective-permute-start.25 = (bf16[512,768]{1,0:T(8,128)(2,1)}, bf16[512,768]{1,0:T(8,128)(2,1)}, u32[]{:S(2)}, u32[]{:S(2)}) collective-permute-start(bf16[512,768]{1,0:T(8,128)(2,1)} %collective-permute-done.24.refs_4_), channel_id=1, source_target_pairs={{0,1},{2,67},{1,64},{3,2},{64,65},{66,3},{65,0},{67,66},{4,5},{6,7... | collective-permute-start | bytes 2359304 | tf_op jit(solution)/shard_map/ppermute | solution.py:149
  76.2 13.5 %collective-permute-start.31 = (bf16[512,768]{1,0:T(8,128)(2,1)}, bf16[512,768]{1,0:T(8,128)(2,1)}, u32[]{:S(2)}, u32[]{:S(2)}) collective-permute-start(bf16[512,768]{1,0:T(8,128)(2,1)} %collective-permute-done.30.refs_8_), channel_id=1, source_target_pairs={{0,16},{2,50},{1,17},{3,51},{64,80},{66,114},{65,81},{67,115},{4,2... | collective-permute-start | bytes 2359304 | tf_op jit(solution)/shard_map/ppermute | solution.py:149
  81.2 23.3 %collective-permute-start.13 = (bf16[512,768]{1,0:T(8,128)(2,1)S(1)}, bf16[512,768]{1,0:T(8,128)(2,1)S(1)}, u32[]{:S(2)}, u32[]{:S(2)}) collective-permute-start(bf16[512,768]{1,0:T(8,128)(2,1)S(1)} %copy-done.17), channel_id=1, source_target_pairs={{0,1},{2,67},{1,64},{3,2},{64,65},{66,3},{65,0},{67,66},{4,5},{6,7... | collective-permute-start | bytes 2359304 | tf_op jit(solution)/shard_map/ppermute | solution.py:149
  81.7 22.9 %collective-permute-start.19 = (bf16[512,768]{1,0:T(8,128)(2,1)}, bf16[512,768]{1,0:T(8,128)(2,1)S(1)}, u32[]{:S(2)}, u32[]{:S(2)}) collective-permute-start(bf16[512,768]{1,0:T(8,128)(2,1)} %collective-permute-done.18.refs_8_), channel_id=1, source_target_pairs={{0,16},{2,50},{1,17},{3,51},{64,80},{66,114},{65,81},{67,115},{4,2... | collective-permute-start | bytes 2359304 | tf_op jit(solution)/shard_map/ppermute | solution.py:149
  (27 other events, 242.5 us)

commit v2 on v0

v2 whole, which is shorter than its diff:
```python
import jax
import jax.numpy as jnp
import numpy as np
from jax import lax
from jax.experimental import pallas as pl
from jax.experimental.pallas import tpu as pltpu
from jax.sharding import PartitionSpec as P

AXES = ("row", "col", "rep")
TOK = 128
LIMIT = 16
TIES = 2
EARLY = 1
LEFT = 1
F32 = jnp.float32
BF16 = jnp.bfloat16


def device(x, y, z, core):
    return ((z // 2) * 4 + x) * 16 + (y * 2 + core) * 2 + z % 2


def every():
    return [(x, y, z, c) for x in range(4) for y in range(4) for z in range(4) for c in range(2)]


def ring(dx, dy, dz):
    pairs = []
    for x, y, z, c in every():
        s = 1 if c == 0 else -1
        to = ((x + s * dx) % 4, (y + s * dy) % 4, (z + s * dz) % 4, c)
        pairs.append((device(x, y, z, c), device(*to)))
    return pairs


X_RING, Z_RING = ring(1, 0, 0), ring(0, 0, 1)
Y_RING, Y_BACK = ring(0, 1, 0), ring(0, -1, 0)
CORE_SWAP = [(device(x, y, z, c), device(x, y, z, 1 - c)) for x, y, z, c in every()]
REP_SWAP = [(device(x, y, z, c), device(x, y, z ^ 1, c)) for x, y, z, c in every()]

KINDS = [[(i, j) for j in (p, p + 2) for i in range(4)] for p in range(2)]


def inner(part, step):
    return [(i, step) if part == 0 else (step, i) for i in (1, 2, 3)]


PASSES = [
    [[(0, 0), (1, 0), (2, 0), (0, 2)] for p in range(2)],
    [[(3, 0), (0, 1), (0, 3)] + inner(p, 1) for p in range(2)],
    [inner(p, 2) + inner(p, 3) for p in range(2)],
]


def tables():
    out = np.zeros((128, 2, 8), np.int32)
    for x0, y0, z0, c0 in every():
        s0 = 1 if c0 == 0 else -1
        for kind in range(2):
            for at, (i, j) in enumerate(KINDS[kind]):
                x, z = (x0 - s0 * i) % 4, (z0 - s0 * j) % 4
                assert z % 2 == (z0 + kind) % 2
                k = (z // 2) * 4 + x
                y, c = k // 2, k % 2
                s = 1 if c == 0 else -1
                back = ((y0 - y) * s) % 4
                out[device(x0, y0, z0, c0), kind, int(c != c0) * 4 + (0, 1, 3, 2)[back]] = at
    return out


def sort_tokens(places, kind, pieces):
    arrays = [p[0] for p in pieces]
    wide = arrays[0].shape[1]
    step = 512

    def kernel(places_ref, *refs):
        n = 0
        for ref, (_, first, blocks) in zip(refs, pieces):
            for b in range(blocks):
                to = pl.multiple_of(places_ref[kind, n] * TOK, TOK)
                refs[-1][pl.ds(to, TOK), :] = ref[first + b * TOK : first + (b + 1) * TOK, :]
                n += 1

    total = TOK * 8
    return pl.pallas_call(
        kernel,
        grid_spec=pltpu.PrefetchScalarGridSpec(
            num_scalar_prefetch=1,
            grid=(wide // step,),
            in_specs=[pl.BlockSpec((a.shape[0], step), lambda i, t: (0, i)) for a in arrays],
            out_specs=pl.BlockSpec((total, step), lambda i, t: (0, i)),
        ),
        out_shape=jax.ShapeDtypeStruct((total, wide), BF16),
        compiler_params=pltpu.CompilerParams(vmem_limit_bytes=LIMIT << 20),
        cost_estimate=pl.CostEstimate(flops=0, bytes_accessed=4 * wide * total, transcendentals=0),
    )(places, *arrays)


def multiply(lefts, number, shared, own, group, partial, before, full):
    width = full // 4
    used = [l for l in lefts if l is not None]
    slot = [None if l is None else sum(m is not None for m in lefts[:n]) for n, l in enumerate(lefts)]
    rows = used[0].shape[1]
    step = 256
    order = PASSES[number]
    depth = TOK * len(order[0])
    n_own = len(own[0])

    def kernel(*refs):
        left_refs, refs = refs[: len(used)], refs[len(used) :]
        shared_refs, refs = refs[: len(shared)], refs[len(shared) :]
        own_refs = [refs[:n_own], refs[n_own : 2 * n_own]]
        refs = refs[2 * n_own :]
        out_ref = refs[-1]
        for part in range(2):
            cols = slice(part * width, (part + 1) * width)
            lhs = []
            for i, j in order[part]:
                at = KINDS[j % 2].index((i, j)) * TOK
                lhs.append(left_refs[slot[j % 2]][at : at + TOK, :])
            lhs = jnp.concatenate(lhs, axis=0)
            rhs = [r[:, cols] for r in shared_refs] + [r[...] for r in own_refs[part]]
            rhs = jnp.concatenate(rhs, axis=0)
            total = lax.dot_general(lhs, rhs, (((0,), (0,)), ((), ())), preferred_element_type=F32)
            if partial is not None:
                total = total + refs[0][:, cols]
            out_ref[:, cols] = total.astype(out_ref.dtype)

    once = pl.Buffered(1)
    operands = used + list(shared) + list(own[0]) + list(own[1])
    high = TOK * 8
    in_specs = [pl.BlockSpec((high, step), lambda m: (0, m)) for _ in used]
    in_specs += [pl.BlockSpec((TOK, 2 * width), lambda m: (0, group), pipeline_mode=once) for _ in shared]
    in_specs += [pl.BlockSpec(b.shape, lambda m: (0, 0), pipeline_mode=once) for b in own[0] + own[1]]
    aliases = {}
    if partial is not None:
        if number < 2:
            aliases = {len(operands): 0}
        operands.append(partial)
        in_specs.append(pl.BlockSpec((step, 2 * width), lambda m: (m, 0)))
    if number == 2:
        out_specs = pl.BlockSpec((step, 2 * width), lambda m: (m, group))
        out_shape = jax.ShapeDtypeStruct((rows, full), BF16)
        if before is not None:
            aliases = {len(operands): 0}
            operands.append(before)
            in_specs.append(pl.BlockSpec(memory_space=pl.ANY))
    else:
        out_specs = pl.BlockSpec((step, 2 * width), lambda m: (m, 0))
        out_shape = jax.ShapeDtypeStruct((rows, 2 * width), F32)
    return pl.pallas_call(
        kernel,
        grid=(rows // step,),
        in_specs=in_specs,
        out_specs=out_specs,
        out_shape=out_shape,
        input_output_aliases=aliases,
        compiler_params=pltpu.CompilerParams(vmem_limit_bytes=LIMIT << 20),
        cost_estimate=pl.CostEstimate(
            flops=4 * rows * width * depth,
            bytes_accessed=4 * rows * TOK * 8 + 4 * depth * width + 12 * rows * width,
            transcendentals=0,
        ),
    )(*operands)


def send(block, pairs):
    return lax.ppermute(block, AXES, pairs)


def join(blocks, cols=slice(None)):
    return jnp.concatenate([b[:, cols] for b in blocks], axis=0)


def shards(activations, out_grad):
    full = out_grad.shape[1]
    width = full // 4
    me = (lax.axis_index("row") * 8 + lax.axis_index("col")) * 2 + lax.axis_index("rep")
    places = lax.dynamic_index_in_dim(jnp.asarray(tables()), me, 0, keepdims=False)
    tie = lax.optimization_barrier

    x1, z1 = send(out_grad, X_RING), send(out_grad, Z_RING)
    other = send(activations, REP_SWAP)
    up, down = send(activations, Y_RING), send(activations, Y_BACK)
    x1, z1, other, up, down = tie((x1, z1, other, up, down))

    x2, z2 = send(x1, X_RING), send(z1, Z_RING)
    far = send(up, Y_RING)
    other_up = send(other, Y_RING)
    swap_1 = send(join([activations, up, down]), CORE_SWAP)
    x2, z2, far, other_up, swap_1 = tie((x2, z2, far, other_up, swap_1))

    x3, z3 = send(x2, X_RING), send(z2, Z_RING)
    other_far, other_down = send(other_up, Y_RING), send(other, Y_BACK)
    swap_2 = send(join([far, other, other_up]), CORE_SWAP)
    mine = [(b, 0, 1) for b in (activations, up, down, far)]
    left_own = sort_tokens(places, 0, mine + [(swap_1, 0, 3), (swap_2, 0, 1)])
    first = [out_grad, x1, x2, z2]
    sums = [multiply([left_own, None], 0, first, [[], []], g, None, None, full) for g in range(2)]
    if EARLY == 0:
        x3, z3, other_far, other_down, swap_2, left_own = tie((x3, z3, other_far, other_down, swap_2, left_own))
    if EARLY == 1:
        x3, z3, other_far, other_down, swap_2, sums[0] = tie((x3, z3, other_far, other_down, swap_2, sums[0]))
    if EARLY == 2:
        x3, z3, other_far, other_down, swap_2, sums = tie((x3, z3, other_far, other_down, swap_2, sums))

    swap_3 = send(join([other_down, other_far]), CORE_SWAP)
    others = [(b, 0, 1) for b in (other, other_up, other_down, other_far)]
    left_other = sort_tokens(places, 1, others + [(swap_2, TOK, 2), (swap_3, 0, 2)])

    a, b = [[], []], [[], []]
    for g in range(2):
        at = 2 * g * width
        a[g].append(send(join([x1, x2, x3], slice(at, at + width)), Z_RING))
        b[g].append(send(join([z1, z2, z3], slice(at + width, at + 2 * width)), X_RING))
    if TIES >= 1:
        a[0][0], b[0][0], sums[0], sums[1] = tie((a[0][0], b[0][0], sums[0], sums[1]))
    if LEFT:
        a[1][0], b[1][0], left_other = tie((a[1][0], b[1][0], left_other))
    lefts = [left_own, left_other]
    for g in range(2):
        sums[g] = multiply(lefts, 1, [x3, z1, z3], (a[g][:1], b[g][:1]), g, sums[g], None, full)
    for step in range(2):
        for g in range(2):
            if step == 1 and TIES >= 2 + g:
                a[g][1], b[g][1], sums[g] = tie((a[g][1], b[g][1], sums[g]))
            a[g].append(send(a[g][-1], Z_RING))
            b[g].append(send(b[g][-1], X_RING))
    result = None
    for g in range(2):
        result = multiply(lefts, 2, [], (a[g][1:], b[g][1:]), g, sums[g], result, full)
    return result


def solution(mesh):
    placed = (P(("col", "rep"), "row"), P(("row", "rep"), "col"))
    return jax.shard_map(
        shards, mesh=mesh, in_specs=placed, out_specs=P("row", "col"), check_vma=False
    )
```

time: 1580 us -> 109 us (0.07)
  waiting for transfers between devices: 1410 us -> 36.2 us
  matrix products: 121 us -> 0 us
  Pallas kernels: 0 us -> 38.7 us
  starting transfers between devices: 0.37 us -> 29.3 us
  other arithmetic: 27.2 us -> 2.38 us
    psum x17 -> x0, waiting for transfers between devices: 1410 us -> none  [the longest x16 1180 us: from_root(): return lax.psum(jnp.where(mine, array, jnp.zeros_like(array)), axis)]
    dot_general x8 -> x0, matrix products: 121 us -> none  [outer_add(): lax.dot_general(left, right, (((0,), (0,)), ((), ())), preferred_element_...]
    pallas_call x0 -> x8, Pallas kernels: none -> 38.7 us  [the longest x6 32.8 us: multiply(): pl.pallas_call(kernel, grid=(rows // step,), in_specs=in_specs, out_specs...]
    ppermute x0 -> x28, waiting for transfers between devices: none -> 36.2 us  [send(): return lax.ppermute(block, AXES, pairs)]
    ppermute x0 -> x28, starting transfers between devices: none -> 29.3 us  [send(): return lax.ppermute(block, AXES, pairs)]
    select_n x16 -> x0, other arithmetic: 15.9 us -> none  [from_root(): return lax.psum(jnp.where(mine, array, jnp.zeros_like(array)), axis)]
  transfers between devices with their start and end apart: 17 -> 28, of which waited for: 17 -> 14; matrix products, arithmetic and copies ran while one was open for 1% -> 1% of each run, Pallas kernels for 0% -> 30%
where the time goes in v2:
time: 109 us
  Pallas kernels  38.7 us (36%)
  waiting for transfers between devices  36.2 us (33%)
  starting transfers between devices  29.3 us (27%)
  other arithmetic  2.38 us (2%)
  local copies, waits for them, and re-layouts  1.93 us (2%)
    ppermute x28, waiting for transfers between devices, send(): return lax.ppermute(block, AXES, pairs)  36.2 us
    pallas_call x6, Pallas kernels, multiply(): pl.pallas_call(kernel, grid=(rows // step,), in_specs=in_specs, out_specs...  32.8 us
    ppermute x28, starting transfers between devices, send(): return lax.ppermute(block, AXES, pairs)  29.3 us
    pallas_call x2, Pallas kernels, sort_tokens(): pl.pallas_call(kernel, grid_spec=pltpu.PrefetchScalarGridSpec(num_scalar_...  5.95 us
    concatenate x7, other arithmetic, join(): return jnp.concatenate([b[:, cols] for b in blocks], axis=0)  2.38 us
  transfers between devices with their start and end apart: 28, of which 14 were waited for; matrix products, arithmetic and copies ran while one was open for 1% of the time, Pallas kernels for 30%

profile of v2, /device:TPU:0, one launch (start us, length us, event | category | flops | bytes accessed | tf_op | source)
XLA Modules:
  0.0 108.8 jit_solution(3536323411206288503)
XLA Ops:
  0.0 2.0 %collective-permute-start.1 = (bf16[128,3072]{1,0:T(8,128)(2,1)}, bf16[128,3072]{1,0:T(8,128)(2,1)S(1)}, u32[]{:S(2)}, u32[]{:S(2)}) collective-permute-start(bf16[128,3072]{1,0:T(8,128)(2,1)} %refs_1_.3), channel_id=1, source_target_pairs={{0,1},{2,67},{1,64},{3,2},{64,65},{66,3},{65,0},{67,66},{4,5},{6,7... | collective-permute-start | bytes 2359304 | tf_op jit(solution)/shard_map/ppermute | solution.py:168
  3.5 3.0 %collective-permute-start.4 = (bf16[128,1536]{1,0:T(8,128)(2,1)}, bf16[128,1536]{1,0:T(8,128)(2,1)S(1)}, u32[]{:S(2)}, u32[]{:S(2)}) collective-permute-start(bf16[128,1536]{1,0:T(8,128)(2,1)} %refs_0_.1), channel_id=1, source_target_pairs={{0,12},{2,6},{1,13},{3,7},{64,76},{66,70},{65,77},{67,71},{4,0},{6... | collective-permute-start | bytes 1179656 | tf_op jit(solution)/shard_map/ppermute | solution.py:168
  6.5 1.9 %collective-permute-start.2 = (bf16[128,1536]{1,0:T(8,128)(2,1)}, bf16[128,1536]{1,0:T(8,128)(2,1)S(1)}, u32[]{:S(2)}, u32[]{:S(2)}) collective-permute-start(bf16[128,1536]{1,0:T(8,128)(2,1)} %refs_0_.1), channel_id=1, source_target_pairs={{0,1},{2,3},{1,0},{3,2},{64,65},{66,67},{65,64},{67,66},{4,5},{6,7... | collective-permute-start | bytes 1179656 | tf_op jit(solution)/shard_map/ppermute | solution.py:168
  8.4 6.1 %collective-permute-done.4.refs_2_ = bf16[128,1536]{1,0:T(8,128)(2,1)S(1)} collective-permute-done((bf16[128,1536]{1,0:T(8,128)(2,1)}, bf16[128,1536]{1,0:T(8,128)(2,1)S(1)}, u32[]{:S(2)}, u32[]{:S(2)}) %collective-permute-start.4) | collective-permute-done | bytes 393248 | tf_op jit(solution)/shard_map/ppermute | solution.py:168
  14.6 4.1 %collective-permute-done.3.refs_1_ = bf16[128,1536]{1,0:T(8,128)(2,1)S(1)} collective-permute-done((bf16[128,1536]{1,0:T(8,128)(2,1)}, bf16[128,1536]{1,0:T(8,128)(2,1)S(1)}, u32[]{:S(2)}, u32[]{:S(2)}) %collective-permute-start.3) | collective-permute-done | bytes 393248 | tf_op jit(solution)/shard_map/ppermute | solution.py:168
  18.7 1.6 %collective-permute-done.2.refs_0_ = bf16[128,1536]{1,0:T(8,128)(2,1)S(1)} collective-permute-done((bf16[128,1536]{1,0:T(8,128)(2,1)}, bf16[128,1536]{1,0:T(8,128)(2,1)S(1)}, u32[]{:S(2)}, u32[]{:S(2)}) %collective-permute-start.2) | collective-permute-done | bytes 393248 | tf_op jit(solution)/shard_map/ppermute | solution.py:168
  23.0 2.4 %collective-permute-start.6 = (bf16[128,3072]{1,0:T(8,128)(2,1)S(1)}, bf16[128,3072]{1,0:T(8,128)(2,1)S(1)}, u32[]{:S(2)}, u32[]{:S(2)}) collective-permute-start(bf16[128,3072]{1,0:T(8,128)(2,1)S(1)} %collective-permute-done.1.refs_3_), channel_id=1, source_target_pairs={{0,1},{2,67},{1,64},{3,2},{64,65},{66,3},{65,0},{67,66},{4,5},{6,7... | collective-permute-start | bytes 2359304 | tf_op jit(solution)/shard_map/ppermute | solution.py:168
  28.5 5.8 %collective-permute-done.7.refs_3_ = bf16[128,1536]{1,0:T(8,128)(2,1)S(1)} collective-permute-done((bf16[128,1536]{1,0:T(8,128)(2,1)S(1)}, bf16[128,1536]{1,0:T(8,128)(2,1)S(1)}, u32[]{:S(2)}, u32[]{:S(2)}) %collective-permute-start.7) | collective-permute-done | bytes 393248 | tf_op jit(solution)/shard_map/ppermute | solution.py:168
  34.4 4.2 %collective-permute-done.8.refs_1_ = bf16[128,1536]{1,0:T(8,128)(2,1)S(1)} collective-permute-done((bf16[128,1536]{1,0:T(8,128)(2,1)S(1)}, bf16[128,1536]{1,0:T(8,128)(2,1)S(1)}, u32[]{:S(2)}, u32[]{:S(2)}) %collective-permute-start.8) | collective-permute-done | bytes 393248 | tf_op jit(solution)/shard_map/ppermute | solution.py:168
  40.7 1.7 %collective-permute-start.10 = (bf16[384,1536]{1,0:T(8,128)(2,1)}, bf16[384,1536]{1,0:T(8,128)(2,1)}, u32[]{:S(2)}, u32[]{:S(2)}) collective-permute-start(bf16[384,1536]{1,0:T(8,128)(2,1)} %pad_maximum_fusion.1), channel_id=1, source_target_pairs={{0,2},{2,0},{1,3},{3,1},{64,66},{66,64},{65,67},{67,65},{4,6},{6,4... | collective-permute-start | bytes 3538952 | tf_op jit(solution)/shard_map/ppermute | solution.py:168
  44.2 2.5 %collective-permute-start.14 = (bf16[128,1536]{1,0:T(8,128)(2,1)S(1)}, bf16[128,1536]{1,0:T(8,128)(2,1)S(1)}, u32[]{:S(2)}, u32[]{:S(2)}) collective-permute-start(bf16[128,1536]{1,0:T(8,128)(2,1)S(1)} %collective-permute-done.2.refs_0_), channel_id=1, source_target_pairs={{0,12},{2,6},{1,13},{3,7},{64,76},{66,70},{65,77},{67,71},{4,0},{6... | collective-permute-start | bytes 1179656 | tf_op jit(solution)/shard_map/ppermute | solution.py:168
  47.0 3.0 %shard_map.37.refs_0_ = bf16[1024,1536]{1,0:T(8,128)(2,1)S(1)} custom-call(s32[2,8]{1,0:T(2,128)S(1)} %dynamic-slice_bitcast_fusion.places_ref, bf16[128,1536]{1,0:T(8,128)(2,1)S(1)} %copy-done.3, bf16[128,1536]{1,0:T(8,128)(2,1)S(1)} %copy-done.7, bf16[128,1536]{1,0:T(8,128)(2,1)S(1)} %copy-done.5, bf16[128,1536]{1,0:T(8,128)(2,1)S(1)} %copy-done.9, ...), custom_call_target="tpu_custom_call" | custom-call | bytes 6291456 | tf_op jit(solution)/shard_map/pallas_call | solution.py:85
  50.0 4.1 %shard_map.38.refs_7_ = f32[1536,1536]{1,0:T(8,128)S(1)} custom-call(bf16[1024,1536]{1,0:T(8,128)(2,1)S(1)} %shard_map.37.refs_0_, bf16[128,3072]{1,0:T(8,128)(2,1)S(1)} %copy-done, bf16[128,3072]{1,0:T(8,128)(2,1)S(1)} %collective-permute-done.refs_2_, bf16[128,3072]{1,0:T(8,128)(2,1)S(1)} %collective-permute-done.5.refs_3_, ...), custom_call_target="tpu_custom_call" | custom-call | flops 2415919104 | bytes 22020096 | tf_op jit(solution)/shard_map/pallas_call | solution.py:151
  54.1 1.9 %collective-permute-done.14.refs_2_ = bf16[128,1536]{1,0:T(8,128)(2,1)S(1)} collective-permute-done((bf16[128,1536]{1,0:T(8,128)(2,1)S(1)}, bf16[128,1536]{1,0:T(8,128)(2,1)S(1)}, u32[]{:S(2)}, u32[]{:S(2)}) %collective-permute-start.14) | collective-permute-done | bytes 393248 | tf_op jit(solution)/shard_map/ppermute | solution.py:168
  55.9 1.6 %collective-permute-done.13.refs_3_ = bf16[128,1536]{1,0:T(8,128)(2,1)S(1)} collective-permute-done((bf16[128,1536]{1,0:T(8,128)(2,1)S(1)}, bf16[128,1536]{1,0:T(8,128)(2,1)S(1)}, u32[]{:S(2)}, u32[]{:S(2)}) %collective-permute-start.13) | collective-permute-done | bytes 393248 | tf_op jit(solution)/shard_map/ppermute | solution.py:168
  61.7 4.1 %shard_map.40.refs_7_ = f32[1536,1536]{1,0:T(8,128)S(1)} custom-call(bf16[1024,1536]{1,0:T(8,128)(2,1)S(1)} %shard_map.37.refs_0_, bf16[128,3072]{1,0:T(8,128)(2,1)S(1)} %copy-done, bf16[128,3072]{1,0:T(8,128)(2,1)S(1)} %collective-permute-done.refs_2_, bf16[128,3072]{1,0:T(8,128)(2,1)S(1)} %collective-permute-done.5.refs_3_, ...), custom_call_target="tpu_custom_call" | custom-call | flops 2415919104 | bytes 22020096 | tf_op jit(solution)/shard_map/pallas_call | solution.py:151
  65.8 3.0 %collective-permute-done.22.refs_5_ = bf16[384,768]{1,0:T(8,128)(2,1)S(1)} collective-permute-done((bf16[384,768]{1,0:T(8,128)(2,1)S(1)}, bf16[384,768]{1,0:T(8,128)(2,1)S(1)}, u32[]{:S(2)}, u32[]{:S(2)}) %collective-permute-start.22) | collective-permute-done | bytes 589856 | tf_op jit(solution)/shard_map/ppermute | solution.py:168
  70.7 2.9 %shard_map.39.refs_1_ = bf16[1024,1536]{1,0:T(8,128)(2,1)S(1)} custom-call(s32[2,8]{1,0:T(2,128)S(1)} %dynamic-slice_bitcast_fusion.places_ref, bf16[128,1536]{1,0:T(8,128)(2,1)S(1)} %collective-permute-done.2.refs_0_, bf16[128,1536]{1,0:T(8,128)(2,1)S(1)} %copy-done.2, bf16[128,1536]{1,0:T(8,128)(2,1)S(1)} %collective-permute-done.14.refs_2_, ...), custom_call_target="tpu_custom_call" | custom-call | bytes 6291456 | tf_op jit(solution)/shard_map/pallas_call | solution.py:85
  77.0 6.0 %shard_map.42.refs_6_ = f32[1536,1536]{1,0:T(8,128)S(1)} custom-call(bf16[1024,1536]{1,0:T(8,128)(2,1)S(1)} %shard_map.37.refs_0_, bf16[1024,1536]{1,0:T(8,128)(2,1)S(1)} %shard_map.39.refs_1_, bf16[128,3072]{1,0:T(8,128)(2,1)S(1)} %collective-permute-done.11.refs_2_, ...), custom_call_target="tpu_custom_call", output_to_operand_aliasing={{}: (7, {})} | custom-call | flops 3623878656 | bytes 22806528 | tf_op jit(solution)/shard_map/pallas_call | solution.py:151
  83.0 2.0 %collective-permute-start.26 = (bf16[384,768]{1,0:T(8,128)(2,1)S(1)}, bf16[384,768]{1,0:T(8,128)(2,1)S(1)}, u32[]{:S(2)}, u32[]{:S(2)}) collective-permute-start(bf16[384,768]{1,0:T(8,128)(2,1)S(1)} %collective-permute-done.24.refs_2_), channel_id=1, source_target_pairs={{0,1},{2,67},{1,64},{3,2},{64,65},{66,3},{65,0},{67,66},{4,5},{6,7... | collective-permute-start | bytes 1769480 | tf_op jit(solution)/shard_map/ppermute | solution.py:168
  85.5 2.3 %collective-permute-done.18.refs_2_ = bf16[384,768]{1,0:T(8,128)(2,1)S(1)} collective-permute-done((bf16[384,768]{1,0:T(8,128)(2,1)S(1)}, bf16[384,768]{1,0:T(8,128)(2,1)S(1)}, u32[]{:S(2)}, u32[]{:S(2)}) %collective-permute-start.18) | collective-permute-done | bytes 589856 | tf_op jit(solution)/shard_map/ppermute | solution.py:168
  88.7 6.0 %shard_map.41.refs_6_ = f32[1536,1536]{1,0:T(8,128)S(1)} custom-call(bf16[1024,1536]{1,0:T(8,128)(2,1)S(1)} %shard_map.37.refs_0_, bf16[1024,1536]{1,0:T(8,128)(2,1)S(1)} %shard_map.39.refs_1_, bf16[128,3072]{1,0:T(8,128)(2,1)S(1)} %collective-permute-done.11.refs_2_, ...), custom_call_target="tpu_custom_call", output_to_operand_aliasing={{}: (7, {})} | custom-call | flops 3623878656 | bytes 22806528 | tf_op jit(solution)/shard_map/pallas_call | solution.py:151
  96.1 6.4 %shard_map.43.refs_7_ = bf16[1536,3072]{1,0:T(8,128)(2,1)} custom-call(bf16[1024,1536]{1,0:T(8,128)(2,1)S(1)} %shard_map.37.refs_0_, bf16[1024,1536]{1,0:T(8,128)(2,1)S(1)} %shard_map.39.refs_1_, bf16[384,768]{1,0:T(8,128)(2,1)S(1)} %collective-permute-done.24.refs_2_, bf16[384,768]{1,0:T(8,128)(2,1)S(1)} %collective-permute-done.26.refs_3_, ...), custom_call_target="tpu_custom_call" | custom-call | flops 3623878656 | bytes 22806528 | tf_op jit(solution)/shard_map/pallas_call | solution.py:151
  102.5 6.4 %shard_map.44 = bf16[1536,3072]{1,0:T(8,128)(2,1)} custom-call(bf16[1024,1536]{1,0:T(8,128)(2,1)S(1)} %shard_map.37.refs_0_, bf16[1024,1536]{1,0:T(8,128)(2,1)S(1)} %shard_map.39.refs_1_, bf16[384,768]{1,0:T(8,128)(2,1)S(1)} %collective-permute-done.18.refs_2_, bf16[384,768]{1,0:T(8,128)(2,1)S(1)} %collective-permute-done.19.refs_3_, ...), custom_call_target="tpu_custom_call", output_to_operand_aliasing={{}: (7, {})} | custom-call | flops 3623878656 | bytes 22806528 | tf_op jit(solution)/shard_map/pallas_call | solution.py:151
  (75 shorter events, 23.6 us)
Async XLA Ops:
  0.0 20.3 %collective-permute-start.1 = (bf16[128,3072]{1,0:T(8,128)(2,1)}, bf16[128,3072]{1,0:T(8,128)(2,1)S(1)}, u32[]{:S(2)}, u32[]{:S(2)}) collective-permute-start(bf16[128,3072]{1,0:T(8,128)(2,1)} %refs_1_.3), channel_id=1, source_target_pairs={{0,1},{2,67},{1,64},{3,2},{64,65},{66,3},{65,0},{67,66},{4,5},{6,7... | collective-permute-start | bytes 2359304 | tf_op jit(solution)/shard_map/ppermute | solution.py:168
  2.0 18.3 %collective-permute-start = (bf16[128,3072]{1,0:T(8,128)(2,1)}, bf16[128,3072]{1,0:T(8,128)(2,1)S(1)}, u32[]{:S(2)}, u32[]{:S(2)}) collective-permute-start(bf16[128,3072]{1,0:T(8,128)(2,1)} %refs_1_.3), channel_id=1, source_target_pairs={{0,16},{2,50},{1,17},{3,51},{64,80},{66,114},{65,81},{67,115},{4,2... | collective-permute-start | bytes 2359304 | tf_op jit(solution)/shard_map/ppermute | solution.py:168
  3.5 11.1 %collective-permute-start.4 = (bf16[128,1536]{1,0:T(8,128)(2,1)}, bf16[128,1536]{1,0:T(8,128)(2,1)S(1)}, u32[]{:S(2)}, u32[]{:S(2)}) collective-permute-start(bf16[128,1536]{1,0:T(8,128)(2,1)} %refs_0_.1), channel_id=1, source_target_pairs={{0,12},{2,6},{1,13},{3,7},{64,76},{66,70},{65,77},{67,71},{4,0},{6... | collective-permute-start | bytes 1179656 | tf_op jit(solution)/shard_map/ppermute | solution.py:168
  6.5 12.1 %collective-permute-start.3 = (bf16[128,1536]{1,0:T(8,128)(2,1)}, bf16[128,1536]{1,0:T(8,128)(2,1)S(1)}, u32[]{:S(2)}, u32[]{:S(2)}) collective-permute-start(bf16[128,1536]{1,0:T(8,128)(2,1)} %refs_0_.1), channel_id=1, source_target_pairs={{0,4},{2,14},{1,5},{3,15},{64,68},{66,78},{65,69},{67,79},{4,8},{6... | collective-permute-start | bytes 1179656 | tf_op jit(solution)/shard_map/ppermute | solution.py:168
  6.5 13.7 %collective-permute-start.2 = (bf16[128,1536]{1,0:T(8,128)(2,1)}, bf16[128,1536]{1,0:T(8,128)(2,1)S(1)}, u32[]{:S(2)}, u32[]{:S(2)}) collective-permute-start(bf16[128,1536]{1,0:T(8,128)(2,1)} %refs_0_.1), channel_id=1, source_target_pairs={{0,1},{2,3},{1,0},{3,2},{64,65},{66,67},{65,64},{67,66},{4,5},{6,7... | collective-permute-start | bytes 1179656 | tf_op jit(solution)/shard_map/ppermute | solution.py:168
  21.3 17.2 %collective-permute-start.9 = (bf16[384,1536]{1,0:T(8,128)(2,1)S(1)}, bf16[384,1536]{1,0:T(8,128)(2,1)S(1)}, u32[]{:S(2)}, u32[]{:S(2)}) collective-permute-start(bf16[384,1536]{1,0:T(8,128)(2,1)S(1)} %pad_maximum_fusion), channel_id=1, source_target_pairs={{0,2},{2,0},{1,3},{3,1},{64,66},{66,64},{65,67},{67,65},{4,6},{6,4... | collective-permute-start | bytes 3538952 | tf_op jit(solution)/shard_map/ppermute | solution.py:168
  21.4 17.1 %collective-permute-start.5 = (bf16[128,3072]{1,0:T(8,128)(2,1)S(1)}, bf16[128,3072]{1,0:T(8,128)(2,1)S(1)}, u32[]{:S(2)}, u32[]{:S(2)}) collective-permute-start(bf16[128,3072]{1,0:T(8,128)(2,1)S(1)} %collective-permute-done.refs_2_), channel_id=1, source_target_pairs={{0,16},{2,50},{1,17},{3,51},{64,80},{66,114},{65,81},{67,115},{4,2... | collective-permute-start | bytes 2359304 | tf_op jit(solution)/shard_map/ppermute | solution.py:168
  23.0 15.6 %collective-permute-start.6 = (bf16[128,3072]{1,0:T(8,128)(2,1)S(1)}, bf16[128,3072]{1,0:T(8,128)(2,1)S(1)}, u32[]{:S(2)}, u32[]{:S(2)}) collective-permute-start(bf16[128,3072]{1,0:T(8,128)(2,1)S(1)} %collective-permute-done.1.refs_3_), channel_id=1, source_target_pairs={{0,1},{2,67},{1,64},{3,2},{64,65},{66,3},{65,0},{67,66},{4,5},{6,7... | collective-permute-start | bytes 2359304 | tf_op jit(solution)/shard_map/ppermute | solution.py:168
  27.0 11.6 %collective-permute-start.8 = (bf16[128,1536]{1,0:T(8,128)(2,1)S(1)}, bf16[128,1536]{1,0:T(8,128)(2,1)S(1)}, u32[]{:S(2)}, u32[]{:S(2)}) collective-permute-start(bf16[128,1536]{1,0:T(8,128)(2,1)S(1)} %collective-permute-done.2.refs_0_), channel_id=1, source_target_pairs={{0,4},{2,14},{1,5},{3,15},{64,68},{66,78},{65,69},{67,79},{4,8},{6... | collective-permute-start | bytes 1179656 | tf_op jit(solution)/shard_map/ppermute | solution.py:168
  42.5 15.1 %collective-permute-start.11 = (bf16[128,3072]{1,0:T(8,128)(2,1)S(1)}, bf16[128,3072]{1,0:T(8,128)(2,1)S(1)}, u32[]{:S(2)}, u32[]{:S(2)}) collective-permute-start(bf16[128,3072]{1,0:T(8,128)(2,1)S(1)} %collective-permute-done.5.refs_3_), channel_id=1, source_target_pairs={{0,16},{2,50},{1,17},{3,51},{64,80},{66,114},{65,81},{67,115},{4,2... | collective-permute-start | bytes 2359304 | tf_op jit(solution)/shard_map/ppermute | solution.py:168
  42.5 15.1 %collective-permute-start.12 = (bf16[128,3072]{1,0:T(8,128)(2,1)S(1)}, bf16[128,3072]{1,0:T(8,128)(2,1)S(1)}, u32[]{:S(2)}, u32[]{:S(2)}) collective-permute-start(bf16[128,3072]{1,0:T(8,128)(2,1)S(1)} %collective-permute-done.6.refs_4_), channel_id=1, source_target_pairs={{0,1},{2,67},{1,64},{3,2},{64,65},{66,3},{65,0},{67,66},{4,5},{6,7... | collective-permute-start | bytes 2359304 | tf_op jit(solution)/shard_map/ppermute | solution.py:168
  44.2 11.7 %collective-permute-start.14 = (bf16[128,1536]{1,0:T(8,128)(2,1)S(1)}, bf16[128,1536]{1,0:T(8,128)(2,1)S(1)}, u32[]{:S(2)}, u32[]{:S(2)}) collective-permute-start(bf16[128,1536]{1,0:T(8,128)(2,1)S(1)} %collective-permute-done.2.refs_0_), channel_id=1, source_target_pairs={{0,12},{2,6},{1,13},{3,7},{64,76},{66,70},{65,77},{67,71},{4,0},{6... | collective-permute-start | bytes 1179656 | tf_op jit(solution)/shard_map/ppermute | solution.py:168
  57.7 11.2 %collective-permute-start.22 = (bf16[384,768]{1,0:T(8,128)(2,1)S(1)}, bf16[384,768]{1,0:T(8,128)(2,1)S(1)}, u32[]{:S(2)}, u32[]{:S(2)}) collective-permute-start(bf16[384,768]{1,0:T(8,128)(2,1)S(1)} %pad_maximum_fusion.5), channel_id=1, source_target_pairs={{0,1},{2,67},{1,64},{3,2},{64,65},{66,3},{65,0},{67,66},{4,5},{6,7... | collective-permute-start | bytes 1769480 | tf_op jit(solution)/shard_map/ppermute | solution.py:168
  58.5 11.2 %collective-permute-start.23 = (bf16[384,768]{1,0:T(8,128)(2,1)S(1)}, bf16[384,768]{1,0:T(8,128)(2,1)S(1)}, u32[]{:S(2)}, u32[]{:S(2)}) collective-permute-start(bf16[384,768]{1,0:T(8,128)(2,1)S(1)} %pad_maximum_fusion.6), channel_id=1, source_target_pairs={{0,16},{2,50},{1,17},{3,51},{64,80},{66,114},{65,81},{67,115},{4,2... | collective-permute-start | bytes 1769480 | tf_op jit(solution)/shard_map/ppermute | solution.py:168
  60.0 15.2 %collective-permute-start.15 = (bf16[384,768]{1,0:T(8,128)(2,1)S(1)}, bf16[384,768]{1,0:T(8,128)(2,1)S(1)}, u32[]{:S(2)}, u32[]{:S(2)}) collective-permute-start(bf16[384,768]{1,0:T(8,128)(2,1)S(1)} %pad_maximum_fusion.3), channel_id=1, source_target_pairs={{0,1},{2,67},{1,64},{3,2},{64,65},{66,3},{65,0},{67,66},{4,5},{6,7... | collective-permute-start | bytes 1769480 | tf_op jit(solution)/shard_map/ppermute | solution.py:168
  60.2 15.9 %collective-permute-start.16 = (bf16[384,768]{1,0:T(8,128)(2,1)S(1)}, bf16[384,768]{1,0:T(8,128)(2,1)S(1)}, u32[]{:S(2)}, u32[]{:S(2)}) collective-permute-start(bf16[384,768]{1,0:T(8,128)(2,1)S(1)} %pad_maximum_fusion.4), channel_id=1, source_target_pairs={{0,16},{2,50},{1,17},{3,51},{64,80},{66,114},{65,81},{67,115},{4,2... | collective-permute-start | bytes 1769480 | tf_op jit(solution)/shard_map/ppermute | solution.py:168
  69.7 13.3 %collective-permute-start.24 = (bf16[384,768]{1,0:T(8,128)(2,1)S(1)}, bf16[384,768]{1,0:T(8,128)(2,1)S(1)}, u32[]{:S(2)}, u32[]{:S(2)}) collective-permute-start(bf16[384,768]{1,0:T(8,128)(2,1)S(1)} %collective-permute-done.22.refs_5_), channel_id=1, source_target_pairs={{0,1},{2,67},{1,64},{3,2},{64,65},{66,3},{65,0},{67,66},{4,5},{6,7... | collective-permute-start | bytes 1769480 | tf_op jit(solution)/shard_map/ppermute | solution.py:168
  70.7 12.3 %collective-permute-start.25 = (bf16[384,768]{1,0:T(8,128)(2,1)S(1)}, bf16[384,768]{1,0:T(8,128)(2,1)S(1)}, u32[]{:S(2)}, u32[]{:S(2)}) collective-permute-start(bf16[384,768]{1,0:T(8,128)(2,1)S(1)} %collective-permute-done.23.refs_6_), channel_id=1, source_target_pairs={{0,16},{2,50},{1,17},{3,51},{64,80},{66,114},{65,81},{67,115},{4,2... | collective-permute-start | bytes 1769480 | tf_op jit(solution)/shard_map/ppermute | solution.py:168
  76.0 11.8 %collective-permute-start.18 = (bf16[384,768]{1,0:T(8,128)(2,1)S(1)}, bf16[384,768]{1,0:T(8,128)(2,1)S(1)}, u32[]{:S(2)}, u32[]{:S(2)}) collective-permute-start(bf16[384,768]{1,0:T(8,128)(2,1)S(1)} %collective-permute-done.15.refs_5_), channel_id=1, source_target_pairs={{0,1},{2,67},{1,64},{3,2},{64,65},{66,3},{65,0},{67,66},{4,5},{6,7... | collective-permute-start | bytes 1769480 | tf_op jit(solution)/shard_map/ppermute | solution.py:168
  77.0 11.7 %collective-permute-start.20 = (bf16[384,768]{1,0:T(8,128)(2,1)S(1)}, bf16[384,768]{1,0:T(8,128)(2,1)S(1)}, u32[]{:S(2)}, u32[]{:S(2)}) collective-permute-start(bf16[384,768]{1,0:T(8,128)(2,1)S(1)} %collective-permute-done.16.refs_6_), channel_id=1, source_target_pairs={{0,16},{2,50},{1,17},{3,51},{64,80},{66,114},{65,81},{67,115},{4,2... | collective-permute-start | bytes 1769480 | tf_op jit(solution)/shard_map/ppermute | solution.py:168
  83.0 11.7 %collective-permute-start.26 = (bf16[384,768]{1,0:T(8,128)(2,1)S(1)}, bf16[384,768]{1,0:T(8,128)(2,1)S(1)}, u32[]{:S(2)}, u32[]{:S(2)}) collective-permute-start(bf16[384,768]{1,0:T(8,128)(2,1)S(1)} %collective-permute-done.24.refs_2_), channel_id=1, source_target_pairs={{0,1},{2,67},{1,64},{3,2},{64,65},{66,3},{65,0},{67,66},{4,5},{6,7... | collective-permute-start | bytes 1769480 | tf_op jit(solution)/shard_map/ppermute | solution.py:168
  85.0 11.1 %collective-permute-start.27 = (bf16[384,768]{1,0:T(8,128)(2,1)S(1)}, bf16[384,768]{1,0:T(8,128)(2,1)S(1)}, u32[]{:S(2)}, u32[]{:S(2)}) collective-permute-start(bf16[384,768]{1,0:T(8,128)(2,1)S(1)} %collective-permute-done.25.refs_4_), channel_id=1, source_target_pairs={{0,16},{2,50},{1,17},{3,51},{64,80},{66,114},{65,81},{67,115},{4,2... | collective-permute-start | bytes 1769480 | tf_op jit(solution)/shard_map/ppermute | solution.py:168
  87.8 14.6 %collective-permute-start.19 = (bf16[384,768]{1,0:T(8,128)(2,1)S(1)}, bf16[384,768]{1,0:T(8,128)(2,1)S(1)}, u32[]{:S(2)}, u32[]{:S(2)}) collective-permute-start(bf16[384,768]{1,0:T(8,128)(2,1)S(1)} %collective-permute-done.18.refs_2_), channel_id=1, source_target_pairs={{0,1},{2,67},{1,64},{3,2},{64,65},{66,3},{65,0},{67,66},{4,5},{6,7... | collective-permute-start | bytes 1769480 | tf_op jit(solution)/shard_map/ppermute | solution.py:168
  88.7 13.8 %collective-permute-start.21 = (bf16[384,768]{1,0:T(8,128)(2,1)S(1)}, bf16[384,768]{1,0:T(8,128)(2,1)S(1)}, u32[]{:S(2)}, u32[]{:S(2)}) collective-permute-start(bf16[384,768]{1,0:T(8,128)(2,1)S(1)} %collective-permute-done.20.refs_4_), channel_id=1, source_target_pairs={{0,16},{2,50},{1,17},{3,51},{64,80},{66,114},{65,81},{67,115},{4,2... | collective-permute-start | bytes 1769480 | tf_op jit(solution)/shard_map/ppermute | solution.py:168
  (16 other events, 81.2 us)

commit v3 on v2

--- a/solution.py
+++ b/solution.py
@@ -10,8 +10,10 @@
 TOK = 128
 LIMIT = 16
 TIES = 2
-EARLY = 1
-LEFT = 1
+HOLD = 2
+SPLIT = 1
+SWAP = 0
+STEP = 512
 F32 = jnp.float32
 BF16 = jnp.bfloat16
 
@@ -38,7 +40,10 @@
 CORE_SWAP = [(device(x, y, z, c), device(x, y, z, 1 - c)) for x, y, z, c in every()]
 REP_SWAP = [(device(x, y, z, c), device(x, y, z ^ 1, c)) for x, y, z, c in every()]
 
-KINDS = [[(i, j) for j in (p, p + 2) for i in range(4)] for p in range(2)]
+KINDS = [
+    [(0, 0), (1, 0), (2, 0), (0, 2), (3, 0), (1, 2), (2, 2), (3, 2)],
+    [(i, j) for j in (1, 3) for i in range(4)],
+]
 
 
 def inner(part, step):
@@ -71,27 +76,35 @@
 def sort_tokens(places, kind, pieces):
     arrays = [p[0] for p in pieces]
     wide = arrays[0].shape[1]
-    step = 512
 
     def kernel(places_ref, *refs):
-        n = 0
+        sems = refs[-1]
+        copies = []
         for ref, (_, first, blocks) in zip(refs, pieces):
             for b in range(blocks):
+                n = len(copies)
                 to = pl.multiple_of(places_ref[kind, n] * TOK, TOK)
-                refs[-1][pl.ds(to, TOK), :] = ref[first + b * TOK : first + (b + 1) * TOK, :]
-                n += 1
+                copies.append(
+                    pltpu.make_async_copy(
+                        ref.at[pl.ds(first + b * TOK, TOK)], refs[-2].at[pl.ds(to, TOK)], sems.at[n]
+                    )
+                )
+                copies[-1].start()
+        for copy in copies:
+            copy.wait()
 
     total = TOK * 8
     return pl.pallas_call(
         kernel,
         grid_spec=pltpu.PrefetchScalarGridSpec(
             num_scalar_prefetch=1,
-            grid=(wide // step,),
-            in_specs=[pl.BlockSpec((a.shape[0], step), lambda i, t: (0, i)) for a in arrays],
-            out_specs=pl.BlockSpec((total, step), lambda i, t: (0, i)),
+            grid=(1,),
+            in_specs=[pl.BlockSpec(memory_space=pl.ANY) for a in arrays],
+            out_specs=pl.BlockSpec(memory_space=pl.ANY),
+            scratch_shapes=[pltpu.SemaphoreType.DMA((8,))],
         ),
         out_shape=jax.ShapeDtypeStruct((total, wide), BF16),
-        compiler_params=pltpu.CompilerParams(vmem_limit_bytes=LIMIT << 20),
+        compiler_params=pltpu.CompilerParams(vmem_limit_bytes=1 << 20),
         cost_estimate=pl.CostEstimate(flops=0, bytes_accessed=4 * wide * total, transcendentals=0),
     )(places, *arrays)
 
@@ -101,10 +114,11 @@
     used = [l for l in lefts if l is not None]
     slot = [None if l is None else sum(m is not None for m in lefts[:n]) for n, l in enumerate(lefts)]
     rows = used[0].shape[1]
-    step = 256
+    step = STEP
     order = PASSES[number]
     depth = TOK * len(order[0])
     n_own = len(own[0])
+    skip = (0 if number == 0 else 4, 0)
 
     def kernel(*refs):
         left_refs, refs = refs[: len(used)], refs[len(used) :]
@@ -116,7 +130,7 @@
             cols = slice(part * width, (part + 1) * width)
             lhs = []
             for i, j in order[part]:
-                at = KINDS[j % 2].index((i, j)) * TOK
+                at = (KINDS[j % 2].index((i, j)) - skip[j % 2]) * TOK
                 lhs.append(left_refs[slot[j % 2]][at : at + TOK, :])
             lhs = jnp.concatenate(lhs, axis=0)
             rhs = [r[:, cols] for r in shared_refs] + [r[...] for r in own_refs[part]]
@@ -128,8 +142,8 @@
 
     once = pl.Buffered(1)
     operands = used + list(shared) + list(own[0]) + list(own[1])
-    high = TOK * 8
-    in_specs = [pl.BlockSpec((high, step), lambda m: (0, m)) for _ in used]
+    in_specs = [pl.BlockSpec((4 * TOK, step), lambda m: (skip[0] // 4, m))]
+    in_specs += [pl.BlockSpec((8 * TOK, step), lambda m: (0, m)) for _ in used[1:]]
     in_specs += [pl.BlockSpec((TOK, 2 * width), lambda m: (0, group), pipeline_mode=once) for _ in shared]
     in_specs += [pl.BlockSpec(b.shape, lambda m: (0, 0), pipeline_mode=once) for b in own[0] + own[1]]
     aliases = {}
@@ -172,6 +186,10 @@
     return jnp.concatenate([b[:, cols] for b in blocks], axis=0)
 
 
+def whole(arrays):
+    return [(a, 0, a.shape[0] // TOK) for a in arrays]
+
+
 def shards(activations, out_grad):
     full = out_grad.shape[1]
     width = full // 4
@@ -187,35 +205,48 @@
     x2, z2 = send(x1, X_RING), send(z1, Z_RING)
     far = send(up, Y_RING)
     other_up = send(other, Y_RING)
-    swap_1 = send(join([activations, up, down]), CORE_SWAP)
-    x2, z2, far, other_up, swap_1 = tie((x2, z2, far, other_up, swap_1))
-
+    if SWAP == 0:
+        swap_1 = [send(join([activations, up, down]), CORE_SWAP)]
+    else:
+        swap_1 = []
+    x2, z2 = tie((x2, z2))
     x3, z3 = send(x2, X_RING), send(z2, Z_RING)
+    if HOLD:
+        x2, z2, far, other, other_up, swap_1 = tie((x2, z2, far, other, other_up, swap_1))
+    else:
+        far, other, other_up, swap_1 = tie((far, other, other_up, swap_1))
+
     other_far, other_down = send(other_up, Y_RING), send(other, Y_BACK)
-    swap_2 = send(join([far, other, other_up]), CORE_SWAP)
-    mine = [(b, 0, 1) for b in (activations, up, down, far)]
-    left_own = sort_tokens(places, 0, mine + [(swap_1, 0, 3), (swap_2, 0, 1)])
+    if SWAP == 0:
+        swap_2 = [send(far, CORE_SWAP)]
+    elif SWAP == 1:
+        swap_2 = [send(join([activations, up, down, far]), CORE_SWAP)]
+    else:
+        swap_2 = [send(t, CORE_SWAP) for t in (activations, up, down, far)]
+    owns = len(swap_2)
+    swap_2.append(send(join([other, other_up]), CORE_SWAP))
+    mine = whole([activations, up, down, far])
+    left_own = sort_tokens(places, 0, mine + whole(swap_1 + swap_2[:owns]))
+    if HOLD > 1:
+        left_own, x3, z3 = tie((left_own, x3, z3))
     first = [out_grad, x1, x2, z2]
     sums = [multiply([left_own, None], 0, first, [[], []], g, None, None, full) for g in range(2)]
-    if EARLY == 0:
-        x3, z3, other_far, other_down, swap_2, left_own = tie((x3, z3, other_far, other_down, swap_2, left_own))
-    if EARLY == 1:
-        x3, z3, other_far, other_down, swap_2, sums[0] = tie((x3, z3, other_far, other_down, swap_2, sums[0]))
-    if EARLY == 2:
-        x3, z3, other_far, other_down, swap_2, sums = tie((x3, z3, other_far, other_down, swap_2, sums))
-
-    swap_3 = send(join([other_down, other_far]), CORE_SWAP)
-    others = [(b, 0, 1) for b in (other, other_up, other_down, other_far)]
-    left_other = sort_tokens(places, 1, others + [(swap_2, TOK, 2), (swap_3, 0, 2)])
+    other_far, other_down, swap_2 = tie((other_far, other_down, swap_2))
+
+    swap_3 = [send(join([other_down, other_far]), CORE_SWAP)]
+    others = whole([other, other_up, other_down, other_far])
+    left_other = sort_tokens(places, 1, others + whole(swap_2[owns:] + swap_3))
 
     a, b = [[], []], [[], []]
     for g in range(2):
         at = 2 * g * width
         a[g].append(send(join([x1, x2, x3], slice(at, at + width)), Z_RING))
         b[g].append(send(join([z1, z2, z3], slice(at + width, at + 2 * width)), X_RING))
-    if TIES >= 1:
+    if SPLIT:
+        a[0][0], b[0][0], sums[0] = tie((a[0][0], b[0][0], sums[0]))
+        a[1][0], b[1][0], left_other, sums[1] = tie((a[1][0], b[1][0], left_other, sums[1]))
+    else:
         a[0][0], b[0][0], sums[0], sums[1] = tie((a[0][0], b[0][0], sums[0], sums[1]))
-    if LEFT:
         a[1][0], b[1][0], left_other = tie((a[1][0], b[1][0], left_other))
     lefts = [left_own, left_other]
     for g in range(2):

time: 109 us -> 104 us (0.954)
  Pallas kernels: 38.7 us -> 32.8 us
  starting transfers between devices: 29.3 us -> 33 us
  waiting for transfers between devices: 36.2 us -> 33 us
  other arithmetic: 2.38 us -> 3.59 us
    pallas_call x6, Pallas kernels: 32.8 us -> 28.6 us  [multiply(): pl.pallas_call(kernel, grid=(rows // step,), in_specs=in_specs, out_specs...]
    ppermute x28 -> x29, starting transfers between devices: 29.3 us -> 33 us  [send(): return lax.ppermute(block, AXES, pairs)]
    ppermute x28 -> x29, waiting for transfers between devices: 36.2 us -> 33 us  [send(): return lax.ppermute(block, AXES, pairs)]
    pallas_call x2, Pallas kernels: 5.95 us -> 4.18 us  [sort_tokens(): pl.pallas_call(kernel, grid_spec=pltpu.PrefetchScalarGridSpec(num_scalar_...]
    concatenate x7, other arithmetic: 2.38 us -> 3.59 us  [join(): return jnp.concatenate([b[:, cols] for b in blocks], axis=0)]
  transfers between devices with their start and end apart: 28 -> 29, of which waited for: 14 -> 16; matrix products, arithmetic and copies ran while one was open for 1% -> 2% of each run, Pallas kernels for 30% -> 26%
where the time goes in v3:
time: 104 us; the launch traced here: 103 us
  starting transfers between devices  33 us (32%)
  waiting for transfers between devices  33 us (32%)
  Pallas kernels  32.8 us (32%)
  other arithmetic  3.59 us (3%)
    ppermute x29, starting transfers between devices, send(): return lax.ppermute(block, AXES, pairs)  33 us
    ppermute x29, waiting for transfers between devices, send(): return lax.ppermute(block, AXES, pairs)  33 us
    pallas_call x6, Pallas kernels, multiply(): pl.pallas_call(kernel, grid=(rows // step,), in_specs=in_specs, out_specs...  28.6 us
    pallas_call x2, Pallas kernels, sort_tokens(): pl.pallas_call(kernel, grid_spec=pltpu.PrefetchScalarGridSpec(num_scalar_...  4.18 us
    concatenate x7, other arithmetic, join(): return jnp.concatenate([b[:, cols] for b in blocks], axis=0)  3.59 us
  transfers between devices with their start and end apart: 29, of which 16 were waited for; matrix products, arithmetic and copies ran while one was open for 2% of the time, Pallas kernels for 26%

profile of v3, /device:TPU:0, one launch (start us, length us, event | category | flops | bytes accessed | tf_op | source)
XLA Modules:
  0.0 103.5 jit_solution(2100349883823618231)
XLA Ops:
  0.0 2.0 %collective-permute-start.1 = (bf16[128,3072]{1,0:T(8,128)(2,1)}, bf16[128,3072]{1,0:T(8,128)(2,1)S(1)}, u32[]{:S(2)}, u32[]{:S(2)}) collective-permute-start(bf16[128,3072]{1,0:T(8,128)(2,1)} %refs_1_.3), channel_id=1, source_target_pairs={{0,1},{2,67},{1,64},{3,2},{64,65},{66,3},{65,0},{67,66},{4,5},{6,7... | collective-permute-start | bytes 2359304 | tf_op jit(solution)/shard_map/ppermute | solution.py:182
  3.5 3.0 %collective-permute-start.4 = (bf16[128,1536]{1,0:T(8,128)(2,1)}, bf16[128,1536]{1,0:T(8,128)(2,1)S(1)}, u32[]{:S(2)}, u32[]{:S(2)}) collective-permute-start(bf16[128,1536]{1,0:T(8,128)(2,1)} %refs_0_.1), channel_id=1, source_target_pairs={{0,12},{2,6},{1,13},{3,7},{64,76},{66,70},{65,77},{67,71},{4,0},{6... | collective-permute-start | bytes 1179656 | tf_op jit(solution)/shard_map/ppermute | solution.py:182
  6.5 1.9 %collective-permute-start.2 = (bf16[128,1536]{1,0:T(8,128)(2,1)}, bf16[128,1536]{1,0:T(8,128)(2,1)}, u32[]{:S(2)}, u32[]{:S(2)}) collective-permute-start(bf16[128,1536]{1,0:T(8,128)(2,1)} %refs_0_.1), channel_id=1, source_target_pairs={{0,1},{2,3},{1,0},{3,2},{64,65},{66,67},{65,64},{67,66},{4,5},{6,7... | collective-permute-start | bytes 1179656 | tf_op jit(solution)/shard_map/ppermute | solution.py:182
  8.4 6.1 %collective-permute-done.4.refs_2_ = bf16[128,1536]{1,0:T(8,128)(2,1)S(1)} collective-permute-done((bf16[128,1536]{1,0:T(8,128)(2,1)}, bf16[128,1536]{1,0:T(8,128)(2,1)S(1)}, u32[]{:S(2)}, u32[]{:S(2)}) %collective-permute-start.4) | collective-permute-done | bytes 393248 | tf_op jit(solution)/shard_map/ppermute | solution.py:182
  14.6 4.2 %collective-permute-done.3.refs_1_ = bf16[128,1536]{1,0:T(8,128)(2,1)} collective-permute-done((bf16[128,1536]{1,0:T(8,128)(2,1)}, bf16[128,1536]{1,0:T(8,128)(2,1)}, u32[]{:S(2)}, u32[]{:S(2)}) %collective-permute-start.3) | collective-permute-done | bytes 393248 | tf_op jit(solution)/shard_map/ppermute | solution.py:182
  20.3 2.2 %pad_maximum_fusion = bf16[384,1536]{1,0:T(8,128)(2,1)} fusion(bf16[128,1536]{1,0:T(8,128)(2,1)S(1)} %collective-permute-done.4.refs_2_, bf16[128,1536]{1,0:T(8,128)(2,1)} %collective-permute-done.3.refs_1_, bf16[128,1536]{1,0:T(8,128)(2,1)} %refs_0_.1), kind=kLoop, calls=%fused_computation | loop fusion | flops 3538944 | bytes 2359296 | tf_op jit(solution)/shard_map/concatenate | solution.py:186
  24.0 2.5 %collective-permute-start.6 = (bf16[128,3072]{1,0:T(8,128)(2,1)S(1)}, bf16[128,3072]{1,0:T(8,128)(2,1)S(1)}, u32[]{:S(2)}, u32[]{:S(2)}) collective-permute-start(bf16[128,3072]{1,0:T(8,128)(2,1)S(1)} %collective-permute-done.1.refs_3_), channel_id=1, source_target_pairs={{0,1},{2,67},{1,64},{3,2},{64,65},{66,3},{65,0},{67,66},{4,5},{6,7... | collective-permute-start | bytes 2359304 | tf_op jit(solution)/shard_map/ppermute | solution.py:182
  29.6 6.1 %collective-permute-done.5.refs_3_ = bf16[128,3072]{1,0:T(8,128)(2,1)S(1)} collective-permute-done((bf16[128,3072]{1,0:T(8,128)(2,1)S(1)}, bf16[128,3072]{1,0:T(8,128)(2,1)S(1)}, u32[]{:S(2)}, u32[]{:S(2)}) %collective-permute-start.5) | collective-permute-done | bytes 786464 | tf_op jit(solution)/shard_map/ppermute | solution.py:182
  35.7 2.9 %collective-permute-done.6.refs_4_ = bf16[128,3072]{1,0:T(8,128)(2,1)S(1)} collective-permute-done((bf16[128,3072]{1,0:T(8,128)(2,1)S(1)}, bf16[128,3072]{1,0:T(8,128)(2,1)S(1)}, u32[]{:S(2)}, u32[]{:S(2)}) %collective-permute-start.6) | collective-permute-done | bytes 786464 | tf_op jit(solution)/shard_map/ppermute | solution.py:182
  40.7 2.8 %collective-permute-start.10 = (bf16[128,1536]{1,0:T(8,128)(2,1)}, bf16[128,1536]{1,0:T(8,128)(2,1)S(1)}, u32[]{:S(2)}, u32[]{:S(2)}) collective-permute-start(bf16[128,1536]{1,0:T(8,128)(2,1)} %collective-permute-done.7.refs_3_), channel_id=1, source_target_pairs={{0,2},{2,0},{1,3},{3,1},{64,66},{66,64},{65,67},{67,65},{4,6},{6,4... | collective-permute-start | bytes 1179656 | tf_op jit(solution)/shard_map/ppermute | solution.py:182
  44.9 2.7 %collective-permute-start.16 = (bf16[128,1536]{1,0:T(8,128)(2,1)}, bf16[128,1536]{1,0:T(8,128)(2,1)S(1)}, u32[]{:S(2)}, u32[]{:S(2)}) collective-permute-start(bf16[128,1536]{1,0:T(8,128)(2,1)} %collective-permute-done.2.refs_0_), channel_id=1, source_target_pairs={{0,12},{2,6},{1,13},{3,7},{64,76},{66,70},{65,77},{67,71},{4,0},{6... | collective-permute-start | bytes 1179656 | tf_op jit(solution)/shard_map/ppermute | solution.py:182
  47.7 2.4 %shard_map.37.refs_0_ = bf16[1024,1536]{1,0:T(8,128)(2,1)S(1)} custom-call(s32[2,8]{1,0:T(2,128)S(1)} %dynamic-slice_bitcast_fusion.places_ref, bf16[128,1536]{1,0:T(8,128)(2,1)S(1)} %copy-done.1, bf16[128,1536]{1,0:T(8,128)(2,1)} %collective-permute-done.3.refs_1_, bf16[128,1536]{1,0:T(8,128)(2,1)S(1)} %collective-permute-done.4.refs_2_, ...), custom_call_target="tpu_custom_call" | custom-call | bytes 6291456 | tf_op jit(solution)/shard_map/pallas_call | solution.py:97
  50.1 1.6 %collective-permute-done.11.refs_2_ = bf16[128,3072]{1,0:T(8,128)(2,1)S(1)} collective-permute-done((bf16[128,3072]{1,0:T(8,128)(2,1)S(1)}, bf16[128,3072]{1,0:T(8,128)(2,1)S(1)}, u32[]{:S(2)}, u32[]{:S(2)}) %collective-permute-start.11) | collective-permute-done | bytes 786464 | tf_op jit(solution)/shard_map/ppermute | solution.py:182
  54.7 2.7 %collective-permute-done.16.refs_2_ = bf16[128,1536]{1,0:T(8,128)(2,1)S(1)} collective-permute-done((bf16[128,1536]{1,0:T(8,128)(2,1)}, bf16[128,1536]{1,0:T(8,128)(2,1)S(1)}, u32[]{:S(2)}, u32[]{:S(2)}) %collective-permute-start.16) | collective-permute-done | bytes 393248 | tf_op jit(solution)/shard_map/ppermute | solution.py:182
  59.2 3.3 %shard_map.41.refs_7_ = f32[1536,1536]{1,0:T(8,128)S(1)} custom-call(bf16[1024,1536]{1,0:T(8,128)(2,1)S(1)} %shard_map.37.refs_0_, bf16[128,3072]{1,0:T(8,128)(2,1)S(1)} %copy-done, bf16[128,3072]{1,0:T(8,128)(2,1)S(1)} %collective-permute-done.refs_2_, bf16[128,3072]{1,0:T(8,128)(2,1)S(1)} %collective-permute-done.5.refs_3_, ...), custom_call_target="tpu_custom_call" | custom-call | flops 2415919104 | bytes 22020096 | tf_op jit(solution)/shard_map/pallas_call | solution.py:165
  62.5 2.0 %collective-permute-done.23.refs_5_ = bf16[384,768]{1,0:T(8,128)(2,1)S(1)} collective-permute-done((bf16[384,768]{1,0:T(8,128)(2,1)S(1)}, bf16[384,768]{1,0:T(8,128)(2,1)S(1)}, u32[]{:S(2)}, u32[]{:S(2)}) %collective-permute-start.23) | collective-permute-done | bytes 589856 | tf_op jit(solution)/shard_map/ppermute | solution.py:182
  65.7 3.3 %shard_map.39.refs_7_ = f32[1536,1536]{1,0:T(8,128)S(1)} custom-call(bf16[1024,1536]{1,0:T(8,128)(2,1)S(1)} %shard_map.37.refs_0_, bf16[128,3072]{1,0:T(8,128)(2,1)S(1)} %copy-done, bf16[128,3072]{1,0:T(8,128)(2,1)S(1)} %collective-permute-done.refs_2_, bf16[128,3072]{1,0:T(8,128)(2,1)S(1)} %collective-permute-done.5.refs_3_, ...), custom_call_target="tpu_custom_call" | custom-call | flops 2415919104 | bytes 22020096 | tf_op jit(solution)/shard_map/pallas_call | solution.py:165
  69.0 1.8 %shard_map.38.refs_1_ = bf16[1024,1536]{1,0:T(8,128)(2,1)S(1)} custom-call(s32[2,8]{1,0:T(2,128)S(1)} %dynamic-slice_bitcast_fusion.places_ref, bf16[128,1536]{1,0:T(8,128)(2,1)} %collective-permute-done.2.refs_0_, bf16[128,1536]{1,0:T(8,128)(2,1)} %collective-permute-done.8.refs_1_, bf16[128,1536]{1,0:T(8,128)(2,1)S(1)} %collective-permute-done.16.refs_2_, ...), custom_call_target="tpu_custom_call" | custom-call | bytes 6291456 | tf_op jit(solution)/shard_map/pallas_call | solution.py:97
  72.5 5.2 %shard_map.42.refs_6_ = f32[1536,1536]{1,0:T(8,128)S(1)} custom-call(bf16[1024,1536]{1,0:T(8,128)(2,1)S(1)} %shard_map.37.refs_0_, bf16[1024,1536]{1,0:T(8,128)(2,1)S(1)} %shard_map.38.refs_1_, bf16[128,3072]{1,0:T(8,128)(2,1)S(1)} %collective-permute-done.11.refs_2_, ...), custom_call_target="tpu_custom_call", output_to_operand_aliasing={{}: (7, {})} | custom-call | flops 3623878656 | bytes 22806528 | tf_op jit(solution)/shard_map/pallas_call | solution.py:165
  77.8 2.5 %collective-permute-start.27 = (bf16[384,768]{1,0:T(8,128)(2,1)S(1)}, bf16[384,768]{1,0:T(8,128)(2,1)S(1)}, u32[]{:S(2)}, u32[]{:S(2)}) collective-permute-start(bf16[384,768]{1,0:T(8,128)(2,1)S(1)} %collective-permute-done.25.refs_2_), channel_id=1, source_target_pairs={{0,1},{2,67},{1,64},{3,2},{64,65},{66,3},{65,0},{67,66},{4,5},{6,7... | collective-permute-start | bytes 1769480 | tf_op jit(solution)/shard_map/ppermute | solution.py:182
  81.8 1.7 %collective-permute-done.19.refs_2_ = bf16[384,768]{1,0:T(8,128)(2,1)S(1)} collective-permute-done((bf16[384,768]{1,0:T(8,128)(2,1)S(1)}, bf16[384,768]{1,0:T(8,128)(2,1)S(1)}, u32[]{:S(2)}, u32[]{:S(2)}) %collective-permute-start.19) | collective-permute-done | bytes 589856 | tf_op jit(solution)/shard_map/ppermute | solution.py:182
  84.7 5.2 %shard_map.40.refs_6_ = f32[1536,1536]{1,0:T(8,128)S(1)} custom-call(bf16[1024,1536]{1,0:T(8,128)(2,1)S(1)} %shard_map.37.refs_0_, bf16[1024,1536]{1,0:T(8,128)(2,1)S(1)} %shard_map.38.refs_1_, bf16[128,3072]{1,0:T(8,128)(2,1)S(1)} %collective-permute-done.11.refs_2_, ...), custom_call_target="tpu_custom_call", output_to_operand_aliasing={{}: (7, {})} | custom-call | flops 3623878656 | bytes 22806528 | tf_op jit(solution)/shard_map/pallas_call | solution.py:165
  91.4 5.8 %shard_map.43.refs_7_ = bf16[1536,3072]{1,0:T(8,128)(2,1)} custom-call(bf16[1024,1536]{1,0:T(8,128)(2,1)S(1)} %shard_map.37.refs_0_, bf16[1024,1536]{1,0:T(8,128)(2,1)S(1)} %shard_map.38.refs_1_, bf16[384,768]{1,0:T(8,128)(2,1)S(1)} %collective-permute-done.25.refs_2_, bf16[384,768]{1,0:T(8,128)(2,1)S(1)} %collective-permute-done.27.refs_3_, ...), custom_call_target="tpu_custom_call" | custom-call | flops 3623878656 | bytes 22806528 | tf_op jit(solution)/shard_map/pallas_call | solution.py:165
  97.7 5.8 %shard_map.44 = bf16[1536,3072]{1,0:T(8,128)(2,1)} custom-call(bf16[1024,1536]{1,0:T(8,128)(2,1)S(1)} %shard_map.37.refs_0_, bf16[1024,1536]{1,0:T(8,128)(2,1)S(1)} %shard_map.38.refs_1_, bf16[384,768]{1,0:T(8,128)(2,1)S(1)} %collective-permute-done.19.refs_2_, bf16[384,768]{1,0:T(8,128)(2,1)S(1)} %collective-permute-done.20.refs_3_, ...), custom_call_target="tpu_custom_call", output_to_operand_aliasing={{}: (7, {})} | custom-call | flops 3623878656 | bytes 22806528 | tf_op jit(solution)/shard_map/pallas_call | solution.py:165
  (57 shorter events, 23.6 us)
Async XLA Ops:
  0.0 20.3 %collective-permute-start.1 = (bf16[128,3072]{1,0:T(8,128)(2,1)}, bf16[128,3072]{1,0:T(8,128)(2,1)S(1)}, u32[]{:S(2)}, u32[]{:S(2)}) collective-permute-start(bf16[128,3072]{1,0:T(8,128)(2,1)} %refs_1_.3), channel_id=1, source_target_pairs={{0,1},{2,67},{1,64},{3,2},{64,65},{66,3},{65,0},{67,66},{4,5},{6,7... | collective-permute-start | bytes 2359304 | tf_op jit(solution)/shard_map/ppermute | solution.py:182
  2.0 18.3 %collective-permute-start = (bf16[128,3072]{1,0:T(8,128)(2,1)}, bf16[128,3072]{1,0:T(8,128)(2,1)S(1)}, u32[]{:S(2)}, u32[]{:S(2)}) collective-permute-start(bf16[128,3072]{1,0:T(8,128)(2,1)} %refs_1_.3), channel_id=1, source_target_pairs={{0,16},{2,50},{1,17},{3,51},{64,80},{66,114},{65,81},{67,115},{4,2... | collective-permute-start | bytes 2359304 | tf_op jit(solution)/shard_map/ppermute | solution.py:182
  6.5 12.3 %collective-permute-start.3 = (bf16[128,1536]{1,0:T(8,128)(2,1)}, bf16[128,1536]{1,0:T(8,128)(2,1)}, u32[]{:S(2)}, u32[]{:S(2)}) collective-permute-start(bf16[128,1536]{1,0:T(8,128)(2,1)} %refs_0_.1), channel_id=1, source_target_pairs={{0,4},{2,14},{1,5},{3,15},{64,68},{66,78},{65,69},{67,79},{4,8},{6... | collective-permute-start | bytes 1179656 | tf_op jit(solution)/shard_map/ppermute | solution.py:182
  6.5 13.7 %collective-permute-start.2 = (bf16[128,1536]{1,0:T(8,128)(2,1)}, bf16[128,1536]{1,0:T(8,128)(2,1)}, u32[]{:S(2)}, u32[]{:S(2)}) collective-permute-start(bf16[128,1536]{1,0:T(8,128)(2,1)} %refs_0_.1), channel_id=1, source_target_pairs={{0,1},{2,3},{1,0},{3,2},{64,65},{66,67},{65,64},{67,66},{4,5},{6,7... | collective-permute-start | bytes 1179656 | tf_op jit(solution)/shard_map/ppermute | solution.py:182
  22.5 18.2 %collective-permute-start.9 = (bf16[384,1536]{1,0:T(8,128)(2,1)}, bf16[384,1536]{1,0:T(8,128)(2,1)}, u32[]{:S(2)}, u32[]{:S(2)}) collective-permute-start(bf16[384,1536]{1,0:T(8,128)(2,1)} %pad_maximum_fusion), channel_id=1, source_target_pairs={{0,2},{2,0},{1,3},{3,1},{64,66},{66,64},{65,67},{67,65},{4,6},{6,4... | collective-permute-start | bytes 3538952 | tf_op jit(solution)/shard_map/ppermute | solution.py:182
  22.5 13.2 %collective-permute-start.5 = (bf16[128,3072]{1,0:T(8,128)(2,1)S(1)}, bf16[128,3072]{1,0:T(8,128)(2,1)S(1)}, u32[]{:S(2)}, u32[]{:S(2)}) collective-permute-start(bf16[128,3072]{1,0:T(8,128)(2,1)S(1)} %collective-permute-done.refs_2_), channel_id=1, source_target_pairs={{0,16},{2,50},{1,17},{3,51},{64,80},{66,114},{65,81},{67,115},{4,2... | collective-permute-start | bytes 2359304 | tf_op jit(solution)/shard_map/ppermute | solution.py:182
  24.0 14.6 %collective-permute-start.6 = (bf16[128,3072]{1,0:T(8,128)(2,1)S(1)}, bf16[128,3072]{1,0:T(8,128)(2,1)S(1)}, u32[]{:S(2)}, u32[]{:S(2)}) collective-permute-start(bf16[128,3072]{1,0:T(8,128)(2,1)S(1)} %collective-permute-done.1.refs_3_), channel_id=1, source_target_pairs={{0,1},{2,67},{1,64},{3,2},{64,65},{66,3},{65,0},{67,66},{4,5},{6,7... | collective-permute-start | bytes 2359304 | tf_op jit(solution)/shard_map/ppermute | solution.py:182
  26.4 14.3 %collective-permute-start.8 = (bf16[128,1536]{1,0:T(8,128)(2,1)}, bf16[128,1536]{1,0:T(8,128)(2,1)}, u32[]{:S(2)}, u32[]{:S(2)}) collective-permute-start(bf16[128,1536]{1,0:T(8,128)(2,1)} %collective-permute-done.2.refs_0_), channel_id=1, source_target_pairs={{0,4},{2,14},{1,5},{3,15},{64,68},{66,78},{65,69},{67,79},{4,8},{6... | collective-permute-start | bytes 1179656 | tf_op jit(solution)/shard_map/ppermute | solution.py:182
  28.0 12.7 %collective-permute-start.7 = (bf16[128,1536]{1,0:T(8,128)(2,1)}, bf16[128,1536]{1,0:T(8,128)(2,1)}, u32[]{:S(2)}, u32[]{:S(2)}) collective-permute-start(bf16[128,1536]{1,0:T(8,128)(2,1)} %collective-permute-done.3.refs_1_), channel_id=1, source_target_pairs={{0,4},{2,14},{1,5},{3,15},{64,68},{66,78},{65,69},{67,79},{4,8},{6... | collective-permute-start | bytes 1179656 | tf_op jit(solution)/shard_map/ppermute | solution.py:182
  38.5 13.2 %collective-permute-start.11 = (bf16[128,3072]{1,0:T(8,128)(2,1)S(1)}, bf16[128,3072]{1,0:T(8,128)(2,1)S(1)}, u32[]{:S(2)}, u32[]{:S(2)}) collective-permute-start(bf16[128,3072]{1,0:T(8,128)(2,1)S(1)} %collective-permute-done.5.refs_3_), channel_id=1, source_target_pairs={{0,16},{2,50},{1,17},{3,51},{64,80},{66,114},{65,81},{67,115},{4,2... | collective-permute-start | bytes 2359304 | tf_op jit(solution)/shard_map/ppermute | solution.py:182
  40.0 13.2 %collective-permute-start.12 = (bf16[128,3072]{1,0:T(8,128)(2,1)S(1)}, bf16[128,3072]{1,0:T(8,128)(2,1)S(1)}, u32[]{:S(2)}, u32[]{:S(2)}) collective-permute-start(bf16[128,3072]{1,0:T(8,128)(2,1)S(1)} %collective-permute-done.6.refs_4_), channel_id=1, source_target_pairs={{0,1},{2,67},{1,64},{3,2},{64,65},{66,3},{65,0},{67,66},{4,5},{6,7... | collective-permute-start | bytes 2359304 | tf_op jit(solution)/shard_map/ppermute | solution.py:182
  44.7 13.2 %collective-permute-start.17 = (bf16[256,1536]{1,0:T(8,128)(2,1)S(1)}, bf16[256,1536]{1,0:T(8,128)(2,1)S(1)}, u32[]{:S(2)}, u32[]{:S(2)}) collective-permute-start(bf16[256,1536]{1,0:T(8,128)(2,1)S(1)} %pad_maximum_fusion.1), channel_id=1, source_target_pairs={{0,2},{2,0},{1,3},{3,1},{64,66},{66,64},{65,67},{67,65},{4,6},{6,4... | collective-permute-start | bytes 2359304 | tf_op jit(solution)/shard_map/ppermute | solution.py:182
  44.9 12.5 %collective-permute-start.16 = (bf16[128,1536]{1,0:T(8,128)(2,1)}, bf16[128,1536]{1,0:T(8,128)(2,1)S(1)}, u32[]{:S(2)}, u32[]{:S(2)}) collective-permute-start(bf16[128,1536]{1,0:T(8,128)(2,1)} %collective-permute-done.2.refs_0_), channel_id=1, source_target_pairs={{0,12},{2,6},{1,13},{3,7},{64,76},{66,70},{65,77},{67,71},{4,0},{6... | collective-permute-start | bytes 1179656 | tf_op jit(solution)/shard_map/ppermute | solution.py:182
  53.3 11.2 %collective-permute-start.23 = (bf16[384,768]{1,0:T(8,128)(2,1)S(1)}, bf16[384,768]{1,0:T(8,128)(2,1)S(1)}, u32[]{:S(2)}, u32[]{:S(2)}) collective-permute-start(bf16[384,768]{1,0:T(8,128)(2,1)S(1)} %pad_maximum_fusion.5), channel_id=1, source_target_pairs={{0,1},{2,67},{1,64},{3,2},{64,65},{66,3},{65,0},{67,66},{4,5},{6,7... | collective-permute-start | bytes 1769480 | tf_op jit(solution)/shard_map/ppermute | solution.py:182
  53.5 11.2 %collective-permute-start.24 = (bf16[384,768]{1,0:T(8,128)(2,1)S(1)}, bf16[384,768]{1,0:T(8,128)(2,1)S(1)}, u32[]{:S(2)}, u32[]{:S(2)}) collective-permute-start(bf16[384,768]{1,0:T(8,128)(2,1)S(1)} %pad_maximum_fusion.6), channel_id=1, source_target_pairs={{0,16},{2,50},{1,17},{3,51},{64,80},{66,114},{65,81},{67,115},{4,2... | collective-permute-start | bytes 1769480 | tf_op jit(solution)/shard_map/ppermute | solution.py:182
  58.1 12.7 %collective-permute-start.13 = (bf16[384,768]{1,0:T(8,128)(2,1)S(1)}, bf16[384,768]{1,0:T(8,128)(2,1)S(1)}, u32[]{:S(2)}, u32[]{:S(2)}) collective-permute-start(bf16[384,768]{1,0:T(8,128)(2,1)S(1)} %pad_maximum_fusion.3), channel_id=1, source_target_pairs={{0,1},{2,67},{1,64},{3,2},{64,65},{66,3},{65,0},{67,66},{4,5},{6,7... | collective-permute-start | bytes 1769480 | tf_op jit(solution)/shard_map/ppermute | solution.py:182
  58.2 12.7 %collective-permute-start.14 = (bf16[384,768]{1,0:T(8,128)(2,1)S(1)}, bf16[384,768]{1,0:T(8,128)(2,1)S(1)}, u32[]{:S(2)}, u32[]{:S(2)}) collective-permute-start(bf16[384,768]{1,0:T(8,128)(2,1)S(1)} %pad_maximum_fusion.4), channel_id=1, source_target_pairs={{0,16},{2,50},{1,17},{3,51},{64,80},{66,114},{65,81},{67,115},{4,2... | collective-permute-start | bytes 1769480 | tf_op jit(solution)/shard_map/ppermute | solution.py:182
  64.6 13.2 %collective-permute-start.25 = (bf16[384,768]{1,0:T(8,128)(2,1)S(1)}, bf16[384,768]{1,0:T(8,128)(2,1)S(1)}, u32[]{:S(2)}, u32[]{:S(2)}) collective-permute-start(bf16[384,768]{1,0:T(8,128)(2,1)S(1)} %collective-permute-done.23.refs_5_), channel_id=1, source_target_pairs={{0,1},{2,67},{1,64},{3,2},{64,65},{66,3},{65,0},{67,66},{4,5},{6,7... | collective-permute-start | bytes 1769480 | tf_op jit(solution)/shard_map/ppermute | solution.py:182
  64.6 13.2 %collective-permute-start.26 = (bf16[384,768]{1,0:T(8,128)(2,1)S(1)}, bf16[384,768]{1,0:T(8,128)(2,1)S(1)}, u32[]{:S(2)}, u32[]{:S(2)}) collective-permute-start(bf16[384,768]{1,0:T(8,128)(2,1)S(1)} %collective-permute-done.24.refs_6_), channel_id=1, source_target_pairs={{0,16},{2,50},{1,17},{3,51},{64,80},{66,114},{65,81},{67,115},{4,2... | collective-permute-start | bytes 1769480 | tf_op jit(solution)/shard_map/ppermute | solution.py:182
  70.9 12.5 %collective-permute-start.19 = (bf16[384,768]{1,0:T(8,128)(2,1)S(1)}, bf16[384,768]{1,0:T(8,128)(2,1)S(1)}, u32[]{:S(2)}, u32[]{:S(2)}) collective-permute-start(bf16[384,768]{1,0:T(8,128)(2,1)S(1)} %collective-permute-done.13.refs_5_), channel_id=1, source_target_pairs={{0,1},{2,67},{1,64},{3,2},{64,65},{66,3},{65,0},{67,66},{4,5},{6,7... | collective-permute-start | bytes 1769480 | tf_op jit(solution)/shard_map/ppermute | solution.py:182
  72.1 11.5 %collective-permute-start.21 = (bf16[384,768]{1,0:T(8,128)(2,1)S(1)}, bf16[384,768]{1,0:T(8,128)(2,1)S(1)}, u32[]{:S(2)}, u32[]{:S(2)}) collective-permute-start(bf16[384,768]{1,0:T(8,128)(2,1)S(1)} %collective-permute-done.14.refs_6_), channel_id=1, source_target_pairs={{0,16},{2,50},{1,17},{3,51},{64,80},{66,114},{65,81},{67,115},{4,2... | collective-permute-start | bytes 1769480 | tf_op jit(solution)/shard_map/ppermute | solution.py:182
  77.8 12.2 %collective-permute-start.27 = (bf16[384,768]{1,0:T(8,128)(2,1)S(1)}, bf16[384,768]{1,0:T(8,128)(2,1)S(1)}, u32[]{:S(2)}, u32[]{:S(2)}) collective-permute-start(bf16[384,768]{1,0:T(8,128)(2,1)S(1)} %collective-permute-done.25.refs_2_), channel_id=1, source_target_pairs={{0,1},{2,67},{1,64},{3,2},{64,65},{66,3},{65,0},{67,66},{4,5},{6,7... | collective-permute-start | bytes 1769480 | tf_op jit(solution)/shard_map/ppermute | solution.py:182
  83.4 13.7 %collective-permute-start.20 = (bf16[384,768]{1,0:T(8,128)(2,1)S(1)}, bf16[384,768]{1,0:T(8,128)(2,1)S(1)}, u32[]{:S(2)}, u32[]{:S(2)}) collective-permute-start(bf16[384,768]{1,0:T(8,128)(2,1)S(1)} %collective-permute-done.19.refs_2_), channel_id=1, source_target_pairs={{0,1},{2,67},{1,64},{3,2},{64,65},{66,3},{65,0},{67,66},{4,5},{6,7... | collective-permute-start | bytes 1769480 | tf_op jit(solution)/shard_map/ppermute | solution.py:182
  83.6 14.1 %collective-permute-start.22 = (bf16[384,768]{1,0:T(8,128)(2,1)S(1)}, bf16[384,768]{1,0:T(8,128)(2,1)S(1)}, u32[]{:S(2)}, u32[]{:S(2)}) collective-permute-start(bf16[384,768]{1,0:T(8,128)(2,1)S(1)} %collective-permute-done.21.refs_4_), channel_id=1, source_target_pairs={{0,16},{2,50},{1,17},{3,51},{64,80},{66,114},{65,81},{67,115},{4,2... | collective-permute-start | bytes 1769480 | tf_op jit(solution)/shard_map/ppermute | solution.py:182
  (7 other events, 54.6 us)

commit v4 on v3

--- a/solution.py
+++ b/solution.py
@@ -8,11 +8,7 @@
 
 AXES = ("row", "col", "rep")
 TOK = 128
-LIMIT = 16
-TIES = 2
-HOLD = 2
-SPLIT = 1
-SWAP = 0
+LIMIT = 19
 STEP = 512
 F32 = jnp.float32
 BF16 = jnp.bfloat16
@@ -118,7 +114,7 @@
     order = PASSES[number]
     depth = TOK * len(order[0])
     n_own = len(own[0])
-    skip = (0 if number == 0 else 4, 0)
+    skip = (4 if number in (1, 2) else 0, 0)
 
     def kernel(*refs):
         left_refs, refs = refs[: len(used)], refs[len(used) :]
@@ -205,55 +201,36 @@
     x2, z2 = send(x1, X_RING), send(z1, Z_RING)
     far = send(up, Y_RING)
     other_up = send(other, Y_RING)
-    if SWAP == 0:
-        swap_1 = [send(join([activations, up, down]), CORE_SWAP)]
-    else:
-        swap_1 = []
-    x2, z2 = tie((x2, z2))
+    swap_1 = send(join([activations, up, down]), CORE_SWAP)
     x3, z3 = send(x2, X_RING), send(z2, Z_RING)
-    if HOLD:
-        x2, z2, far, other, other_up, swap_1 = tie((x2, z2, far, other, other_up, swap_1))
-    else:
-        far, other, other_up, swap_1 = tie((far, other, other_up, swap_1))
+    x2, z2, far, other, other_up, swap_1 = tie((x2, z2, far, other, other_up, swap_1))
 
     other_far, other_down = send(other_up, Y_RING), send(other, Y_BACK)
-    if SWAP == 0:
-        swap_2 = [send(far, CORE_SWAP)]
-    elif SWAP == 1:
-        swap_2 = [send(join([activations, up, down, far]), CORE_SWAP)]
-    else:
-        swap_2 = [send(t, CORE_SWAP) for t in (activations, up, down, far)]
-    owns = len(swap_2)
-    swap_2.append(send(join([other, other_up]), CORE_SWAP))
+    swap_2 = [send(far, CORE_SWAP), send(join([other, other_up]), CORE_SWAP)]
     mine = whole([activations, up, down, far])
-    left_own = sort_tokens(places, 0, mine + whole(swap_1 + swap_2[:owns]))
-    if HOLD > 1:
-        left_own, x3, z3 = tie((left_own, x3, z3))
+    left_own = sort_tokens(places, 0, mine + whole([swap_1, swap_2[0]]))
+    left_own, x3, z3 = tie((left_own, x3, z3))
     first = [out_grad, x1, x2, z2]
     sums = [multiply([left_own, None], 0, first, [[], []], g, None, None, full) for g in range(2)]
     other_far, other_down, swap_2 = tie((other_far, other_down, swap_2))
 
     swap_3 = [send(join([other_down, other_far]), CORE_SWAP)]
     others = whole([other, other_up, other_down, other_far])
-    left_other = sort_tokens(places, 1, others + whole(swap_2[owns:] + swap_3))
+    left_other = sort_tokens(places, 1, others + whole([swap_2[1]] + swap_3))
 
     a, b = [[], []], [[], []]
     for g in range(2):
         at = 2 * g * width
         a[g].append(send(join([x1, x2, x3], slice(at, at + width)), Z_RING))
         b[g].append(send(join([z1, z2, z3], slice(at + width, at + 2 * width)), X_RING))
-    if SPLIT:
-        a[0][0], b[0][0], sums[0] = tie((a[0][0], b[0][0], sums[0]))
-        a[1][0], b[1][0], left_other, sums[1] = tie((a[1][0], b[1][0], left_other, sums[1]))
-    else:
-        a[0][0], b[0][0], sums[0], sums[1] = tie((a[0][0], b[0][0], sums[0], sums[1]))
-        a[1][0], b[1][0], left_other = tie((a[1][0], b[1][0], left_other))
+    a[0][0], b[0][0], sums[0] = tie((a[0][0], b[0][0], sums[0]))
+    a[1][0], b[1][0], left_other, sums[1] = tie((a[1][0], b[1][0], left_other, sums[1]))
     lefts = [left_own, left_other]
     for g in range(2):
         sums[g] = multiply(lefts, 1, [x3, z1, z3], (a[g][:1], b[g][:1]), g, sums[g], None, full)
     for step in range(2):
         for g in range(2):
-            if step == 1 and TIES >= 2 + g:
+            if step == 1 and g == 0:
                 a[g][1], b[g][1], sums[g] = tie((a[g][1], b[g][1], sums[g]))
             a[g].append(send(a[g][-1], Z_RING))
             b[g].append(send(b[g][-1], X_RING))

time: 104 us -> 103 us (level)
  starting transfers between devices: 33 us -> 31.9 us
    ppermute x29, starting transfers between devices: 33 us -> 31.9 us  [send(): return lax.ppermute(block, AXES, pairs)]
  transfers between devices with their start and end apart: 29 -> 29, of which waited for: 16 -> 15; matrix products, arithmetic and copies ran while one was open for 2% -> 2% of each run, Pallas kernels for 26% -> 26%
where the time goes in v4:
time: 103 us
  Pallas kernels  32.8 us (32%)
  waiting for transfers between devices  32.7 us (32%)
  starting transfers between devices  31.9 us (31%)
  other arithmetic  3.58 us (3%)
  local copies, waits for them, and re-layouts  1.71 us (2%)
    ppermute x29, waiting for transfers between devices, send(): return lax.ppermute(block, AXES, pairs)  32.7 us
    ppermute x29, starting transfers between devices, send(): return lax.ppermute(block, AXES, pairs)  31.9 us
    pallas_call x6, Pallas kernels, multiply(): pl.pallas_call(kernel, grid=(rows // step,), in_specs=in_specs, out_specs...  28.6 us
    pallas_call x2, Pallas kernels, sort_tokens(): pl.pallas_call(kernel, grid_spec=pltpu.PrefetchScalarGridSpec(num_scalar_...  4.18 us
    concatenate x7, other arithmetic, join(): return jnp.concatenate([b[:, cols] for b in blocks], axis=0)  3.58 us
  transfers between devices with their start and end apart: 29, of which 15 were waited for; matrix products, arithmetic and copies ran while one was open for 2% of the time, Pallas kernels for 26%

profile of v4, /device:TPU:0, one launch (start us, length us, event | category | flops | bytes accessed | tf_op | source)
XLA Modules:
  0.0 103.0 jit_solution(5162621620526564545)
XLA Ops:
  0.0 2.0 %collective-permute-start.1 = (bf16[128,3072]{1,0:T(8,128)(2,1)}, bf16[128,3072]{1,0:T(8,128)(2,1)S(1)}, u32[]{:S(2)}, u32[]{:S(2)}) collective-permute-start(bf16[128,3072]{1,0:T(8,128)(2,1)} %refs_1_.3), channel_id=1, source_target_pairs={{0,1},{2,67},{1,64},{3,2},{64,65},{66,3},{65,0},{67,66},{4,5},{6,7... | collective-permute-start | bytes 2359304 | tf_op jit(solution)/shard_map/ppermute | solution.py:178
  3.5 3.0 %collective-permute-start.4 = (bf16[128,1536]{1,0:T(8,128)(2,1)}, bf16[128,1536]{1,0:T(8,128)(2,1)S(1)}, u32[]{:S(2)}, u32[]{:S(2)}) collective-permute-start(bf16[128,1536]{1,0:T(8,128)(2,1)} %refs_0_.1), channel_id=1, source_target_pairs={{0,12},{2,6},{1,13},{3,7},{64,76},{66,70},{65,77},{67,71},{4,0},{6... | collective-permute-start | bytes 1179656 | tf_op jit(solution)/shard_map/ppermute | solution.py:178
  6.5 1.9 %collective-permute-start.2 = (bf16[128,1536]{1,0:T(8,128)(2,1)}, bf16[128,1536]{1,0:T(8,128)(2,1)}, u32[]{:S(2)}, u32[]{:S(2)}) collective-permute-start(bf16[128,1536]{1,0:T(8,128)(2,1)} %refs_0_.1), channel_id=1, source_target_pairs={{0,1},{2,3},{1,0},{3,2},{64,65},{66,67},{65,64},{67,66},{4,5},{6,7... | collective-permute-start | bytes 1179656 | tf_op jit(solution)/shard_map/ppermute | solution.py:178
  8.4 6.1 %collective-permute-done.4.refs_2_ = bf16[128,1536]{1,0:T(8,128)(2,1)S(1)} collective-permute-done((bf16[128,1536]{1,0:T(8,128)(2,1)}, bf16[128,1536]{1,0:T(8,128)(2,1)S(1)}, u32[]{:S(2)}, u32[]{:S(2)}) %collective-permute-start.4) | collective-permute-done | bytes 393248 | tf_op jit(solution)/shard_map/ppermute | solution.py:178
  14.6 4.2 %collective-permute-done.3.refs_1_ = bf16[128,1536]{1,0:T(8,128)(2,1)} collective-permute-done((bf16[128,1536]{1,0:T(8,128)(2,1)}, bf16[128,1536]{1,0:T(8,128)(2,1)}, u32[]{:S(2)}, u32[]{:S(2)}) %collective-permute-start.3) | collective-permute-done | bytes 393248 | tf_op jit(solution)/shard_map/ppermute | solution.py:178
  20.3 2.2 %pad_maximum_fusion = bf16[384,1536]{1,0:T(8,128)(2,1)} fusion(bf16[128,1536]{1,0:T(8,128)(2,1)S(1)} %collective-permute-done.4.refs_2_, bf16[128,1536]{1,0:T(8,128)(2,1)} %collective-permute-done.3.refs_1_, bf16[128,1536]{1,0:T(8,128)(2,1)} %refs_0_.1), kind=kLoop, calls=%fused_computation | loop fusion | flops 3538944 | bytes 2359296 | tf_op jit(solution)/shard_map/concatenate | solution.py:182
  24.0 2.5 %collective-permute-start.6 = (bf16[128,3072]{1,0:T(8,128)(2,1)S(1)}, bf16[128,3072]{1,0:T(8,128)(2,1)S(1)}, u32[]{:S(2)}, u32[]{:S(2)}) collective-permute-start(bf16[128,3072]{1,0:T(8,128)(2,1)S(1)} %collective-permute-done.1.refs_3_), channel_id=1, source_target_pairs={{0,1},{2,67},{1,64},{3,2},{64,65},{66,3},{65,0},{67,66},{4,5},{6,7... | collective-permute-start | bytes 2359304 | tf_op jit(solution)/shard_map/ppermute | solution.py:178
  29.6 6.1 %collective-permute-done.5.refs_3_ = bf16[128,3072]{1,0:T(8,128)(2,1)S(1)} collective-permute-done((bf16[128,3072]{1,0:T(8,128)(2,1)S(1)}, bf16[128,3072]{1,0:T(8,128)(2,1)S(1)}, u32[]{:S(2)}, u32[]{:S(2)}) %collective-permute-start.5) | collective-permute-done | bytes 786464 | tf_op jit(solution)/shard_map/ppermute | solution.py:178
  36.0 2.6 %collective-permute-done.6.refs_4_ = bf16[128,3072]{1,0:T(8,128)(2,1)S(1)} collective-permute-done((bf16[128,3072]{1,0:T(8,128)(2,1)S(1)}, bf16[128,3072]{1,0:T(8,128)(2,1)S(1)}, u32[]{:S(2)}, u32[]{:S(2)}) %collective-permute-start.6) | collective-permute-done | bytes 786464 | tf_op jit(solution)/shard_map/ppermute | solution.py:178
  40.0 3.0 %collective-permute-start.10 = (bf16[128,1536]{1,0:T(8,128)(2,1)}, bf16[128,1536]{1,0:T(8,128)(2,1)S(1)}, u32[]{:S(2)}, u32[]{:S(2)}) collective-permute-start(bf16[128,1536]{1,0:T(8,128)(2,1)} %collective-permute-done.7.refs_3_), channel_id=1, source_target_pairs={{0,2},{2,0},{1,3},{3,1},{64,66},{66,64},{65,67},{67,65},{4,6},{6,4... | collective-permute-start | bytes 1179656 | tf_op jit(solution)/shard_map/ppermute | solution.py:178
  44.3 2.7 %collective-permute-start.16 = (bf16[128,1536]{1,0:T(8,128)(2,1)}, bf16[128,1536]{1,0:T(8,128)(2,1)S(1)}, u32[]{:S(2)}, u32[]{:S(2)}) collective-permute-start(bf16[128,1536]{1,0:T(8,128)(2,1)} %collective-permute-done.2.refs_0_), channel_id=1, source_target_pairs={{0,12},{2,6},{1,13},{3,7},{64,76},{66,70},{65,77},{67,71},{4,0},{6... | collective-permute-start | bytes 1179656 | tf_op jit(solution)/shard_map/ppermute | solution.py:178
  47.2 2.4 %shard_map.37.refs_0_ = bf16[1024,1536]{1,0:T(8,128)(2,1)S(1)} custom-call(s32[2,8]{1,0:T(2,128)S(1)} %dynamic-slice_bitcast_fusion.places_ref, bf16[128,1536]{1,0:T(8,128)(2,1)S(1)} %copy-done.1, bf16[128,1536]{1,0:T(8,128)(2,1)} %collective-permute-done.3.refs_1_, bf16[128,1536]{1,0:T(8,128)(2,1)S(1)} %collective-permute-done.4.refs_2_, ...), custom_call_target="tpu_custom_call" | custom-call | bytes 6291456 | tf_op jit(solution)/shard_map/pallas_call | solution.py:93
  49.6 2.1 %collective-permute-done.12.refs_4_ = bf16[128,3072]{1,0:T(8,128)(2,1)S(1)} collective-permute-done((bf16[128,3072]{1,0:T(8,128)(2,1)S(1)}, bf16[128,3072]{1,0:T(8,128)(2,1)S(1)}, u32[]{:S(2)}, u32[]{:S(2)}) %collective-permute-start.12) | collective-permute-done | bytes 786464 | tf_op jit(solution)/shard_map/ppermute | solution.py:178
  53.5 3.3 %collective-permute-done.16.refs_2_ = bf16[128,1536]{1,0:T(8,128)(2,1)S(1)} collective-permute-done((bf16[128,1536]{1,0:T(8,128)(2,1)}, bf16[128,1536]{1,0:T(8,128)(2,1)S(1)}, u32[]{:S(2)}, u32[]{:S(2)}) %collective-permute-start.16) | collective-permute-done | bytes 393248 | tf_op jit(solution)/shard_map/ppermute | solution.py:178
  58.6 3.3 %shard_map.41.refs_7_ = f32[1536,1536]{1,0:T(8,128)S(1)} custom-call(bf16[1024,1536]{1,0:T(8,128)(2,1)S(1)} %shard_map.37.refs_0_, bf16[128,3072]{1,0:T(8,128)(2,1)S(1)} %copy-done, bf16[128,3072]{1,0:T(8,128)(2,1)S(1)} %collective-permute-done.refs_2_, bf16[128,3072]{1,0:T(8,128)(2,1)S(1)} %collective-permute-done.5.refs_3_, ...), custom_call_target="tpu_custom_call" | custom-call | flops 2415919104 | bytes 22020096 | tf_op jit(solution)/shard_map/pallas_call | solution.py:161
  64.5 3.3 %shard_map.39.refs_7_ = f32[1536,1536]{1,0:T(8,128)S(1)} custom-call(bf16[1024,1536]{1,0:T(8,128)(2,1)S(1)} %shard_map.37.refs_0_, bf16[128,3072]{1,0:T(8,128)(2,1)S(1)} %copy-done, bf16[128,3072]{1,0:T(8,128)(2,1)S(1)} %collective-permute-done.refs_2_, bf16[128,3072]{1,0:T(8,128)(2,1)S(1)} %collective-permute-done.5.refs_3_, ...), custom_call_target="tpu_custom_call" | custom-call | flops 2415919104 | bytes 22020096 | tf_op jit(solution)/shard_map/pallas_call | solution.py:161
  67.8 1.8 %shard_map.38.refs_1_ = bf16[1024,1536]{1,0:T(8,128)(2,1)S(1)} custom-call(s32[2,8]{1,0:T(2,128)S(1)} %dynamic-slice_bitcast_fusion.places_ref, bf16[128,1536]{1,0:T(8,128)(2,1)} %collective-permute-done.2.refs_0_, bf16[128,1536]{1,0:T(8,128)(2,1)} %collective-permute-done.8.refs_1_, bf16[128,1536]{1,0:T(8,128)(2,1)S(1)} %collective-permute-done.16.refs_2_, ...), custom_call_target="tpu_custom_call" | custom-call | bytes 6291456 | tf_op jit(solution)/shard_map/pallas_call | solution.py:93
  69.7 1.8 %collective-permute-start.19 = (bf16[384,768]{1,0:T(8,128)(2,1)S(1)}, bf16[384,768]{1,0:T(8,128)(2,1)S(1)}, u32[]{:S(2)}, u32[]{:S(2)}) collective-permute-start(bf16[384,768]{1,0:T(8,128)(2,1)S(1)} %collective-permute-done.13.refs_5_), channel_id=1, source_target_pairs={{0,1},{2,67},{1,64},{3,2},{64,65},{66,3},{65,0},{67,66},{4,5},{6,7... | collective-permute-start | bytes 1769480 | tf_op jit(solution)/shard_map/ppermute | solution.py:178
  72.1 5.2 %shard_map.42.refs_6_ = f32[1536,1536]{1,0:T(8,128)S(1)} custom-call(bf16[1024,1536]{1,0:T(8,128)(2,1)S(1)} %shard_map.37.refs_0_, bf16[1024,1536]{1,0:T(8,128)(2,1)S(1)} %shard_map.38.refs_1_, bf16[128,3072]{1,0:T(8,128)(2,1)S(1)} %collective-permute-done.11.refs_2_, ...), custom_call_target="tpu_custom_call", output_to_operand_aliasing={{}: (7, {})} | custom-call | flops 3623878656 | bytes 22806528 | tf_op jit(solution)/shard_map/pallas_call | solution.py:161
  77.3 2.5 %collective-permute-start.27 = (bf16[384,768]{1,0:T(8,128)(2,1)S(1)}, bf16[384,768]{1,0:T(8,128)(2,1)S(1)}, u32[]{:S(2)}, u32[]{:S(2)}) collective-permute-start(bf16[384,768]{1,0:T(8,128)(2,1)S(1)} %collective-permute-done.25.refs_2_), channel_id=1, source_target_pairs={{0,1},{2,67},{1,64},{3,2},{64,65},{66,3},{65,0},{67,66},{4,5},{6,7... | collective-permute-start | bytes 1769480 | tf_op jit(solution)/shard_map/ppermute | solution.py:178
  83.5 5.2 %shard_map.40.refs_6_ = f32[1536,1536]{1,0:T(8,128)S(1)} custom-call(bf16[1024,1536]{1,0:T(8,128)(2,1)S(1)} %shard_map.37.refs_0_, bf16[1024,1536]{1,0:T(8,128)(2,1)S(1)} %shard_map.38.refs_1_, bf16[128,3072]{1,0:T(8,128)(2,1)S(1)} %collective-permute-done.11.refs_2_, ...), custom_call_target="tpu_custom_call", output_to_operand_aliasing={{}: (7, {})} | custom-call | flops 3623878656 | bytes 22806528 | tf_op jit(solution)/shard_map/pallas_call | solution.py:161
  88.7 2.2 %collective-permute-done.28.refs_5_ = bf16[384,768]{1,0:T(8,128)(2,1)S(1)} collective-permute-done((bf16[384,768]{1,0:T(8,128)(2,1)S(1)}, bf16[384,768]{1,0:T(8,128)(2,1)S(1)}, u32[]{:S(2)}, u32[]{:S(2)}) %collective-permute-start.28) | collective-permute-done | bytes 589856 | tf_op jit(solution)/shard_map/ppermute | solution.py:178
  90.9 5.8 %shard_map.43.refs_7_ = bf16[1536,3072]{1,0:T(8,128)(2,1)} custom-call(bf16[1024,1536]{1,0:T(8,128)(2,1)S(1)} %shard_map.37.refs_0_, bf16[1024,1536]{1,0:T(8,128)(2,1)S(1)} %shard_map.38.refs_1_, bf16[384,768]{1,0:T(8,128)(2,1)S(1)} %collective-permute-done.25.refs_2_, bf16[384,768]{1,0:T(8,128)(2,1)S(1)} %collective-permute-done.27.refs_3_, ...), custom_call_target="tpu_custom_call" | custom-call | flops 3623878656 | bytes 22806528 | tf_op jit(solution)/shard_map/pallas_call | solution.py:161
  97.2 5.8 %shard_map.44 = bf16[1536,3072]{1,0:T(8,128)(2,1)} custom-call(bf16[1024,1536]{1,0:T(8,128)(2,1)S(1)} %shard_map.37.refs_0_, bf16[1024,1536]{1,0:T(8,128)(2,1)S(1)} %shard_map.38.refs_1_, bf16[384,768]{1,0:T(8,128)(2,1)S(1)} %collective-permute-done.19.refs_2_, bf16[384,768]{1,0:T(8,128)(2,1)S(1)} %collective-permute-done.20.refs_3_, ...), custom_call_target="tpu_custom_call", output_to_operand_aliasing={{}: (7, {})} | custom-call | flops 3623878656 | bytes 22806528 | tf_op jit(solution)/shard_map/pallas_call | solution.py:161
  (57 shorter events, 21.6 us)
Async XLA Ops:
  0.0 20.3 %collective-permute-start.1 = (bf16[128,3072]{1,0:T(8,128)(2,1)}, bf16[128,3072]{1,0:T(8,128)(2,1)S(1)}, u32[]{:S(2)}, u32[]{:S(2)}) collective-permute-start(bf16[128,3072]{1,0:T(8,128)(2,1)} %refs_1_.3), channel_id=1, source_target_pairs={{0,1},{2,67},{1,64},{3,2},{64,65},{66,3},{65,0},{67,66},{4,5},{6,7... | collective-permute-start | bytes 2359304 | tf_op jit(solution)/shard_map/ppermute | solution.py:178
  2.0 18.3 %collective-permute-start = (bf16[128,3072]{1,0:T(8,128)(2,1)}, bf16[128,3072]{1,0:T(8,128)(2,1)S(1)}, u32[]{:S(2)}, u32[]{:S(2)}) collective-permute-start(bf16[128,3072]{1,0:T(8,128)(2,1)} %refs_1_.3), channel_id=1, source_target_pairs={{0,16},{2,50},{1,17},{3,51},{64,80},{66,114},{65,81},{67,115},{4,2... | collective-permute-start | bytes 2359304 | tf_op jit(solution)/shard_map/ppermute | solution.py:178
  6.5 12.3 %collective-permute-start.3 = (bf16[128,1536]{1,0:T(8,128)(2,1)}, bf16[128,1536]{1,0:T(8,128)(2,1)}, u32[]{:S(2)}, u32[]{:S(2)}) collective-permute-start(bf16[128,1536]{1,0:T(8,128)(2,1)} %refs_0_.1), channel_id=1, source_target_pairs={{0,4},{2,14},{1,5},{3,15},{64,68},{66,78},{65,69},{67,79},{4,8},{6... | collective-permute-start | bytes 1179656 | tf_op jit(solution)/shard_map/ppermute | solution.py:178
  6.5 13.7 %collective-permute-start.2 = (bf16[128,1536]{1,0:T(8,128)(2,1)}, bf16[128,1536]{1,0:T(8,128)(2,1)}, u32[]{:S(2)}, u32[]{:S(2)}) collective-permute-start(bf16[128,1536]{1,0:T(8,128)(2,1)} %refs_0_.1), channel_id=1, source_target_pairs={{0,1},{2,3},{1,0},{3,2},{64,65},{66,67},{65,64},{67,66},{4,5},{6,7... | collective-permute-start | bytes 1179656 | tf_op jit(solution)/shard_map/ppermute | solution.py:178
  22.5 17.5 %collective-permute-start.9 = (bf16[384,1536]{1,0:T(8,128)(2,1)}, bf16[384,1536]{1,0:T(8,128)(2,1)}, u32[]{:S(2)}, u32[]{:S(2)}) collective-permute-start(bf16[384,1536]{1,0:T(8,128)(2,1)} %pad_maximum_fusion), channel_id=1, source_target_pairs={{0,2},{2,0},{1,3},{3,1},{64,66},{66,64},{65,67},{67,65},{4,6},{6,4... | collective-permute-start | bytes 3538952 | tf_op jit(solution)/shard_map/ppermute | solution.py:178
  22.5 13.2 %collective-permute-start.5 = (bf16[128,3072]{1,0:T(8,128)(2,1)S(1)}, bf16[128,3072]{1,0:T(8,128)(2,1)S(1)}, u32[]{:S(2)}, u32[]{:S(2)}) collective-permute-start(bf16[128,3072]{1,0:T(8,128)(2,1)S(1)} %collective-permute-done.refs_2_), channel_id=1, source_target_pairs={{0,16},{2,50},{1,17},{3,51},{64,80},{66,114},{65,81},{67,115},{4,2... | collective-permute-start | bytes 2359304 | tf_op jit(solution)/shard_map/ppermute | solution.py:178
  24.0 14.6 %collective-permute-start.6 = (bf16[128,3072]{1,0:T(8,128)(2,1)S(1)}, bf16[128,3072]{1,0:T(8,128)(2,1)S(1)}, u32[]{:S(2)}, u32[]{:S(2)}) collective-permute-start(bf16[128,3072]{1,0:T(8,128)(2,1)S(1)} %collective-permute-done.1.refs_3_), channel_id=1, source_target_pairs={{0,1},{2,67},{1,64},{3,2},{64,65},{66,3},{65,0},{67,66},{4,5},{6,7... | collective-permute-start | bytes 2359304 | tf_op jit(solution)/shard_map/ppermute | solution.py:178
  26.4 12.8 %collective-permute-start.8 = (bf16[128,1536]{1,0:T(8,128)(2,1)}, bf16[128,1536]{1,0:T(8,128)(2,1)}, u32[]{:S(2)}, u32[]{:S(2)}) collective-permute-start(bf16[128,1536]{1,0:T(8,128)(2,1)} %collective-permute-done.2.refs_0_), channel_id=1, source_target_pairs={{0,4},{2,14},{1,5},{3,15},{64,68},{66,78},{65,69},{67,79},{4,8},{6... | collective-permute-start | bytes 1179656 | tf_op jit(solution)/shard_map/ppermute | solution.py:178
  28.0 11.9 %collective-permute-start.7 = (bf16[128,1536]{1,0:T(8,128)(2,1)}, bf16[128,1536]{1,0:T(8,128)(2,1)}, u32[]{:S(2)}, u32[]{:S(2)}) collective-permute-start(bf16[128,1536]{1,0:T(8,128)(2,1)} %collective-permute-done.3.refs_1_), channel_id=1, source_target_pairs={{0,4},{2,14},{1,5},{3,15},{64,68},{66,78},{65,69},{67,79},{4,8},{6... | collective-permute-start | bytes 1179656 | tf_op jit(solution)/shard_map/ppermute | solution.py:178
  35.7 13.9 %collective-permute-start.11 = (bf16[128,3072]{1,0:T(8,128)(2,1)S(1)}, bf16[128,3072]{1,0:T(8,128)(2,1)S(1)}, u32[]{:S(2)}, u32[]{:S(2)}) collective-permute-start(bf16[128,3072]{1,0:T(8,128)(2,1)S(1)} %collective-permute-done.5.refs_3_), channel_id=1, source_target_pairs={{0,16},{2,50},{1,17},{3,51},{64,80},{66,114},{65,81},{67,115},{4,2... | collective-permute-start | bytes 2359304 | tf_op jit(solution)/shard_map/ppermute | solution.py:178
  38.5 13.2 %collective-permute-start.12 = (bf16[128,3072]{1,0:T(8,128)(2,1)S(1)}, bf16[128,3072]{1,0:T(8,128)(2,1)S(1)}, u32[]{:S(2)}, u32[]{:S(2)}) collective-permute-start(bf16[128,3072]{1,0:T(8,128)(2,1)S(1)} %collective-permute-done.6.refs_4_), channel_id=1, source_target_pairs={{0,1},{2,67},{1,64},{3,2},{64,65},{66,3},{65,0},{67,66},{4,5},{6,7... | collective-permute-start | bytes 2359304 | tf_op jit(solution)/shard_map/ppermute | solution.py:178
  44.2 13.2 %collective-permute-start.17 = (bf16[256,1536]{1,0:T(8,128)(2,1)S(1)}, bf16[256,1536]{1,0:T(8,128)(2,1)S(1)}, u32[]{:S(2)}, u32[]{:S(2)}) collective-permute-start(bf16[256,1536]{1,0:T(8,128)(2,1)S(1)} %pad_maximum_fusion.1), channel_id=1, source_target_pairs={{0,2},{2,0},{1,3},{3,1},{64,66},{66,64},{65,67},{67,65},{4,6},{6,4... | collective-permute-start | bytes 2359304 | tf_op jit(solution)/shard_map/ppermute | solution.py:178
  44.3 12.5 %collective-permute-start.16 = (bf16[128,1536]{1,0:T(8,128)(2,1)}, bf16[128,1536]{1,0:T(8,128)(2,1)S(1)}, u32[]{:S(2)}, u32[]{:S(2)}) collective-permute-start(bf16[128,1536]{1,0:T(8,128)(2,1)} %collective-permute-done.2.refs_0_), channel_id=1, source_target_pairs={{0,12},{2,6},{1,13},{3,7},{64,76},{66,70},{65,77},{67,71},{4,0},{6... | collective-permute-start | bytes 1179656 | tf_op jit(solution)/shard_map/ppermute | solution.py:178
  51.8 11.2 %collective-permute-start.23 = (bf16[384,768]{1,0:T(8,128)(2,1)S(1)}, bf16[384,768]{1,0:T(8,128)(2,1)S(1)}, u32[]{:S(2)}, u32[]{:S(2)}) collective-permute-start(bf16[384,768]{1,0:T(8,128)(2,1)S(1)} %pad_maximum_fusion.5), channel_id=1, source_target_pairs={{0,1},{2,67},{1,64},{3,2},{64,65},{66,3},{65,0},{67,66},{4,5},{6,7... | collective-permute-start | bytes 1769480 | tf_op jit(solution)/shard_map/ppermute | solution.py:178
  52.0 11.2 %collective-permute-start.24 = (bf16[384,768]{1,0:T(8,128)(2,1)S(1)}, bf16[384,768]{1,0:T(8,128)(2,1)S(1)}, u32[]{:S(2)}, u32[]{:S(2)}) collective-permute-start(bf16[384,768]{1,0:T(8,128)(2,1)S(1)} %pad_maximum_fusion.6), channel_id=1, source_target_pairs={{0,16},{2,50},{1,17},{3,51},{64,80},{66,114},{65,81},{67,115},{4,2... | collective-permute-start | bytes 1769480 | tf_op jit(solution)/shard_map/ppermute | solution.py:178
  57.6 12.1 %collective-permute-start.13 = (bf16[384,768]{1,0:T(8,128)(2,1)S(1)}, bf16[384,768]{1,0:T(8,128)(2,1)S(1)}, u32[]{:S(2)}, u32[]{:S(2)}) collective-permute-start(bf16[384,768]{1,0:T(8,128)(2,1)S(1)} %pad_maximum_fusion.3), channel_id=1, source_target_pairs={{0,1},{2,67},{1,64},{3,2},{64,65},{66,3},{65,0},{67,66},{4,5},{6,7... | collective-permute-start | bytes 1769480 | tf_op jit(solution)/shard_map/ppermute | solution.py:178
  57.7 12.0 %collective-permute-start.14 = (bf16[384,768]{1,0:T(8,128)(2,1)S(1)}, bf16[384,768]{1,0:T(8,128)(2,1)S(1)}, u32[]{:S(2)}, u32[]{:S(2)}) collective-permute-start(bf16[384,768]{1,0:T(8,128)(2,1)S(1)} %pad_maximum_fusion.4), channel_id=1, source_target_pairs={{0,16},{2,50},{1,17},{3,51},{64,80},{66,114},{65,81},{67,115},{4,2... | collective-permute-start | bytes 1769480 | tf_op jit(solution)/shard_map/ppermute | solution.py:178
  63.1 14.2 %collective-permute-start.25 = (bf16[384,768]{1,0:T(8,128)(2,1)S(1)}, bf16[384,768]{1,0:T(8,128)(2,1)S(1)}, u32[]{:S(2)}, u32[]{:S(2)}) collective-permute-start(bf16[384,768]{1,0:T(8,128)(2,1)S(1)} %collective-permute-done.23.refs_5_), channel_id=1, source_target_pairs={{0,1},{2,67},{1,64},{3,2},{64,65},{66,3},{65,0},{67,66},{4,5},{6,7... | collective-permute-start | bytes 1769480 | tf_op jit(solution)/shard_map/ppermute | solution.py:178
  63.8 13.5 %collective-permute-start.26 = (bf16[384,768]{1,0:T(8,128)(2,1)S(1)}, bf16[384,768]{1,0:T(8,128)(2,1)S(1)}, u32[]{:S(2)}, u32[]{:S(2)}) collective-permute-start(bf16[384,768]{1,0:T(8,128)(2,1)S(1)} %collective-permute-done.24.refs_6_), channel_id=1, source_target_pairs={{0,16},{2,50},{1,17},{3,51},{64,80},{66,114},{65,81},{67,115},{4,2... | collective-permute-start | bytes 1769480 | tf_op jit(solution)/shard_map/ppermute | solution.py:178
  69.7 12.3 %collective-permute-start.19 = (bf16[384,768]{1,0:T(8,128)(2,1)S(1)}, bf16[384,768]{1,0:T(8,128)(2,1)S(1)}, u32[]{:S(2)}, u32[]{:S(2)}) collective-permute-start(bf16[384,768]{1,0:T(8,128)(2,1)S(1)} %collective-permute-done.13.refs_5_), channel_id=1, source_target_pairs={{0,1},{2,67},{1,64},{3,2},{64,65},{66,3},{65,0},{67,66},{4,5},{6,7... | collective-permute-start | bytes 1769480 | tf_op jit(solution)/shard_map/ppermute | solution.py:178
  71.5 11.1 %collective-permute-start.21 = (bf16[384,768]{1,0:T(8,128)(2,1)S(1)}, bf16[384,768]{1,0:T(8,128)(2,1)S(1)}, u32[]{:S(2)}, u32[]{:S(2)}) collective-permute-start(bf16[384,768]{1,0:T(8,128)(2,1)S(1)} %collective-permute-done.14.refs_6_), channel_id=1, source_target_pairs={{0,16},{2,50},{1,17},{3,51},{64,80},{66,114},{65,81},{67,115},{4,2... | collective-permute-start | bytes 1769480 | tf_op jit(solution)/shard_map/ppermute | solution.py:178
  77.3 11.4 %collective-permute-start.27 = (bf16[384,768]{1,0:T(8,128)(2,1)S(1)}, bf16[384,768]{1,0:T(8,128)(2,1)S(1)}, u32[]{:S(2)}, u32[]{:S(2)}) collective-permute-start(bf16[384,768]{1,0:T(8,128)(2,1)S(1)} %collective-permute-done.25.refs_2_), channel_id=1, source_target_pairs={{0,1},{2,67},{1,64},{3,2},{64,65},{66,3},{65,0},{67,66},{4,5},{6,7... | collective-permute-start | bytes 1769480 | tf_op jit(solution)/shard_map/ppermute | solution.py:178
  82.0 14.7 %collective-permute-start.20 = (bf16[384,768]{1,0:T(8,128)(2,1)S(1)}, bf16[384,768]{1,0:T(8,128)(2,1)S(1)}, u32[]{:S(2)}, u32[]{:S(2)}) collective-permute-start(bf16[384,768]{1,0:T(8,128)(2,1)S(1)} %collective-permute-done.19.refs_2_), channel_id=1, source_target_pairs={{0,1},{2,67},{1,64},{3,2},{64,65},{66,3},{65,0},{67,66},{4,5},{6,7... | collective-permute-start | bytes 1769480 | tf_op jit(solution)/shard_map/ppermute | solution.py:178
  82.6 14.6 %collective-permute-start.22 = (bf16[384,768]{1,0:T(8,128)(2,1)S(1)}, bf16[384,768]{1,0:T(8,128)(2,1)S(1)}, u32[]{:S(2)}, u32[]{:S(2)}) collective-permute-start(bf16[384,768]{1,0:T(8,128)(2,1)S(1)} %collective-permute-done.21.refs_4_), channel_id=1, source_target_pairs={{0,16},{2,50},{1,17},{3,51},{64,80},{66,114},{65,81},{67,115},{4,2... | collective-permute-start | bytes 1769480 | tf_op jit(solution)/shard_map/ppermute | solution.py:178
  (7 other events, 54.1 us)

commit v5 on v4

--- a/solution.py
+++ b/solution.py
@@ -196,7 +196,7 @@
     x1, z1 = send(out_grad, X_RING), send(out_grad, Z_RING)
     other = send(activations, REP_SWAP)
     up, down = send(activations, Y_RING), send(activations, Y_BACK)
-    x1, z1, other, up, down = tie((x1, z1, other, up, down))
+    x1, z1, other, up, down, places = tie((x1, z1, other, up, down, places))
 
     x2, z2 = send(x1, X_RING), send(z1, Z_RING)
     far = send(up, Y_RING)

time: 103 us -> 102 us (level)
  other arithmetic: 3.58 us -> 1.34 us
  waiting for transfers between devices: 32.7 us -> 34.8 us
    concatenate x7, other arithmetic: 3.58 us -> 1.34 us  [join(): return jnp.concatenate([b[:, cols] for b in blocks], axis=0)]
    ppermute x29, waiting for transfers between devices: 32.7 us -> 34.8 us  [send(): return lax.ppermute(block, AXES, pairs)]
  transfers between devices with their start and end apart: 29 -> 29, of which waited for: 15 -> 16; matrix products, arithmetic and copies ran while one was open for 2% -> 1% of each run, Pallas kernels for 26% -> 27%
where the time goes in v5:
time: 102 us
  waiting for transfers between devices  34.8 us (34%)
  Pallas kernels  33 us (32%)
  starting transfers between devices  32.1 us (31%)
  other arithmetic  1.34 us (1%)
    ppermute x29, waiting for transfers between devices, send(): return lax.ppermute(block, AXES, pairs)  34.8 us
    ppermute x29, starting transfers between devices, send(): return lax.ppermute(block, AXES, pairs)  32.1 us
    pallas_call x6, Pallas kernels, multiply(): pl.pallas_call(kernel, grid=(rows // step,), in_specs=in_specs, out_specs...  28.6 us
    pallas_call x2, Pallas kernels, sort_tokens(): pl.pallas_call(kernel, grid_spec=pltpu.PrefetchScalarGridSpec(num_scalar_...  4.34 us
  transfers between devices with their start and end apart: 29, of which 16 were waited for; matrix products, arithmetic and copies ran while one was open for 1% of the time, Pallas kernels for 27%

profile of v5, /device:TPU:0, one launch (start us, length us, event | category | flops | bytes accessed | tf_op | source)
XLA Modules:
  0.0 102.3 jit_solution(4773579494570378952)
XLA Ops:
  0.0 2.0 %collective-permute-start.1 = (bf16[128,3072]{1,0:T(8,128)(2,1)}, bf16[128,3072]{1,0:T(8,128)(2,1)S(1)}, u32[]{:S(2)}, u32[]{:S(2)}) collective-permute-start(bf16[128,3072]{1,0:T(8,128)(2,1)} %refs_1_.3), channel_id=1, source_target_pairs={{0,1},{2,67},{1,64},{3,2},{64,65},{66,3},{65,0},{67,66},{4,5},{6,7... | collective-permute-start | bytes 2359304 | tf_op jit(solution)/shard_map/ppermute | solution.py:178
  3.5 3.0 %collective-permute-start.4 = (bf16[128,1536]{1,0:T(8,128)(2,1)}, bf16[128,1536]{1,0:T(8,128)(2,1)S(1)}, u32[]{:S(2)}, u32[]{:S(2)}) collective-permute-start(bf16[128,1536]{1,0:T(8,128)(2,1)} %refs_0_.1), channel_id=1, source_target_pairs={{0,12},{2,6},{1,13},{3,7},{64,76},{66,70},{65,77},{67,71},{4,0},{6... | collective-permute-start | bytes 1179656 | tf_op jit(solution)/shard_map/ppermute | solution.py:178
  6.5 1.9 %collective-permute-start.2 = (bf16[128,1536]{1,0:T(8,128)(2,1)}, bf16[128,1536]{1,0:T(8,128)(2,1)S(1)}, u32[]{:S(2)}, u32[]{:S(2)}) collective-permute-start(bf16[128,1536]{1,0:T(8,128)(2,1)} %refs_0_.1), channel_id=1, source_target_pairs={{0,1},{2,3},{1,0},{3,2},{64,65},{66,67},{65,64},{67,66},{4,5},{6,7... | collective-permute-start | bytes 1179656 | tf_op jit(solution)/shard_map/ppermute | solution.py:178
  9.1 5.5 %collective-permute-done.4.refs_2_ = bf16[128,1536]{1,0:T(8,128)(2,1)S(1)} collective-permute-done((bf16[128,1536]{1,0:T(8,128)(2,1)}, bf16[128,1536]{1,0:T(8,128)(2,1)S(1)}, u32[]{:S(2)}, u32[]{:S(2)}) %collective-permute-start.4) | collective-permute-done | bytes 393248 | tf_op jit(solution)/shard_map/ppermute | solution.py:178
  14.6 4.1 %collective-permute-done.3.refs_1_ = bf16[128,1536]{1,0:T(8,128)(2,1)S(1)} collective-permute-done((bf16[128,1536]{1,0:T(8,128)(2,1)}, bf16[128,1536]{1,0:T(8,128)(2,1)S(1)}, u32[]{:S(2)}, u32[]{:S(2)}) %collective-permute-start.3) | collective-permute-done | bytes 393248 | tf_op jit(solution)/shard_map/ppermute | solution.py:178
  18.7 1.6 %collective-permute-done.2.refs_0_ = bf16[128,1536]{1,0:T(8,128)(2,1)S(1)} collective-permute-done((bf16[128,1536]{1,0:T(8,128)(2,1)}, bf16[128,1536]{1,0:T(8,128)(2,1)S(1)}, u32[]{:S(2)}, u32[]{:S(2)}) %collective-permute-start.2) | collective-permute-done | bytes 393248 | tf_op jit(solution)/shard_map/ppermute | solution.py:178
  23.0 2.4 %collective-permute-start.6 = (bf16[128,3072]{1,0:T(8,128)(2,1)S(1)}, bf16[128,3072]{1,0:T(8,128)(2,1)S(1)}, u32[]{:S(2)}, u32[]{:S(2)}) collective-permute-start(bf16[128,3072]{1,0:T(8,128)(2,1)S(1)} %collective-permute-done.1.refs_3_), channel_id=1, source_target_pairs={{0,1},{2,67},{1,64},{3,2},{64,65},{66,3},{65,0},{67,66},{4,5},{6,7... | collective-permute-start | bytes 2359304 | tf_op jit(solution)/shard_map/ppermute | solution.py:178
  28.5 6.2 %collective-permute-done.5.refs_3_ = bf16[128,3072]{1,0:T(8,128)(2,1)S(1)} collective-permute-done((bf16[128,3072]{1,0:T(8,128)(2,1)S(1)}, bf16[128,3072]{1,0:T(8,128)(2,1)S(1)}, u32[]{:S(2)}, u32[]{:S(2)}) %collective-permute-start.5) | collective-permute-done | bytes 786464 | tf_op jit(solution)/shard_map/ppermute | solution.py:178
  35.0 2.5 %collective-permute-done.6.refs_4_ = bf16[128,3072]{1,0:T(8,128)(2,1)S(1)} collective-permute-done((bf16[128,3072]{1,0:T(8,128)(2,1)S(1)}, bf16[128,3072]{1,0:T(8,128)(2,1)S(1)}, u32[]{:S(2)}, u32[]{:S(2)}) %collective-permute-start.6) | collective-permute-done | bytes 786464 | tf_op jit(solution)/shard_map/ppermute | solution.py:178
  38.6 2.5 %collective-permute-start.10 = (bf16[128,1536]{1,0:T(8,128)(2,1)S(1)}, bf16[128,1536]{1,0:T(8,128)(2,1)S(1)}, u32[]{:S(2)}, u32[]{:S(2)}) collective-permute-start(bf16[128,1536]{1,0:T(8,128)(2,1)S(1)} %collective-permute-done.7.refs_3_), channel_id=1, source_target_pairs={{0,2},{2,0},{1,3},{3,1},{64,66},{66,64},{65,67},{67,65},{4,6},{6,4... | collective-permute-start | bytes 1179656 | tf_op jit(solution)/shard_map/ppermute | solution.py:178
  41.3 3.0 %collective-permute-start.16 = (bf16[128,1536]{1,0:T(8,128)(2,1)S(1)}, bf16[128,1536]{1,0:T(8,128)(2,1)S(1)}, u32[]{:S(2)}, u32[]{:S(2)}) collective-permute-start(bf16[128,1536]{1,0:T(8,128)(2,1)S(1)} %collective-permute-done.2.refs_0_), channel_id=1, source_target_pairs={{0,12},{2,6},{1,13},{3,7},{64,76},{66,70},{65,77},{67,71},{4,0},{6... | collective-permute-start | bytes 1179656 | tf_op jit(solution)/shard_map/ppermute | solution.py:178
  44.4 2.2 %shard_map.37.refs_0_ = bf16[1024,1536]{1,0:T(8,128)(2,1)S(1)} custom-call(s32[2,8]{1,0:T(2,128)S(1)} %dynamic-slice_bitcast_fusion.places_ref, bf16[128,1536]{1,0:T(8,128)(2,1)S(1)} %copy-done.1, bf16[128,1536]{1,0:T(8,128)(2,1)S(1)} %collective-permute-done.3.refs_1_, bf16[128,1536]{1,0:T(8,128)(2,1)S(1)} %collective-permute-done.4.refs_2_, ...), custom_call_target="tpu_custom_call" | custom-call | bytes 6291456 | tf_op jit(solution)/shard_map/pallas_call | solution.py:93
  47.9 2.8 %collective-permute-done.12.refs_4_ = bf16[128,3072]{1,0:T(8,128)(2,1)S(1)} collective-permute-done((bf16[128,3072]{1,0:T(8,128)(2,1)S(1)}, bf16[128,3072]{1,0:T(8,128)(2,1)S(1)}, u32[]{:S(2)}, u32[]{:S(2)}) %collective-permute-start.12) | collective-permute-done | bytes 786464 | tf_op jit(solution)/shard_map/ppermute | solution.py:178
  55.7 3.3 %shard_map.41.refs_7_ = f32[1536,1536]{1,0:T(8,128)S(1)} custom-call(bf16[1024,1536]{1,0:T(8,128)(2,1)S(1)} %shard_map.37.refs_0_, bf16[128,3072]{1,0:T(8,128)(2,1)S(1)} %copy-done, bf16[128,3072]{1,0:T(8,128)(2,1)S(1)} %collective-permute-done.refs_2_, bf16[128,3072]{1,0:T(8,128)(2,1)S(1)} %collective-permute-done.5.refs_3_, ...), custom_call_target="tpu_custom_call" | custom-call | flops 2415919104 | bytes 22020096 | tf_op jit(solution)/shard_map/pallas_call | solution.py:161
  59.1 2.8 %collective-permute-done.23.refs_5_ = bf16[384,768]{1,0:T(8,128)(2,1)S(1)} collective-permute-done((bf16[384,768]{1,0:T(8,128)(2,1)S(1)}, bf16[384,768]{1,0:T(8,128)(2,1)S(1)}, u32[]{:S(2)}, u32[]{:S(2)}) %collective-permute-start.23) | collective-permute-done | bytes 589856 | tf_op jit(solution)/shard_map/ppermute | solution.py:178
  63.4 3.3 %shard_map.39.refs_7_ = f32[1536,1536]{1,0:T(8,128)S(1)} custom-call(bf16[1024,1536]{1,0:T(8,128)(2,1)S(1)} %shard_map.37.refs_0_, bf16[128,3072]{1,0:T(8,128)(2,1)S(1)} %copy-done, bf16[128,3072]{1,0:T(8,128)(2,1)S(1)} %collective-permute-done.refs_2_, bf16[128,3072]{1,0:T(8,128)(2,1)S(1)} %collective-permute-done.5.refs_3_, ...), custom_call_target="tpu_custom_call" | custom-call | flops 2415919104 | bytes 22020096 | tf_op jit(solution)/shard_map/pallas_call | solution.py:161
  66.8 2.2 %shard_map.38.refs_1_ = bf16[1024,1536]{1,0:T(8,128)(2,1)S(1)} custom-call(s32[2,8]{1,0:T(2,128)S(1)} %dynamic-slice_bitcast_fusion.places_ref, bf16[128,1536]{1,0:T(8,128)(2,1)S(1)} %collective-permute-done.2.refs_0_, bf16[128,1536]{1,0:T(8,128)(2,1)S(1)} %collective-permute-done.8.refs_1_, bf16[128,1536]{1,0:T(8,128)(2,1)S(1)} %collective-permute-done.16.refs_2_, ...), custom_call_target="tpu_custom_call" | custom-call | bytes 6291456 | tf_op jit(solution)/shard_map/pallas_call | solution.py:93
  69.0 1.9 %collective-permute-start.19 = (bf16[384,768]{1,0:T(8,128)(2,1)S(1)}, bf16[384,768]{1,0:T(8,128)(2,1)S(1)}, u32[]{:S(2)}, u32[]{:S(2)}) collective-permute-start(bf16[384,768]{1,0:T(8,128)(2,1)S(1)} %collective-permute-done.13.refs_5_), channel_id=1, source_target_pairs={{0,1},{2,67},{1,64},{3,2},{64,65},{66,3},{65,0},{67,66},{4,5},{6,7... | collective-permute-start | bytes 1769480 | tf_op jit(solution)/shard_map/ppermute | solution.py:178
  71.4 5.2 %shard_map.42.refs_6_ = f32[1536,1536]{1,0:T(8,128)S(1)} custom-call(bf16[1024,1536]{1,0:T(8,128)(2,1)S(1)} %shard_map.37.refs_0_, bf16[1024,1536]{1,0:T(8,128)(2,1)S(1)} %shard_map.38.refs_1_, bf16[128,3072]{1,0:T(8,128)(2,1)S(1)} %collective-permute-done.11.refs_2_, ...), custom_call_target="tpu_custom_call", output_to_operand_aliasing={{}: (7, {})} | custom-call | flops 3623878656 | bytes 22806528 | tf_op jit(solution)/shard_map/pallas_call | solution.py:161
  76.6 2.5 %collective-permute-start.27 = (bf16[384,768]{1,0:T(8,128)(2,1)S(1)}, bf16[384,768]{1,0:T(8,128)(2,1)S(1)}, u32[]{:S(2)}, u32[]{:S(2)}) collective-permute-start(bf16[384,768]{1,0:T(8,128)(2,1)S(1)} %collective-permute-done.25.refs_2_), channel_id=1, source_target_pairs={{0,1},{2,67},{1,64},{3,2},{64,65},{66,3},{65,0},{67,66},{4,5},{6,7... | collective-permute-start | bytes 1769480 | tf_op jit(solution)/shard_map/ppermute | solution.py:178
  82.6 5.2 %shard_map.40.refs_6_ = f32[1536,1536]{1,0:T(8,128)S(1)} custom-call(bf16[1024,1536]{1,0:T(8,128)(2,1)S(1)} %shard_map.37.refs_0_, bf16[1024,1536]{1,0:T(8,128)(2,1)S(1)} %shard_map.38.refs_1_, bf16[128,3072]{1,0:T(8,128)(2,1)S(1)} %collective-permute-done.11.refs_2_, ...), custom_call_target="tpu_custom_call", output_to_operand_aliasing={{}: (7, {})} | custom-call | flops 3623878656 | bytes 22806528 | tf_op jit(solution)/shard_map/pallas_call | solution.py:161
  87.8 2.4 %collective-permute-done.28.refs_5_ = bf16[384,768]{1,0:T(8,128)(2,1)S(1)} collective-permute-done((bf16[384,768]{1,0:T(8,128)(2,1)S(1)}, bf16[384,768]{1,0:T(8,128)(2,1)S(1)}, u32[]{:S(2)}, u32[]{:S(2)}) %collective-permute-start.28) | collective-permute-done | bytes 589856 | tf_op jit(solution)/shard_map/ppermute | solution.py:178
  90.2 5.8 %shard_map.43.refs_7_ = bf16[1536,3072]{1,0:T(8,128)(2,1)} custom-call(bf16[1024,1536]{1,0:T(8,128)(2,1)S(1)} %shard_map.37.refs_0_, bf16[1024,1536]{1,0:T(8,128)(2,1)S(1)} %shard_map.38.refs_1_, bf16[384,768]{1,0:T(8,128)(2,1)S(1)} %collective-permute-done.25.refs_2_, bf16[384,768]{1,0:T(8,128)(2,1)S(1)} %collective-permute-done.27.refs_3_, ...), custom_call_target="tpu_custom_call" | custom-call | flops 3623878656 | bytes 22806528 | tf_op jit(solution)/shard_map/pallas_call | solution.py:161
  96.5 5.8 %shard_map.44 = bf16[1536,3072]{1,0:T(8,128)(2,1)} custom-call(bf16[1024,1536]{1,0:T(8,128)(2,1)S(1)} %shard_map.37.refs_0_, bf16[1024,1536]{1,0:T(8,128)(2,1)S(1)} %shard_map.38.refs_1_, bf16[384,768]{1,0:T(8,128)(2,1)S(1)} %collective-permute-done.19.refs_2_, bf16[384,768]{1,0:T(8,128)(2,1)S(1)} %collective-permute-done.20.refs_3_, ...), custom_call_target="tpu_custom_call", output_to_operand_aliasing={{}: (7, {})} | custom-call | flops 3623878656 | bytes 22806528 | tf_op jit(solution)/shard_map/pallas_call | solution.py:161
  (57 shorter events, 22.2 us)
Async XLA Ops:
  0.0 20.3 %collective-permute-start.1 = (bf16[128,3072]{1,0:T(8,128)(2,1)}, bf16[128,3072]{1,0:T(8,128)(2,1)S(1)}, u32[]{:S(2)}, u32[]{:S(2)}) collective-permute-start(bf16[128,3072]{1,0:T(8,128)(2,1)} %refs_1_.3), channel_id=1, source_target_pairs={{0,1},{2,67},{1,64},{3,2},{64,65},{66,3},{65,0},{67,66},{4,5},{6,7... | collective-permute-start | bytes 2359304 | tf_op jit(solution)/shard_map/ppermute | solution.py:178
  2.0 18.3 %collective-permute-start = (bf16[128,3072]{1,0:T(8,128)(2,1)}, bf16[128,3072]{1,0:T(8,128)(2,1)S(1)}, u32[]{:S(2)}, u32[]{:S(2)}) collective-permute-start(bf16[128,3072]{1,0:T(8,128)(2,1)} %refs_1_.3), channel_id=1, source_target_pairs={{0,16},{2,50},{1,17},{3,51},{64,80},{66,114},{65,81},{67,115},{4,2... | collective-permute-start | bytes 2359304 | tf_op jit(solution)/shard_map/ppermute | solution.py:178
  6.5 12.1 %collective-permute-start.3 = (bf16[128,1536]{1,0:T(8,128)(2,1)}, bf16[128,1536]{1,0:T(8,128)(2,1)S(1)}, u32[]{:S(2)}, u32[]{:S(2)}) collective-permute-start(bf16[128,1536]{1,0:T(8,128)(2,1)} %refs_0_.1), channel_id=1, source_target_pairs={{0,4},{2,14},{1,5},{3,15},{64,68},{66,78},{65,69},{67,79},{4,8},{6... | collective-permute-start | bytes 1179656 | tf_op jit(solution)/shard_map/ppermute | solution.py:178
  6.5 13.7 %collective-permute-start.2 = (bf16[128,1536]{1,0:T(8,128)(2,1)}, bf16[128,1536]{1,0:T(8,128)(2,1)S(1)}, u32[]{:S(2)}, u32[]{:S(2)}) collective-permute-start(bf16[128,1536]{1,0:T(8,128)(2,1)} %refs_0_.1), channel_id=1, source_target_pairs={{0,1},{2,3},{1,0},{3,2},{64,65},{66,67},{65,64},{67,66},{4,5},{6,7... | collective-permute-start | bytes 1179656 | tf_op jit(solution)/shard_map/ppermute | solution.py:178
  21.3 17.2 %collective-permute-start.9 = (bf16[384,1536]{1,0:T(8,128)(2,1)S(1)}, bf16[384,1536]{1,0:T(8,128)(2,1)S(1)}, u32[]{:S(2)}, u32[]{:S(2)}) collective-permute-start(bf16[384,1536]{1,0:T(8,128)(2,1)S(1)} %pad_maximum_fusion), channel_id=1, source_target_pairs={{0,2},{2,0},{1,3},{3,1},{64,66},{66,64},{65,67},{67,65},{4,6},{6,4... | collective-permute-start | bytes 3538952 | tf_op jit(solution)/shard_map/ppermute | solution.py:178
  21.4 13.3 %collective-permute-start.5 = (bf16[128,3072]{1,0:T(8,128)(2,1)S(1)}, bf16[128,3072]{1,0:T(8,128)(2,1)S(1)}, u32[]{:S(2)}, u32[]{:S(2)}) collective-permute-start(bf16[128,3072]{1,0:T(8,128)(2,1)S(1)} %collective-permute-done.refs_2_), channel_id=1, source_target_pairs={{0,16},{2,50},{1,17},{3,51},{64,80},{66,114},{65,81},{67,115},{4,2... | collective-permute-start | bytes 2359304 | tf_op jit(solution)/shard_map/ppermute | solution.py:178
  23.0 14.5 %collective-permute-start.6 = (bf16[128,3072]{1,0:T(8,128)(2,1)S(1)}, bf16[128,3072]{1,0:T(8,128)(2,1)S(1)}, u32[]{:S(2)}, u32[]{:S(2)}) collective-permute-start(bf16[128,3072]{1,0:T(8,128)(2,1)S(1)} %collective-permute-done.1.refs_3_), channel_id=1, source_target_pairs={{0,1},{2,67},{1,64},{3,2},{64,65},{66,3},{65,0},{67,66},{4,5},{6,7... | collective-permute-start | bytes 2359304 | tf_op jit(solution)/shard_map/ppermute | solution.py:178
  25.4 12.1 %collective-permute-start.8 = (bf16[128,1536]{1,0:T(8,128)(2,1)S(1)}, bf16[128,1536]{1,0:T(8,128)(2,1)S(1)}, u32[]{:S(2)}, u32[]{:S(2)}) collective-permute-start(bf16[128,1536]{1,0:T(8,128)(2,1)S(1)} %collective-permute-done.2.refs_0_), channel_id=1, source_target_pairs={{0,4},{2,14},{1,5},{3,15},{64,68},{66,78},{65,69},{67,79},{4,8},{6... | collective-permute-start | bytes 1179656 | tf_op jit(solution)/shard_map/ppermute | solution.py:178
  26.9 11.6 %collective-permute-start.7 = (bf16[128,1536]{1,0:T(8,128)(2,1)S(1)}, bf16[128,1536]{1,0:T(8,128)(2,1)S(1)}, u32[]{:S(2)}, u32[]{:S(2)}) collective-permute-start(bf16[128,1536]{1,0:T(8,128)(2,1)S(1)} %collective-permute-done.3.refs_1_), channel_id=1, source_target_pairs={{0,4},{2,14},{1,5},{3,15},{64,68},{66,78},{65,69},{67,79},{4,8},{6... | collective-permute-start | bytes 1179656 | tf_op jit(solution)/shard_map/ppermute | solution.py:178
  34.7 13.2 %collective-permute-start.11 = (bf16[128,3072]{1,0:T(8,128)(2,1)S(1)}, bf16[128,3072]{1,0:T(8,128)(2,1)S(1)}, u32[]{:S(2)}, u32[]{:S(2)}) collective-permute-start(bf16[128,3072]{1,0:T(8,128)(2,1)S(1)} %collective-permute-done.5.refs_3_), channel_id=1, source_target_pairs={{0,16},{2,50},{1,17},{3,51},{64,80},{66,114},{65,81},{67,115},{4,2... | collective-permute-start | bytes 2359304 | tf_op jit(solution)/shard_map/ppermute | solution.py:178
  37.5 13.2 %collective-permute-start.12 = (bf16[128,3072]{1,0:T(8,128)(2,1)S(1)}, bf16[128,3072]{1,0:T(8,128)(2,1)S(1)}, u32[]{:S(2)}, u32[]{:S(2)}) collective-permute-start(bf16[128,3072]{1,0:T(8,128)(2,1)S(1)} %collective-permute-done.6.refs_4_), channel_id=1, source_target_pairs={{0,1},{2,67},{1,64},{3,2},{64,65},{66,3},{65,0},{67,66},{4,5},{6,7... | collective-permute-start | bytes 2359304 | tf_op jit(solution)/shard_map/ppermute | solution.py:178
  41.1 13.0 %collective-permute-start.17 = (bf16[256,1536]{1,0:T(8,128)(2,1)S(1)}, bf16[256,1536]{1,0:T(8,128)(2,1)S(1)}, u32[]{:S(2)}, u32[]{:S(2)}) collective-permute-start(bf16[256,1536]{1,0:T(8,128)(2,1)S(1)} %pad_maximum_fusion.1), channel_id=1, source_target_pairs={{0,2},{2,0},{1,3},{3,1},{64,66},{66,64},{65,67},{67,65},{4,6},{6,4... | collective-permute-start | bytes 2359304 | tf_op jit(solution)/shard_map/ppermute | solution.py:178
  41.3 12.1 %collective-permute-start.16 = (bf16[128,1536]{1,0:T(8,128)(2,1)S(1)}, bf16[128,1536]{1,0:T(8,128)(2,1)S(1)}, u32[]{:S(2)}, u32[]{:S(2)}) collective-permute-start(bf16[128,1536]{1,0:T(8,128)(2,1)S(1)} %collective-permute-done.2.refs_0_), channel_id=1, source_target_pairs={{0,12},{2,6},{1,13},{3,7},{64,76},{66,70},{65,77},{67,71},{4,0},{6... | collective-permute-start | bytes 1179656 | tf_op jit(solution)/shard_map/ppermute | solution.py:178
  50.8 11.2 %collective-permute-start.23 = (bf16[384,768]{1,0:T(8,128)(2,1)S(1)}, bf16[384,768]{1,0:T(8,128)(2,1)S(1)}, u32[]{:S(2)}, u32[]{:S(2)}) collective-permute-start(bf16[384,768]{1,0:T(8,128)(2,1)S(1)} %pad_maximum_fusion.5), channel_id=1, source_target_pairs={{0,1},{2,67},{1,64},{3,2},{64,65},{66,3},{65,0},{67,66},{4,5},{6,7... | collective-permute-start | bytes 1769480 | tf_op jit(solution)/shard_map/ppermute | solution.py:178
  50.9 11.2 %collective-permute-start.24 = (bf16[384,768]{1,0:T(8,128)(2,1)S(1)}, bf16[384,768]{1,0:T(8,128)(2,1)S(1)}, u32[]{:S(2)}, u32[]{:S(2)}) collective-permute-start(bf16[384,768]{1,0:T(8,128)(2,1)S(1)} %pad_maximum_fusion.6), channel_id=1, source_target_pairs={{0,16},{2,50},{1,17},{3,51},{64,80},{66,114},{65,81},{67,115},{4,2... | collective-permute-start | bytes 1769480 | tf_op jit(solution)/shard_map/ppermute | solution.py:178
  54.1 12.6 %collective-permute-start.18 = (bf16[256,1536]{1,0:T(8,128)(2,1)S(1)}, bf16[256,1536]{1,0:T(8,128)(2,1)S(1)}, u32[]{:S(2)}, u32[]{:S(2)}) collective-permute-start(bf16[256,1536]{1,0:T(8,128)(2,1)S(1)} %pad_maximum_fusion.2), channel_id=1, source_target_pairs={{0,2},{2,0},{1,3},{3,1},{64,66},{66,64},{65,67},{67,65},{4,6},{6,4... | collective-permute-start | bytes 2359304 | tf_op jit(solution)/shard_map/ppermute | solution.py:178
  54.3 14.6 %collective-permute-start.13 = (bf16[384,768]{1,0:T(8,128)(2,1)S(1)}, bf16[384,768]{1,0:T(8,128)(2,1)S(1)}, u32[]{:S(2)}, u32[]{:S(2)}) collective-permute-start(bf16[384,768]{1,0:T(8,128)(2,1)S(1)} %pad_maximum_fusion.3), channel_id=1, source_target_pairs={{0,1},{2,67},{1,64},{3,2},{64,65},{66,3},{65,0},{67,66},{4,5},{6,7... | collective-permute-start | bytes 1769480 | tf_op jit(solution)/shard_map/ppermute | solution.py:178
  54.5 14.5 %collective-permute-start.14 = (bf16[384,768]{1,0:T(8,128)(2,1)S(1)}, bf16[384,768]{1,0:T(8,128)(2,1)S(1)}, u32[]{:S(2)}, u32[]{:S(2)}) collective-permute-start(bf16[384,768]{1,0:T(8,128)(2,1)S(1)} %pad_maximum_fusion.4), channel_id=1, source_target_pairs={{0,16},{2,50},{1,17},{3,51},{64,80},{66,114},{65,81},{67,115},{4,2... | collective-permute-start | bytes 1769480 | tf_op jit(solution)/shard_map/ppermute | solution.py:178
  62.1 14.6 %collective-permute-start.25 = (bf16[384,768]{1,0:T(8,128)(2,1)S(1)}, bf16[384,768]{1,0:T(8,128)(2,1)S(1)}, u32[]{:S(2)}, u32[]{:S(2)}) collective-permute-start(bf16[384,768]{1,0:T(8,128)(2,1)S(1)} %collective-permute-done.23.refs_5_), channel_id=1, source_target_pairs={{0,1},{2,67},{1,64},{3,2},{64,65},{66,3},{65,0},{67,66},{4,5},{6,7... | collective-permute-start | bytes 1769480 | tf_op jit(solution)/shard_map/ppermute | solution.py:178
  62.8 13.8 %collective-permute-start.26 = (bf16[384,768]{1,0:T(8,128)(2,1)S(1)}, bf16[384,768]{1,0:T(8,128)(2,1)S(1)}, u32[]{:S(2)}, u32[]{:S(2)}) collective-permute-start(bf16[384,768]{1,0:T(8,128)(2,1)S(1)} %collective-permute-done.24.refs_6_), channel_id=1, source_target_pairs={{0,16},{2,50},{1,17},{3,51},{64,80},{66,114},{65,81},{67,115},{4,2... | collective-permute-start | bytes 1769480 | tf_op jit(solution)/shard_map/ppermute | solution.py:178
  69.0 11.9 %collective-permute-start.19 = (bf16[384,768]{1,0:T(8,128)(2,1)S(1)}, bf16[384,768]{1,0:T(8,128)(2,1)S(1)}, u32[]{:S(2)}, u32[]{:S(2)}) collective-permute-start(bf16[384,768]{1,0:T(8,128)(2,1)S(1)} %collective-permute-done.13.refs_5_), channel_id=1, source_target_pairs={{0,1},{2,67},{1,64},{3,2},{64,65},{66,3},{65,0},{67,66},{4,5},{6,7... | collective-permute-start | bytes 1769480 | tf_op jit(solution)/shard_map/ppermute | solution.py:178
  76.6 11.2 %collective-permute-start.27 = (bf16[384,768]{1,0:T(8,128)(2,1)S(1)}, bf16[384,768]{1,0:T(8,128)(2,1)S(1)}, u32[]{:S(2)}, u32[]{:S(2)}) collective-permute-start(bf16[384,768]{1,0:T(8,128)(2,1)S(1)} %collective-permute-done.25.refs_2_), channel_id=1, source_target_pairs={{0,1},{2,67},{1,64},{3,2},{64,65},{66,3},{65,0},{67,66},{4,5},{6,7... | collective-permute-start | bytes 1769480 | tf_op jit(solution)/shard_map/ppermute | solution.py:178
  80.9 15.1 %collective-permute-start.20 = (bf16[384,768]{1,0:T(8,128)(2,1)S(1)}, bf16[384,768]{1,0:T(8,128)(2,1)S(1)}, u32[]{:S(2)}, u32[]{:S(2)}) collective-permute-start(bf16[384,768]{1,0:T(8,128)(2,1)S(1)} %collective-permute-done.19.refs_2_), channel_id=1, source_target_pairs={{0,1},{2,67},{1,64},{3,2},{64,65},{66,3},{65,0},{67,66},{4,5},{6,7... | collective-permute-start | bytes 1769480 | tf_op jit(solution)/shard_map/ppermute | solution.py:178
  81.9 14.6 %collective-permute-start.22 = (bf16[384,768]{1,0:T(8,128)(2,1)S(1)}, bf16[384,768]{1,0:T(8,128)(2,1)S(1)}, u32[]{:S(2)}, u32[]{:S(2)}) collective-permute-start(bf16[384,768]{1,0:T(8,128)(2,1)S(1)} %collective-permute-done.21.refs_4_), channel_id=1, source_target_pairs={{0,16},{2,50},{1,17},{3,51},{64,80},{66,114},{65,81},{67,115},{4,2... | collective-permute-start | bytes 1769480 | tf_op jit(solution)/shard_map/ppermute | solution.py:178
  (7 other events, 53.4 us)
